TPU v7x, 32 devices: a whole 2x2x4 slice. The times are simulated.
32 devices in a mesh: dp: 8 (over z, x), rows: 4 (over y, core).
Axes of the slice: x: 2, y: 2, z: 4, core: 2. Of those that a mesh axis runs over, the one named last changes fastest.
Arguments:
- images: bfloat16 [48, 32, 128, 256], P('dp', 'rows'), may hold values from -120 to 120
- kernel: bfloat16 [3, 3, 256, 128], replicated, may hold values from -0.25 to 0.25
- colors: float32 [2, 64, 64], replicated, may hold values from -0.75 to 0.75
- offset: float32 [128], replicated, may hold values from -4 to 4
- upstream: bfloat16 [48, 32, 128, 128], P('dp', 'rows'), may hold values from -8 to 8
Outputs:
- colored: bfloat16 [48, 32, 128, 128], P('dp', 'rows')
- grad_images: bfloat16 [48, 32, 128, 256], P('dp', 'rows')
- grad_kernel: float32 [3, 3, 256, 128], replicated
- grad_colors: float32 [2, 64, 64], replicated
All inputs are finite; a program needn't handle non-finite values.
Results may differ from a plain program's by a relative error of at most 0.0044.
The roundings to bfloat16 on the way count: a program that leaves them out, or rounds other values in their place, can miss the bound.
Values may be sent and summed in bfloat16 or wider, within the bound.
No kernel may reach another device: no remote copies, remote signals or barrier semaphores. Data moves between devices by JAX's collectives and lax.ppermute only.
A program may use at most 128 MiB of HBM per device.

v0:
```python
import math

import jax
import jax.numpy as jnp
from jax import lax
from jax.sharding import PartitionSpec as P

NS_ITERS = 5


EPSILON = 1e-05
PRECISE = lax.Precision.HIGHEST


def with_halo(block, sides, width):
    for axis, dim in sides:
        count = lax.axis_size(axis)
        forward = [(i, i + 1) for i in range(count - 1)]
        backward = [(target, source) for source, target in forward]
        low = lax.ppermute(
            lax.slice_in_dim(block, block.shape[dim] - width, None, axis=dim), axis, forward
        )
        high = lax.ppermute(lax.slice_in_dim(block, 0, width, axis=dim), axis, backward)
        block = jnp.concatenate([low, block, high], axis=dim)
    return block


def batched(left, right):
    return jnp.einsum("gij,gjk->gik", left, right, precision=PRECISE)


def inv_root(sigma_mat):
    traces = jnp.trace(sigma_mat, axis1=1, axis2=2)
    normed = sigma_mat / traces[:, None, None]
    estimate = jnp.broadcast_to(
        jnp.eye(sigma_mat.shape[-1], dtype=sigma_mat.dtype), sigma_mat.shape
    )
    for repeat in range(NS_ITERS):
        cubed = batched(batched(estimate, estimate), estimate)
        estimate = 1.5 * estimate - 0.5 * batched(cubed, normed)
    return estimate / jnp.sqrt(traces)[:, None, None]


def filter_valid(source, weights):
    return lax.conv_general_dilated(
        source,
        weights,
        (1, 1),
        "VALID",
        dimension_numbers=("NHWC", "HWIO", "NHWC"),
        preferred_element_type=jnp.float32,
    )


def body(images, kernel, colors, offset, upstream):
    img_count, band_rows, width_n, in_chan = images.shape
    out_chan = kernel.shape[3]
    groups = colors.shape[0]
    group_size = colors.shape[1]
    total_pix = img_count * band_rows * width_n * lax.axis_size("dp") * lax.axis_size("rows")
    rimmed = with_halo(images, (("rows", 1),), 1)
    padded = jnp.pad(rimmed, ((0, 0), (0, 0), (1, 1), (0, 0)))
    pre = filter_valid(padded, kernel)
    raw_cols = pre.reshape(-1, groups, group_size)
    identity = jnp.eye(group_size, dtype=jnp.float32)
    average = lax.psum(jnp.sum(raw_cols, axis=0), ("dp", "rows")) / total_pix
    centred = raw_cols - average
    local_cov = jnp.einsum("pgi,pgj->gij", centred, centred, precision=PRECISE)
    covariance = lax.psum(local_cov, ("dp", "rows")) / total_pix
    sigma_mat = covariance + EPSILON * identity
    whitener, pullback = jax.vjp(inv_root, sigma_mat)
    whitened = jnp.einsum("gij,pgj->pgi", whitener, centred, precision=PRECISE)
    colored = jnp.einsum("gij,pgj->pgi", colors, whitened, precision=PRECISE) + offset.reshape(
        groups, group_size
    )
    colored = colored.astype(jnp.bfloat16).reshape(pre.shape)
    upward = upstream.reshape(-1, groups, group_size).astype(jnp.float32)
    white_grad = jnp.einsum("gji,pgj->pgi", colors, upward, precision=PRECISE)
    local_up = jnp.sum(upward, axis=0)
    local_color = jnp.einsum("pgi,pgj->gij", upward, whitened, precision=PRECISE)
    local_whiten = jnp.einsum("pgi,pgj->gij", white_grad, centred, precision=PRECISE)
    up_total, color_sum, whiten_grad = lax.psum(
        (local_up, local_color, local_whiten), ("dp", "rows")
    )
    (sigma_grad,) = pullback(whiten_grad)
    symmetric = sigma_grad + jnp.transpose(sigma_grad, (0, 2, 1))
    mean_grad = jnp.einsum("gji,gj->gi", colors, up_total, precision=PRECISE) / total_pix
    centred_grad = jnp.einsum("gji,pgj->pgi", whitener, white_grad, precision=PRECISE)
    centred_grad = (
        centred_grad + jnp.einsum("gij,pgj->pgi", symmetric, centred, precision=PRECISE) / total_pix
    )
    pre_grad = centred_grad - jnp.einsum("gji,gj->gi", whitener, mean_grad, precision=PRECISE)
    pre_grad = pre_grad.astype(jnp.bfloat16).reshape(pre.shape)
    grad_rimmed = with_halo(pre_grad, (("rows", 1),), 1)
    grad_padded = jnp.pad(grad_rimmed, ((0, 0), (0, 0), (1, 1), (0, 0)))
    flipped = jnp.transpose(kernel[::-1, ::-1], (0, 1, 3, 2))
    grad_images = filter_valid(grad_padded, flipped).astype(jnp.bfloat16)
    grad_flat = pre_grad.reshape(-1, out_chan)
    outer = []
    for row_off in range(3):
        inner = []
        for col_off in range(3):
            window = padded[
                :, row_off : row_off + band_rows, col_off : col_off + width_n, :
            ].reshape(-1, in_chan)
            inner.append(
                lax.dot_general(
                    window, grad_flat, (((0,), (0,)), ((), ())), preferred_element_type=jnp.float32
                )
            )
        outer.append(jnp.stack(inner))
    kernel_term = jnp.stack(outer)
    summed = lax.psum(kernel_term, ("dp", "rows"))
    scaling = 1.0 / math.sqrt(total_pix)
    return (colored, grad_images, summed * scaling, color_sum * scaling)


def solution(mesh):
    placed = (P("dp", "rows", None, None), P(), P(), P(), P("dp", "rows", None, None))
    return jax.shard_map(
        body,
        mesh=mesh,
        in_specs=placed,
        out_specs=(P("dp", "rows", None, None), P("dp", "rows", None, None), P(), P()),
        check_vma=False,
    )
```

profile of v0, /device:TPU:0, one launch (start us, length us, event | category | flops | bytes accessed | tf_op | source)
XLA Modules:
  0.0 509.8 jit_solution(1571709535847726581)
XLA Ops:
  10.6 3.1 collective-permute-start
  21.1 3.1 convolution_bitcast_fusion
  27.4 6.3 %pad_maximum_fusion.1 = (bf16[6,8,128,256]{3,2,1,0:T(8,128)(2,1)}, bf16[6,8,128,256]{3,2,1,0:T(8,128)(2,1)}, bf16[6,10,128,256]{3,2,1,0:T(8,128)(2,1)S(1)}) fusion(bf16[6,8,128,256]{3,2,1,0:T(8,128)(2,1)} %param.5, bf16[6,1,128,256]{3,2,1,0:T(8,128)(2,1)S(1)} %collective-permute-done, bf16[6,1,128,256]{3,2,1,0:T(8,128)(2,1)S(1)} %collective-permute-done.1, ...), kind=kLoop, calls=%fused_computation.19 | loop fusion | flops 12582912 | bytes 13369344 | tf_op jit(solution)/shard_map/concatenate | solution.py:24
  33.7 13.9 %pad_slice_fusion.5 = (bf16[6,8,128,256]{3,2,1,0:T(8,128)(2,1)}, bf16[6,8,128,256]{3,2,1,0:T(8,128)(2,1)}, bf16[6,8,128,256]{3,2,1,0:T(8,128)(2,1)}, bf16[6,8,12...) fusion(bf16[6,10,128,256]{3,2,1,0:T(8,128)(2,1)S(1)} %constant_dynamic-update-slice_fusion), kind=kLoop, calls=%fused_computation.37 | loop fusion | bytes 22806528 | tf_op jit(solution)/shard_map/slice | solution.py:103
  48.1 4.7 pad.7.clone
  52.7 7.9 %reshape.99 = bf16[10,6,8,17,256]{4,3,2,1,0:T(8,128)(2,1)} reshape(bf16[10,6,136,256]{3,2,1,0:T(8,128)(2,1)} %pad.7.clone) | data formatting | bytes 8355840 | tf_op jit(solution)/shard_map/conv_general_dilated | solution.py:45
  62.3 4.4 fusion.4
  66.8 10.0 %select_reduce_fusion = (f32[128]{0:T(128)S(1)}, f32[8,48,17,128]{3,1,2,0:T(8,128)}) fusion(pred[48,17]{0,1:T(8,128)(4,1)S(1)} %copy-done.21, bf16[3,3,256,128]{3,2,1,0:T(8,128)(2,1)S(1)} %copy-done, bf16[10,6,8,19,256]{4,3,2,1,0:T(8,128)(2,1)S(1)} %fusion.4), kind=kOutput, calls=%fused_computation.17 | convolution fusion | flops 3852877824 | bytes 8602928 | tf_op jit(solution)/shard_map/conv_general_dilated | solution.py:45
  76.8 42.5 %psum.42 = f32[2,64]{1,0:T(2,128)S(1)} all-reduce(f32[2,64]{1,0:T(2,128)S(1)} %reduce_sum.59), channel_id=1, replica_groups=mesh['dp'=8,'rows'=4] {'dp','rows'}, use_global_device_ids=true, to_apply=%region_1.2 | all-reduce | flops 128 | bytes 1024 | tf_op jit(solution)/shard_map/psum | solution.py:66
  119.3 3.0 copy.71
  124.2 3.6 copy.72
  127.8 4.2 reshape.84
  132.0 6.2 %fusion.14 = f32[2,64,64]{2,1,0:T(8,128)S(1)} fusion(f32[6144,2,64]{0,2,1:T(8,128)} %reshape.84, f32[2,64]{1,0:T(2,128)S(1)} %broadcast_multiply_fusion.3), kind=kOutput, calls=%fused_computation.28 | convolution fusion | flops 604766208 | bytes 3179008 | tf_op jit(solution)/shard_map/pgi,pgj->gij/dot_general | solution.py:68
  138.3 5.6 %fusion.11 = f32[2,64,64]{2,1,0:T(8,128)} fusion(f32[6144,2,64]{0,2,1:T(8,128)} %convolution_bitcast_fusion, f32[6144,2,64]{0,2,1:T(8,128)S(1)} %copy-done.1, f32[2,64]{1,0:T(2,128)S(1)} %broadcast_multiply_fusion.3), kind=kOutput, calls=%fused_computation.25 | convolution fusion | flops 604766208 | bytes 6324736 | tf_op jit(solution)/shard_map/pgi,pgj->gij/dot_general | solution.py:81
  143.9 40.6 %psum.43 = f32[2,64,64]{2,1,0:T(8,128)S(1)} all-reduce(f32[2,64,64]{2,1,0:T(8,128)S(1)} %fusion.14), channel_id=1, replica_groups=mesh['dp'=8,'rows'=4] {'dp','rows'}, use_global_device_ids=true, to_apply=%region_2.3 | all-reduce | flops 8192 | bytes 65536 | tf_op jit(solution)/shard_map/psum | solution.py:69
  187.7 5.2 %convolution_bitcast_fusion.1 = f32[6144,2,64]{0,2,1:T(8,128)S(1)} fusion(f32[6144,2,64]{0,2,1:T(8,128)} %reshape.84, f32[2,64]{1,0:T(2,128)S(1)} %broadcast_multiply_fusion.3, f32[2,64,64]{2,1,0:T(8,128)S(1)} %fusion.27, f32[2]{0:T(128)S(1)} %get-tuple-element.36), kind=kOutput, calls=%fused_computation.6 | convolution fusion | flops 604774400 | bytes 6324744 | tf_op jit(solution)/shard_map/gij,pgj->pgi/dot_general | solution.py:72
  197.0 4.9 fusion.2
  204.3 114.8 %all-reduce.7.cloned.1.call-done = (f32[2,64,64]{2,1,0:T(8,128)}, f32[2,64]{1,0:T(2,128)}, f32[2,64,64]{1,2,0:T(8,128)}) async-done(((f32[2,64,64]{2,1,0:T(8,128)}, f32[2,64]{1,0:T(2,128)}, f32[2,64,64]{1,2,0:T(8,128)}), (f32[2,64,64]{2,1,0:T(8,128)}, f32[2,64]{1,0:T(2,128)}, f32[2,64,64]{1,2,0:T(8,128)})) %all-reduce.7.cloned.1.call-update) | async-done | bytes 66064 | tf_op jit(solution)/shard_map/psum | solution.py:82
  329.5 5.2 %convolution_multiply_fusion = f32[2,6144,64]{1,2,0:T(8,128)S(1)} fusion(f32[6144,2,64]{0,2,1:T(8,128)} %reshape.84, f32[2,64]{1,0:T(2,128)S(1)} %broadcast_multiply_fusion.3, f32[2,64,64]{2,1,0:T(8,128)S(1)} %get-tuple-element.33, f32[2,64,64]{1,2,0:T(8,128)S(1)} %copy.93, f32[2]{0:T(128)S(1)} %negate_add_fusion, pred[64,64]{0,1:T(8,128)(4,1)S(1)} %get-tuple-element.39, ...), kind=kOutput, calls=%fused_computation.3 | convolution fusion | flops 605593600 | bytes 6365704 | tf_op jit(solution)/shard_map/gij,pgj->pgi/dot_general | solution.py:90
  334.8 3.1 fusion.3
  349.0 4.5 collective-permute-start.2
  370.3 3.6 reshape.107
  375.4 4.8 select_convert_fusion
  384.1 116.3 %all-reduce.5.cloned.1.call-done = f32[3,3,256,128]{3,2,1,0:T(8,128)} async-done(((f32[3,3,256,128]{3,2,1,0:T(8,128)}), f32[3,3,256,128]{3,2,1,0:T(8,128)}) %all-reduce.5.cloned.1.call-update) | async-done | bytes 1179664 | tf_op jit(solution)/shard_map/psum | solution.py:113
  (155 shorter events, 73.3 us)
Async XLA Ops:
  7.2 59.6 %copy-start = (bf16[3,3,256,128]{3,2,1,0:T(8,128)(2,1)S(1)}, bf16[3,3,256,128]{3,2,1,0:T(8,128)(2,1)}, u32[]{:S(2)}) copy-start(bf16[3,3,256,128]{3,2,1,0:T(8,128)(2,1)} %param.6) | copy-start | bytes 1769476
  7.2 8.7 %copy-start.13 = (bf16[6,8,128,128]{3,2,1,0:T(8,128)(2,1)S(1)}, bf16[6,8,128,128]{3,2,1,0:T(8,128)(2,1)}, u32[]{:S(2)}) copy-start(bf16[6,8,128,128]{3,2,1,0:T(8,128)(2,1)} %param.9) | copy-start | bytes 4718596
  7.2 311.9 %all-reduce.7.cloned.1.call-start = ((), (), s32[]{:S(2)}) async-start(), calls=%async_computation.1 | async-start | bytes 264192 | tf_op jit(solution)/shard_map/psum | solution.py:82
  9.3 18.1 %collective-permute-start.1 = (bf16[6,1,128,256]{3,2,1,0:T(8,128)(2,1)S(1)}, bf16[6,1,128,256]{3,2,1,0:T(8,128)(2,1)S(1)}, u32[]{:S(2)}, u32[]{:S(2)}) collective-permute-start(bf16[6,1,128,256]{3,2,1,0:T(8,128)(2,1)S(1)} %get-tuple-element.28), channel_id=1, source_target_pairs={{1,0},{2,1},{3,2},{5,4},{6,5},{7,6},{9,8},{10,9},{11,10},{13,12},{... | collective-permute-start | bytes 1179656 | tf_op jit(solution)/shard_map/ppermute | solution.py:23
  10.6 16.8 %collective-permute-start = (bf16[6,1,128,256]{3,2,1,0:T(8,128)(2,1)}, bf16[6,1,128,256]{3,2,1,0:T(8,128)(2,1)S(1)}, u32[]{:S(2)}, u32[]{:S(2)}) collective-permute-start(bf16[6,1,128,256]{3,2,1,0:T(8,128)(2,1)} %get-tuple-element.29), channel_id=1, source_target_pairs={{0,1},{1,2},{2,3},{4,5},{5,6},{6,7},{8,9},{9,10},{10,11},{12,13},{... | collective-permute-start | bytes 1179656 | tf_op jit(solution)/shard_map/ppermute | solution.py:20
  15.9 5.2 %copy-start.14 = (f32[2,64,64]{2,1,0:T(8,128)S(1)}, f32[2,64,64]{2,1,0:T(8,128)}, u32[]{:S(2)}) copy-start(f32[2,64,64]{2,1,0:T(8,128)} %param.7) | copy-start | bytes 98308
  21.1 3.8 copy-start.20
  62.3 4.4 copy-start.21
  132.0 6.2 %copy-start.1 = (f32[6144,2,64]{0,2,1:T(8,128)S(1)}, f32[6144,2,64]{0,2,1:T(8,128)}, u32[]{:S(2)}) copy-start(f32[6144,2,64]{0,2,1:T(8,128)} %reshape.84) | copy-start | bytes 9437188
  138.3 46.4 %copy-start.17 = (f32[64,64]{1,0:T(8,128)S(1)}, f32[64,64]{1,0:T(8,128)}, u32[]{:S(2)}) copy-start(f32[64,64]{1,0:T(8,128)} %copy.73) | copy-start | bytes 49156
  194.6 2.3 copy-start.19
  196.9 303.5 %all-reduce.5.cloned.1.call-start = ((), (), s32[]{:S(2)}) async-start(), calls=%async_computation | async-start | bytes 2359296 | tf_op jit(solution)/shard_map/psum | solution.py:113
  319.1 7.9 %copy-start.15 = (f32[2,64,64]{2,1,0:T(8,128)S(1)}, f32[2,64,64]{2,1,0:T(8,128)}, u32[]{:S(2)}) copy-start(f32[2,64,64]{2,1,0:T(8,128)} %get-tuple-element.16) | copy-start | bytes 98308
  319.1 8.1 %copy-start.18 = (f32[2,64]{1,0:T(2,128)S(1)}, f32[2,64]{1,0:T(2,128)}, u32[]{:S(2)}) copy-start(f32[2,64]{1,0:T(2,128)} %get-tuple-element.17) | copy-start | bytes 1540
  329.5 5.2 %copy-start.2 = (f32[6144,2,64]{0,2,1:T(8,128)S(1)}, f32[6144,2,64]{0,2,1:T(8,128)}, u32[]{:S(2)}) copy-start(f32[6144,2,64]{0,2,1:T(8,128)} %convolution_bitcast_fusion) | copy-start | bytes 9437188
  334.8 3.1 copy-start.6
  338.9 2.3 copy-start.16
  338.9 2.3 copy-start.4
  347.1 10.7 %copy-start.11 = (bf16[6,8,128,256]{3,2,1,0:T(8,128)(2,1)S(1)}, bf16[6,8,128,256]{3,2,1,0:T(8,128)(2,1)}, u32[]{:S(2)}) copy-start(bf16[6,8,128,256]{3,2,1,0:T(8,128)(2,1)} %get-tuple-element.20) | copy-start | bytes 9437188
  349.0 17.9 %collective-permute-start.2 = (bf16[6,1,128,128]{3,2,0,1:T(8,128)(2,1)}, bf16[6,1,128,128]{3,2,0,1:T(8,128)(2,1)}, u32[]{:S(2)}, u32[]{:S(2)}) collective-permute-start(bf16[6,1,128,128]{3,2,0,1:T(8,128)(2,1)} %get-tuple-element.30), channel_id=1, source_target_pairs={{0,1},{1,2},{2,3},{4,5},{5,6},{6,7},{8,9},{9,10},{10,11},{12,13},{... | collective-permute-start | bytes 589832 | tf_op jit(solution)/shard_map/ppermute | solution.py:20
  353.5 13.4 %collective-permute-start.3 = (bf16[6,1,128,128]{3,2,0,1:T(8,128)(2,1)}, bf16[6,1,128,128]{3,2,0,1:T(8,128)(2,1)}, u32[]{:S(2)}, u32[]{:S(2)}) collective-permute-start(bf16[6,1,128,128]{3,2,0,1:T(8,128)(2,1)} %get-tuple-element.31), channel_id=1, source_target_pairs={{1,0},{2,1},{3,2},{5,4},{6,5},{7,6},{9,8},{10,9},{11,10},{13,12},{... | collective-permute-start | bytes 589832 | tf_op jit(solution)/shard_map/ppermute | solution.py:23
  358.8 2.1 copy-start.9
  361.9 2.1 copy-start.7
  365.0 2.0 copy-start.12
  (5 other events, 8.7 us)
Sparse Core Ops, SparseCore 0:
  197.0 122.0 all-reduce.6
  367.1 133.3 all-reduce.4
where the time goes:
time: 519 us; the launch traced here: 510 us
  waiting for transfers between devices  231 us (45%)
  blocking collectives  83 us (16%)
  matrix products  76.9 us (15%)
  local copies, waits for them, and re-layouts  74 us (14%)
  other arithmetic  19.3 us (4%)
  between operations  15.1 us (3%)
  starting transfers between devices  10.2 us (2%)
    psum x1, waiting for transfers between devices, body(): summed = lax.psum(kernel_term, ('dp', 'rows'))  116 us
    psum x1, waiting for transfers between devices, body(): lax.psum((local_up, local_color, local_whiten), ('dp', 'rows'))  115 us
    psum x1, blocking collectives, body(): average = lax.psum(jnp.sum(raw_cols, axis=0), ('dp', 'rows')) / total_pix  42.5 us
    psum x1, blocking collectives, body(): covariance = lax.psum(local_cov, ('dp', 'rows')) / total_pix  40.6 us
    conv_general_dilated x7, local copies, waits for them, and re-layouts, filter_valid(): lax.conv_general_dilated(source, weights, (1, 1), 'VALID', dimension_numb...  21.9 us
    conv_general_dilated x2, matrix products, filter_valid(): lax.conv_general_dilated(source, weights, (1, 1), 'VALID', dimension_numb...  14.7 us
    dot_general x40, matrix products, batched(): return jnp.einsum('gij,gjk->gik', left, right, precision=PRECISE)  14.3 us
    unnamed x54, local copies, waits for them, and re-layouts  13.9 us
  transfers between devices with their start and end apart: 6, of which 2 were waited for; matrix products, arithmetic and copies ran while one was open for 9% of the time, Pallas kernels for 0%

commit v1 on v0

v1 whole, which is shorter than its diff:
```python
import functools
import math

import jax
import jax.numpy as jnp
from jax import lax
from jax.experimental import pallas as pl
from jax.experimental.pallas import tpu as pltpu
from jax.sharding import PartitionSpec as P

NS_ITERS = 5
EPSILON = 1e-05
F32 = jnp.float32
BF16 = jnp.bfloat16
MIB = 1024 * 1024
AXES = ("dp", "rows")


def device_index():
    return lax.axis_index("dp") * lax.axis_size("rows") + lax.axis_index("rows")


def is_even():
    return lax.axis_index("rows") % 2 == 0


def is_upper(stage):
    index = device_index()
    return index & jnp.where(index & 1 != 0, stage[1], stage[0]) != 0


def stages(devices):
    bits = [1 << i for i in range(devices.bit_length() - 1)]
    plan = [(bit, bit) for bit in bits]
    if len(bits) > 2:
        plan[1:3] = [(2, 4), (4, 2)]
    return plan


def split(value):
    high = value.astype(BF16)
    return high, (value - high.astype(F32)).astype(BF16)


def dot(left, right, dims=((1,), (0,))):
    return lax.dot_general(left, right, (dims, ((), ())), preferred_element_type=F32)


def dot3(left, right):
    lh, ll = split(left)
    rh, rl = split(right)
    return dot(
        jnp.concatenate([lh, lh, ll], axis=1), jnp.concatenate([rh, rl, rh], axis=0)
    )


def shifted(value):
    width = value.shape[1]
    col = lax.broadcasted_iota(jnp.int32, (1, *value.shape[1:]), 1)
    after = jnp.where(col == width - 1, 0.0, pltpu.roll(value, width - 1, 1))
    before = jnp.where(col == 0, 0.0, pltpu.roll(value, 1, 1))
    return after, before


def merged(prod, shape):
    cout = shape[2]
    _, left = shifted(prod[:, :cout].reshape(shape))
    right, _ = shifted(prod[:, 2 * cout :].reshape(shape))
    return prod[:, cout : 2 * cout].reshape(shape) + left + right


def column(row):
    size = row.shape[1]
    return jnp.broadcast_to(row, (size, size)).T


def pack(full):
    half = full.shape[0] // 2
    lane = lax.broadcasted_iota(jnp.int32, (half, full.shape[1]), 1)
    return jnp.where(lane < half, full[:half], full[half:])


def unpack(packed):
    half = packed.shape[0]
    lane = lax.broadcasted_iota(jnp.int32, packed.shape, 1)
    return jnp.concatenate(
        [jnp.where(lane < half, packed, 0.0), jnp.where(lane < half, 0.0, packed)], axis=0
    )


def statistics(held):
    third = held.shape[1] // 3
    return dot(held[:, third:], held[:, : 2 * third], ((0,), (0,)))


def forward_kernel(img, kern, ups, pre_out, acc, sums, wts, held):
    step = pl.program_id(0)
    last = pl.num_programs(0) - 1
    rows, width, cin = img.shape[1:]
    cout = kern.shape[3]
    inner = (rows - 2) * width

    @pl.when(step == 0)
    def _():
        for a in range(3):
            for c in range(3):
                wts[a * cin : (a + 1) * cin, c * cout : (c + 1) * cout] = kern[a, c]
        acc[...] = jnp.zeros_like(acc)
        sums[...] = jnp.zeros_like(sums)
        held[...] = jnp.zeros_like(held)

    acc[...] += statistics(held[...])
    blank = jnp.zeros((1, width, cin), BF16)
    padded = jnp.concatenate([blank, img[0], blank], axis=0)
    wide = jnp.concatenate([padded[a : a + rows] for a in range(3)], axis=2)
    prod = dot(wide.reshape(rows * width, 3 * cin), wts[...])
    pre = merged(prod, (rows, width, cout))
    pre_out[0] = pre
    mid = pre[1 : rows - 1].reshape(inner, cout)
    mean = jnp.sum(mid, axis=0, keepdims=True) / inner
    shift = jnp.where(step == 0, mean, sums[2:3])
    sums[2:3] = shift
    delta = mid - shift
    up = ups[0, 1 : rows - 1].reshape(inner, cout)
    high, low = split(delta)
    held[:, :cout] = low
    held[:, cout : 2 * cout] = high
    held[:, 2 * cout :] = up
    sums[0:1] += jnp.sum(delta, axis=0, keepdims=True)
    sums[1:2] += jnp.sum(up.astype(F32), axis=0, keepdims=True)

    @pl.when(step == last)
    def _():
        acc[...] += statistics(held[...])


def sides(ahead, across):
    even = is_even()
    return jnp.where(even, across, ahead), jnp.where(even, ahead, across)


def slice_kernel(first, final, ahead, across):
    across[...], ahead[...] = sides(final[...], first[...])


def edge_kernel(
    total,
    stage,
    ahead,
    across,
    pre_top,
    pre_bot,
    ups_top,
    ups_bot,
    kern,
    acc,
    sums,
    low,
    high,
    keep,
    send,
    stats,
):
    count, _, width, cin = ahead.shape
    cout = kern.shape[3]
    top, bot = sides(ahead[...], across[...])
    pixels = count * width
    shape = (count, width, cout)
    edges = []
    for a, source, part, out in ((0, top, pre_top, low), (2, bot, pre_bot, high)):
        taps = jnp.concatenate([kern[a, c] for c in range(3)], axis=1)
        value = merged(dot(source.reshape(pixels, cin), taps), shape) + part[:, 0]
        out[:, 0] = value
        edges.append(value.reshape(pixels, cout))
    shift = sums[2:3]
    delta = jnp.concatenate(edges, axis=0) - shift
    up = jnp.concatenate(
        [ups_top[...].reshape(pixels, cout), ups_bot[...].reshape(pixels, cout)], axis=0
    )
    big, small = split(delta)
    gram = acc[...] + statistics(jnp.concatenate([small, big, up], axis=1))
    moved = sums[0:1] + jnp.sum(delta, axis=0, keepdims=True)
    up_sum = sums[1:2] + jnp.sum(up.astype(F32), axis=0, keepdims=True)
    mixed = gram[:cout, :cout]
    square = gram[:cout, cout:] + mixed + mixed.T
    cross = gram[cout:, :cout] + gram[cout:, cout:]
    raw = moved + total * shift
    square = square + column(moved) * shift + column(shift) * raw
    cross = cross + column(up_sum) * shift
    half = cout // 2
    stats[0:half] = pack(square)
    stats[half : 2 * half] = pack(cross)
    stats[2 * half :] = jnp.zeros_like(stats[2 * half :])
    stats[2 * half : 2 * half + 1] = raw
    stats[2 * half + 1 : 2 * half + 2] = up_sum
    part = keep.shape[0]
    upper = is_upper(stage)
    keep[...] = jnp.where(upper, stats[part:], stats[:part])
    send[...] = jnp.where(upper, stats[:part], stats[part:])


def spread(blocks):
    zero = jnp.zeros(blocks.shape[1:], F32)
    return jnp.concatenate(
        [
            jnp.concatenate([blocks[0], zero], axis=1),
            jnp.concatenate([zero, blocks[1]], axis=1),
        ],
        axis=0,
    )


def group_sum(value, half):
    cols = jnp.sum(value, axis=0, keepdims=True)
    lane = lax.broadcasted_iota(jnp.int32, cols.shape, 1)
    low = jnp.sum(jnp.where(lane < half, cols, 0.0), axis=1, keepdims=True)
    high = jnp.sum(jnp.where(lane < half, 0.0, cols), axis=1, keepdims=True)
    return jnp.where(lane < half, low, high)


def whitening(stats, colors, offset, total_pix, half):
    cout = 2 * half
    row_i = lax.broadcasted_iota(jnp.int32, (cout, cout), 0)
    col_i = lax.broadcasted_iota(jnp.int32, (cout, cout), 1)
    eye = jnp.where(row_i == col_i, 1.0, 0.0)
    block = jnp.where((row_i < half) == (col_i < half), 1.0, 0.0)
    square = unpack(stats[0:half])
    cross = unpack(stats[half : 2 * half])
    average = stats[2 * half : 2 * half + 1] / total_pix
    up_total = stats[2 * half + 1 : 2 * half + 2]
    sigma = square / total_pix - block * (column(average) * average) + EPSILON * eye
    cross = cross - block * (column(up_total) * average)
    grad = dot3(colors.T, cross)
    direction = grad + grad.T
    traces = group_sum(sigma * eye, half)
    normed = sigma / traces
    zero = jnp.zeros_like(normed)

    def stacked(value, tangent):
        return jnp.concatenate(
            [
                jnp.concatenate([value, tangent], axis=1),
                jnp.concatenate([zero, value], axis=1),
            ],
            axis=0,
        )

    source = stacked(normed, direction)
    value = 1.5 * eye - 0.5 * normed
    tangent = -0.5 * direction
    for _ in range(NS_ITERS - 1):
        first = jnp.concatenate([value, tangent], axis=1)
        both = dot3(first, jnp.concatenate([stacked(value, tangent), source], axis=1))
        squared = both[:, : 2 * cout]
        scaled = stacked(both[:, 2 * cout : 3 * cout], both[:, 3 * cout :])
        cubed = dot3(squared, scaled)
        value = 1.5 * value - 0.5 * cubed[:, :cout]
        tangent = 1.5 * tangent - 0.5 * cubed[:, cout:]
    inverse = 1.0 / jnp.sqrt(traces)
    whitener = value * inverse
    shared = group_sum(tangent * normed, half) + 0.5 * group_sum(direction * value, half)
    symmetric = (tangent - eye * shared) * (inverse / traces)
    mixed = dot3(colors, whitener)
    color_sum = dot3(cross, whitener.T)
    up_mean = jnp.broadcast_to(up_total / total_pix, (8, cout))
    bias = -dot3(up_mean, mixed)[0:1]
    return average, mixed, symmetric / total_pix, bias, offset, color_sum


def backward_kernel(
    total_pix,
    stage,
    own,
    other,
    colors,
    offset,
    pre,
    low,
    high,
    ups,
    img,
    ahead,
    across,
    colored,
    pre_grad,
    edge_ahead,
    edge_across,
    keep,
    send,
    grad_colors,
    stats,
    mats,
    rowsbuf,
    acc,
    turned,
):
    step = pl.program_id(0)
    last = pl.num_programs(0) - 1
    rows, width, cin = img.shape[1:]
    cout = pre.shape[3]
    half = cout // 2
    pixels = rows * width
    scaling = 1.0 / math.sqrt(total_pix)

    @pl.when(step == 0)
    def _():
        join_kernel(stage, own, other, stats)
        average, mixed, symmetric, bias, offs, color_sum = whitening(
            stats[...], spread(colors[...]), offset[...], total_pix, half
        )
        zero = jnp.zeros((cout, cout), BF16)
        mixed_h, mixed_l = split(mixed)
        color_h, color_l = split(mixed.T)
        sym_h, sym_l = split(symmetric)
        for index, (one, two) in enumerate(
            ((sym_h, color_h), (sym_h, color_h), (sym_l, color_l), (mixed_h, zero), (mixed_l, zero))
        ):
            mats[index * cout : (index + 1) * cout, :cout] = one
            mats[index * cout : (index + 1) * cout, cout:] = two
        rowsbuf[0:1, :cout] = average
        rowsbuf[1:2, :cout] = bias
        rowsbuf[1:2, cout:] = offs
        scaled = color_sum * scaling
        grad_colors[0] = scaled[:half, :half]
        grad_colors[1] = pltpu.roll(scaled[half:], half, 1)[:, :half]
        acc[...] = jnp.zeros_like(acc)
        turned[...] = jnp.zeros_like(turned)

    top, bot = sides(ahead[0], across[0])
    padded = jnp.concatenate([top, img[0], bot], axis=0)
    for a in range(3):
        acc[a] += dot(turned[...], padded[a : a + rows].reshape(pixels, cin))
    full = jnp.concatenate([low[0], pre[0, 1 : rows - 1], high[0]], axis=0)
    centred = full.reshape(pixels, cout) - rowsbuf[0:1, :cout]
    big, small = split(centred)
    up = ups[0].reshape(pixels, cout)
    result = dot(jnp.concatenate([big, small, big, up, up], axis=1), mats[...]) + rowsbuf[1:2]
    colored[0] = result[:, cout:].astype(BF16).reshape(rows, width, cout)
    grad = result[:, :cout].astype(BF16)
    shaped = grad.reshape(rows, width, cout)
    pre_grad[0] = shaped
    edge_across[0], edge_ahead[0] = sides(shaped[rows - 1 :], shaped[:1])
    after, before = shifted(shaped.astype(F32))
    after = after.astype(BF16).reshape(pixels, cout)
    before = before.astype(BF16).reshape(pixels, cout)
    turned[:cout] = after.T
    turned[cout : 2 * cout] = grad.T
    turned[2 * cout :] = before.T

    @pl.when(step == last)
    def _():
        upper = is_upper(stage)
        parts = [
            acc[tap // 3, tap % 3 * cout : (tap % 3 + 1) * cout, piece * cin // 2 : (piece + 1) * cin // 2].T
            * scaling
            for tap in range(9)
            for piece in range(2)
        ]
        for index in range(9):
            place = slice(index * cin // 2, (index + 1) * cin // 2)
            keep[place] = jnp.where(upper, parts[9 + index], parts[index])
            send[place] = jnp.where(upper, parts[index], parts[9 + index])


def turn_kernel(kern, out):
    cout = kern.shape[3]
    for a in range(3):
        for c in range(3):
            tap = (a * 3 + c) * cout
            out[tap : tap + cout] = kern[a, c].T


def image_kernel(pre_grad, ahead, across, wts, *rest):
    out = rest[-1]
    top, bot = sides(ahead[0], across[0])
    rows, width, cout = pre_grad.shape[1:]
    cin = wts.shape[1]
    exact = jnp.concatenate([top, pre_grad[0], bot], axis=0).astype(F32)
    after, before = shifted(exact)
    taps = [value.astype(BF16) for value in (after, exact, before)]
    wide = jnp.concatenate(
        [taps[c][2 - a : 2 - a + rows] for a in range(3) for c in range(3)], axis=2
    )
    result = dot(wide.reshape(rows * width, 9 * cout), wts[...])
    out[0] = result.astype(BF16).reshape(rows, width, cin)


def fold_kernel(stage, value, received, keep, send):
    upper = is_upper(stage)
    part = keep.shape[0]
    low = value[:part] + received[:part]
    high = value[part:] + received[part:]
    keep[...] = jnp.where(upper, high, low)
    send[...] = jnp.where(upper, low, high)


def join_kernel(stage, value, received, out):
    upper = is_upper(stage)
    part = value.shape[0]
    out[:part] = jnp.where(upper, received[...], value[...])
    out[part:] = jnp.where(upper, value[...], received[...])


def finish_kernel(stage, value, received, out):
    size = out.shape[0]
    steps = value.shape[0] // size
    step = pl.program_id(0)
    place = pl.ds(pl.multiple_of(step % steps * size, size), size)
    own = is_upper(stage) == (step >= steps)
    out[...] = jnp.where(own, value[place], received[place]).astype(F32)


def image_spec(shape, place=lambda b: b):
    return pl.BlockSpec((1, *shape[1:]), lambda b: (place(b),) + (0,) * (len(shape) - 1))


def whole_spec(shape):
    return pl.BlockSpec(shape, lambda b: (0,) * len(shape))


def in_hbm(value):
    return pltpu.with_memory_space_constraint(value, pltpu.HBM)


def resident():
    return pl.BlockSpec(memory_space=pltpu.VMEM)


def row_spec(shape, row):
    return pl.BlockSpec((shape[0], 1, *shape[2:]), lambda b: (0, row, 0, 0))


def forward(images, kernel, upstream):
    count, rows, width, cin = images.shape
    cout = kernel.shape[3]
    pre_shape = (count, rows, width, cout)
    return pl.pallas_call(
        forward_kernel,
        grid=(count,),
        in_specs=[
            image_spec(images.shape),
            whole_spec(kernel.shape),
            image_spec(upstream.shape),
        ],
        out_specs=[
            image_spec(pre_shape),
            whole_spec((2 * cout, 2 * cout)),
            whole_spec((8, cout)),
        ],
        out_shape=[
            jax.ShapeDtypeStruct(pre_shape, F32),
            jax.ShapeDtypeStruct((2 * cout, 2 * cout), F32),
            jax.ShapeDtypeStruct((8, cout), F32),
        ],
        scratch_shapes=[
            pltpu.VMEM((3 * cin, 3 * cout), BF16),
            pltpu.VMEM(((rows - 2) * width, 3 * cout), BF16),
        ],
        compiler_params=pltpu.CompilerParams(vmem_limit_bytes=20 * MIB),
        cost_estimate=pl.CostEstimate(
            flops=2 * count * rows * width * 9 * cin * cout,
            bytes_accessed=2 * images.size + 2 * upstream.size + 4 * upstream.size,
            transcendentals=0,
        ),
        name="forward_inner",
    )(
        in_hbm(images), in_hbm(kernel), in_hbm(upstream)
    )


def edges(stage, top, bot, pre, upstream, kernel, acc, sums):
    count, rows, width, cout = pre.shape
    edge = (count, 1, width, cout)

    part = (cout + 16) // 2
    shapes = [edge, edge, (part, cout), (part, cout)]
    return pl.pallas_call(
        functools.partial(edge_kernel, count * rows * width, stage),
        grid=(1,),
        in_specs=[
            resident(),
            resident(),
            row_spec(pre.shape, 0),
            row_spec(pre.shape, rows - 1),
            row_spec(upstream.shape, 0),
            row_spec(upstream.shape, rows - 1),
            resident(),
            resident(),
            resident(),
        ],
        out_specs=[whole_spec(edge), whole_spec(edge), resident(), resident()],
        out_shape=[jax.ShapeDtypeStruct(shape, F32) for shape in shapes],
        scratch_shapes=[pltpu.VMEM((2 * part, cout), F32)],
        compiler_params=pltpu.CompilerParams(vmem_limit_bytes=12 * MIB),
        cost_estimate=pl.CostEstimate(
            flops=2 * 2 * count * width * 3 * top.shape[3] * cout,
            bytes_accessed=4 * top.size + 24 * count * width * cout,
            transcendentals=0,
        ),
        name="forward_edges",
    )(top, bot, pre, pre, upstream, upstream, kernel, acc, sums)


def backward(total_pix, stage, own, other, colors, offset, pre, low, high, upstream, images, top, bot):
    count, rows, width, cin = images.shape
    cout = upstream.shape[3]
    half = cout // 2
    edge = (count, 1, width, cout)

    def here(b):
        return jnp.minimum(b, count - 1)

    def behind(b):
        return jnp.maximum(b - 1, 0)

    out_shapes = [
        (upstream.shape, BF16),
        (upstream.shape, BF16),
        (edge, BF16),
        (edge, BF16),
        ((9 * cin // 2, cout), F32),
        ((9 * cin // 2, cout), F32),
        ((2, half, half), F32),
    ]
    return pl.pallas_call(
        functools.partial(backward_kernel, total_pix, stage),
        grid=(count + 1,),
        in_specs=[
            resident(),
            resident(),
            resident(),
            resident(),
            image_spec(pre.shape, here),
            image_spec(low.shape, here),
            image_spec(high.shape, here),
            image_spec(upstream.shape, here),
            image_spec(images.shape, behind),
            image_spec(top.shape, behind),
            image_spec(bot.shape, behind),
        ],
        out_specs=[image_spec(shape, here) for shape, _ in out_shapes[:4]]
        + [resident(), resident(), resident()],
        out_shape=[jax.ShapeDtypeStruct(shape, dtype) for shape, dtype in out_shapes],
        scratch_shapes=[
            pltpu.VMEM((cout + 16, cout), F32),
            pltpu.VMEM((5 * cout, 2 * cout), BF16),
            pltpu.VMEM((8, 2 * cout), F32),
            pltpu.VMEM((3, 3 * cout, cin), F32),
            pltpu.VMEM((3 * cout, rows * width), BF16),
        ],
        compiler_params=pltpu.CompilerParams(vmem_limit_bytes=20 * MIB),
        cost_estimate=pl.CostEstimate(
            flops=2 * count * rows * width * 11 * cin * cout,
            bytes_accessed=2 * images.size + 10 * upstream.size,
            transcendentals=0,
        ),
        name="whitening_backward",
    )(own, other, colors, offset, pre, low, high, upstream, images, top, bot)


def turned_weights(kernel):
    cin, cout = kernel.shape[2:]
    return pl.pallas_call(
        turn_kernel,
        out_shape=jax.ShapeDtypeStruct((9 * cout, cin), BF16),
        compiler_params=pltpu.CompilerParams(vmem_limit_bytes=4 * MIB),
        name="turned_weights",
    )(kernel)


def image_gradient(first, count, pre_grad, top, bot, turned, out=None):
    images, rows, width, cout = pre_grad.shape
    cin = turned.shape[1]
    shape = (images, rows, width, cin)

    def place(b):
        return b + first

    operands = [pre_grad, top, bot, turned]
    in_specs = [image_spec(part.shape, place) for part in operands[:3]]
    in_specs.append(whole_spec(turned.shape))
    aliases = {}
    if out is not None:
        operands.append(out)
        in_specs.append(pl.BlockSpec(memory_space=pl.ANY))
        aliases = {4: 0}
    return pl.pallas_call(
        image_kernel,
        grid=(count,),
        in_specs=in_specs,
        out_specs=image_spec(shape, place),
        out_shape=jax.ShapeDtypeStruct(shape, BF16),
        input_output_aliases=aliases,
        compiler_params=pltpu.CompilerParams(vmem_limit_bytes=12 * MIB),
        cost_estimate=pl.CostEstimate(
            flops=2 * count * rows * width * 9 * cin * cout,
            bytes_accessed=2 * count * rows * width * (cin + cout),
            transcendentals=0,
        ),
        name="image_gradient",
    )(*operands)


def sliced(images):
    count, rows, width, cin = images.shape
    shape = (count, 1, width, cin)
    source = in_hbm(images)
    return pl.pallas_call(
        slice_kernel,
        grid=(1,),
        in_specs=[row_spec(images.shape, 0), row_spec(images.shape, rows - 1)],
        out_specs=[resident(), resident()],
        out_shape=[jax.ShapeDtypeStruct(shape, BF16)] * 2,
        compiler_params=pltpu.CompilerParams(vmem_limit_bytes=8 * MIB),
        name="edge_rows",
    )(source, source)


def small_call(kernel, name, *operands, out):
    return pl.pallas_call(
        kernel,
        in_specs=[resident()] * len(operands),
        out_specs=[resident()] * len(out),
        out_shape=out,
        compiler_params=pltpu.CompilerParams(vmem_limit_bytes=4 * MIB),
        name=name,
    )(*operands)


def fold(value, received, stage):
    half = jax.ShapeDtypeStruct((value.shape[0] // 2, value.shape[1]), value.dtype)
    return small_call(
        functools.partial(fold_kernel, stage), "fold", value, received, out=[half, half]
    )


def join(value, received, stage):
    whole = jax.ShapeDtypeStruct((value.shape[0] * 2, value.shape[1]), value.dtype)
    return small_call(
        functools.partial(join_kernel, stage), "join", value, received, out=[whole]
    )[0]


def finish(value, received, stage):
    part, lanes = value.shape
    size = part // 2
    return pl.pallas_call(
        functools.partial(finish_kernel, stage),
        grid=(4,),
        in_specs=[resident(), resident()],
        out_specs=pl.BlockSpec((size, lanes), lambda b: (b, 0)),
        out_shape=jax.ShapeDtypeStruct((2 * part, lanes), F32),
        compiler_params=pltpu.CompilerParams(vmem_limit_bytes=8 * MIB),
        name="finish",
    )(value, received)


def halos(ahead, across):
    count = lax.axis_size("rows")
    pairs = []
    for first in (0, 1):
        found = [(i, i + 1) for i in range(first, count - 1, 2)]
        pairs.append(found + [(i, j) for j, i in found])
    return lax.ppermute(ahead, "rows", pairs[0]), lax.ppermute(across, "rows", pairs[1])


def exchange(value, devices, stage):
    pairs = [(i, i ^ (stage[1] if i & 1 else stage[0])) for i in range(devices)]
    return lax.ppermute(value, AXES, pairs)


def beside(send, devices, stage, task, operands):
    send, operands = lax.optimization_barrier((send, operands))
    received = exchange(send, devices, stage)
    result = task(*operands)
    return lax.optimization_barrier((received, result))


def body(images, kernel, colors, offset, upstream):
    count, rows, width, cin = images.shape
    cout = kernel.shape[3]
    devices = lax.axis_size("dp") * lax.axis_size("rows")
    total_pix = count * rows * width * devices
    plan = stages(devices)
    top, bot = halos(*sliced(images))
    pre, acc, sums = forward(images, kernel, upstream)
    low, high, value, send = edges(plan[0], top, bot, pre, upstream, kernel, acc, sums)
    value = value + exchange(send, devices, plan[0])
    for stage in plan[1:-1]:
        value = value + exchange(value, devices, stage)
    received, turned = beside(value, devices, plan[-1], turned_weights, (kernel,))
    value = value + received
    received = exchange(value, devices, plan[0])
    colored, pre_grad, edge_ahead, edge_across, value, send, grad_colors = backward(
        total_pix,
        plan[0],
        value,
        received,
        colors,
        offset.reshape(1, cout),
        pre,
        low,
        high,
        upstream,
        images,
        top,
        bot,
    )
    shares = [1, 1, 2, 1, 1]
    state = {"next": 0, "grad": None}

    def transfer(send, stage):
        first = state["next"]
        if first >= count:
            return exchange(send, devices, stage)
        many = min(shares.pop(0), count - first) if shares else count - first
        state["next"] = first + many
        operands = (pre_grad, grad_top, grad_bot, turned)
        if state["grad"] is not None:
            operands = (*operands, state["grad"])
        received, state["grad"] = beside(
            send, devices, stage, functools.partial(image_gradient, first, many), operands
        )
        return received

    cuts = []
    received = exchange(send, devices, plan[0])
    for stage in plan[1:]:
        if value.shape[0] % 32 == 0 and value.shape[0] > 144:
            value, send = fold(value, received, stage)
            cuts.append(stage)
        else:
            value = send = value + received
        if stage == plan[1]:
            received, (grad_top, grad_bot) = beside(
                send, devices, stage, halos, (edge_ahead, edge_across)
            )
        else:
            received = transfer(send, stage)
    value = (value + received).astype(BF16)
    for stage in reversed(cuts):
        value = join(value, transfer(value, stage), stage)
    grad_kernel = finish(value, exchange(value, devices, plan[0]), plan[0])
    return colored, state["grad"], grad_kernel.reshape(3, 3, cin, cout), grad_colors


def solution(mesh):
    placed = (P("dp", "rows", None, None), P(), P(), P(), P("dp", "rows", None, None))
    return jax.shard_map(
        body,
        mesh=mesh,
        in_specs=placed,
        out_specs=(P("dp", "rows", None, None), P("dp", "rows", None, None), P(), P()),
        check_vma=False,
    )
```

time: 519 us -> 94.1 us (0.18); the launches traced: 510 us -> 93.9 us
  waiting for transfers between devices: 231 us -> 33.4 us
  blocking collectives: 83 us -> 0 us
  matrix products: 76.9 us -> 0 us
  local copies, waits for them, and re-layouts: 74 us -> 0.03 us
  Pallas kernels: 0 us -> 36.7 us
  other arithmetic: 19.3 us -> 0.05 us
  between operations: 15.1 us -> 0.8 us
  starting transfers between devices: 10.2 us -> 23 us
    psum x2 -> x0, waiting for transfers between devices: 231 us -> none  [the longest x1 116 us: body(): summed = lax.psum(kernel_term, ('dp', 'rows'))]
    psum x2 -> x0, blocking collectives: 83 us -> none  [the longest x1 42.5 us: body(): average = lax.psum(jnp.sum(raw_cols, axis=0), ('dp', 'rows')) / total_pix]
    dot_general x59 -> x0, matrix products: 62.2 us -> none  [the longest x40 14.3 us: batched(): return jnp.einsum('gij,gjk->gik', left, right, precision=PRECISE)]
    pallas_call x0 -> x17, Pallas kernels: none -> 36.7 us  [the longest x1 13.4 us: backward(): pl.pallas_call(functools.partial(backward_kernel, total_pix, stage), grid...]
    ppermute x4 -> x19, waiting for transfers between devices: 0.01 us -> 33.4 us  [the longest x15 33 us: exchange(): return lax.ppermute(value, AXES, pairs)]
    conv_general_dilated x7 -> x0, local copies, waits for them, and re-layouts: 21.9 us -> none  [filter_valid(): lax.conv_general_dilated(source, weights, (1, 1), 'VALID', dimension_numb...]
    slice x3 -> x0, local copies, waits for them, and re-layouts: 17.9 us -> none  [the longest x1 13.9 us: body(): padded[:, row_off:row_off + band_rows, col_off:col_off + width_n, :]]
    conv_general_dilated x2 -> x0, matrix products: 14.7 us -> none  [filter_valid(): lax.conv_general_dilated(source, weights, (1, 1), 'VALID', dimension_numb...]
  transfers between devices with their start and end apart: 6 -> 19, of which waited for: 2 -> 16; matrix products, arithmetic and copies ran while one was open for 9% -> 0% of each run, Pallas kernels for 0% -> 20%
where the time goes in v1:
time: 94.1 us; the launch traced here: 93.9 us
  Pallas kernels  36.7 us (39%)
  waiting for transfers between devices  33.4 us (35%)
  starting transfers between devices  23 us (24%)
    ppermute x15, waiting for transfers between devices, exchange(): return lax.ppermute(value, AXES, pairs)  33 us
    ppermute x15, starting transfers between devices, exchange(): return lax.ppermute(value, AXES, pairs)  20.1 us
    pallas_call x1, Pallas kernels, backward(): pl.pallas_call(functools.partial(backward_kernel, total_pix, stage), grid...  13.4 us
    pallas_call x1, Pallas kernels, forward(): pl.pallas_call(forward_kernel, grid=(count,), in_specs=[image_spec(images...  9.79 us
    pallas_call x5, Pallas kernels, image_gradient(): pl.pallas_call(image_kernel, grid=(count,), in_specs=in_specs, out_specs=...  9.1 us
  transfers between devices with their start and end apart: 19, of which 16 were waited for; matrix products, arithmetic and copies ran while one was open for 0% of the time, Pallas kernels for 20%

profile of v1, /device:TPU:0, one launch (start us, length us, event | category | flops | bytes accessed | tf_op | source)
XLA Modules:
  0.0 93.9 jit_solution(18257272348756962331)
XLA Ops:
  3.2 9.8 %forward_inner.1 = (f32[6,8,128,128]{3,2,1,0:T(8,128)S(1)}, f32[256,256]{1,0:T(8,128)S(1)}, f32[8,128]{1,0:T(8,128)S(1)}) custom-call(bf16[6,8,128,256]{3,2,1,0:T(8,128)(2,1)} %img.3, bf16[3,3,256,128]{3,2,1,0:T(8,128)(2,1)} %kern.4, bf16[6,8,128,128]{3,2,1,0:T(8,128)(2,1)} %ups.3), custom_call_target="tpu_custom_call" | custom-call | flops 3623878656 | bytes 7864320 | tf_op jit(solution)/shard_map/forward_inner/pallas_call | solution.py:437
  14.2 3.9 %collective-permute-start.2 = (f32[72,128]{1,0:T(8,128)S(1)}, f32[72,128]{1,0:T(8,128)S(1)}, u32[]{:S(2)}, u32[]{:S(2)}) collective-permute-start(f32[72,128]{1,0:T(8,128)S(1)} %get-tuple-element.81), channel_id=1, source_target_pairs={{0,1},{1,0},{2,3},{3,2},{4,5},{5,4},{6,7},{7,6},{8,9},{9,8},{10,11... | collective-permute-start | bytes 110600 | tf_op jit(solution)/shard_map/ppermute | solution.py:669
  19.2 3.7 %collective-permute-done.3 = f32[72,128]{1,0:T(8,128)S(1)} collective-permute-done((f32[72,128]{1,0:T(8,128)S(1)}, f32[72,128]{1,0:T(8,128)S(1)}, u32[]{:S(2)}, u32[]{:S(2)}) %collective-permute-start.3) | collective-permute-done | bytes 36896 | tf_op jit(solution)/shard_map/ppermute | solution.py:669
  24.4 2.5 %collective-permute-done.4 = f32[72,128]{1,0:T(8,128)S(1)} collective-permute-done((f32[72,128]{1,0:T(8,128)S(1)}, f32[72,128]{1,0:T(8,128)S(1)}, u32[]{:S(2)}, u32[]{:S(2)}) %collective-permute-start.4) | collective-permute-done | bytes 36896 | tf_op jit(solution)/shard_map/ppermute | solution.py:669
  26.8 1.6 %collective-permute-start.5 = (f32[72,128]{1,0:T(8,128)S(1)}, f32[72,128]{1,0:T(8,128)S(1)}, u32[]{:S(2)}, u32[]{:S(2)}) collective-permute-start(f32[72,128]{1,0:T(8,128)S(1)} %add.23), channel_id=1, source_target_pairs={{0,8},{1,9},{2,10},{3,11},{4,12},{5,13},{6,14},{7,15},{8,0},{9,1},... | collective-permute-start | bytes 110600 | tf_op jit(solution)/shard_map/ppermute | solution.py:669
  28.4 2.4 %collective-permute-done.5 = f32[72,128]{1,0:T(8,128)S(1)} collective-permute-done((f32[72,128]{1,0:T(8,128)S(1)}, f32[72,128]{1,0:T(8,128)S(1)}, u32[]{:S(2)}, u32[]{:S(2)}) %collective-permute-start.5) | collective-permute-done | bytes 36896 | tf_op jit(solution)/shard_map/ppermute | solution.py:669
  30.8 2.8 %collective-permute-start.6 = (f32[72,128]{1,0:T(8,128)S(1)}, f32[72,128]{1,0:T(8,128)S(1)}, u32[]{:S(2)}, u32[]{:S(2)}) collective-permute-start(f32[72,128]{1,0:T(8,128)S(1)} %add.24), channel_id=1, source_target_pairs={{0,16},{1,17},{2,18},{3,19},{4,20},{5,21},{6,22},{7,23},{8,24},{9,... | collective-permute-start | bytes 110600 | tf_op jit(solution)/shard_map/ppermute | solution.py:669
  33.8 1.9 %collective-permute-done.6 = f32[72,128]{1,0:T(8,128)S(1)} collective-permute-done((f32[72,128]{1,0:T(8,128)S(1)}, f32[72,128]{1,0:T(8,128)S(1)}, u32[]{:S(2)}, u32[]{:S(2)}) %collective-permute-start.6) | collective-permute-done | bytes 36896 | tf_op jit(solution)/shard_map/ppermute | solution.py:669
  36.9 13.4 %whitening_backward.1 = (bf16[6,8,128,128]{3,2,1,0:T(8,128)(2,1)}, bf16[6,8,128,128]{3,2,1,0:T(8,128)(2,1)S(1)}, bf16[6,1,128,128]{3,2,1,0:T(8,128)(2,1)S(1)}, b...) custom-call(f32[72,128]{1,0:T(8,128)S(1)} %add.25.own, ...), custom_call_target="tpu_custom_call" | custom-call | flops 4429185024 | bytes 11010048 | tf_op jit(solution)/shard_map/whitening_backward/pallas_call | solution.py:525
  50.4 1.9 %collective-permute-done.8.received = f32[1152,128]{1,0:T(8,128)S(1)} collective-permute-done((f32[1152,128]{1,0:T(8,128)S(1)}, f32[1152,128]{1,0:T(8,128)S(1)}, u32[]{:S(2)}, u32[]{:S(2)}) %collective-permute-start.8) | collective-permute-done | bytes 589856 | tf_op jit(solution)/shard_map/ppermute | solution.py:669
  54.9 4.3 %collective-permute-done.9.received = f32[576,128]{1,0:T(8,128)S(1)} collective-permute-done((f32[576,128]{1,0:T(8,128)S(1)}, f32[576,128]{1,0:T(8,128)S(1)}, u32[]{:S(2)}, u32[]{:S(2)}) %collective-permute-start.9) | collective-permute-done | bytes 294944 | tf_op jit(solution)/shard_map/ppermute | solution.py:669
  60.8 1.6 %image_gradient.5.rest_0_ = bf16[6,8,128,256]{3,2,1,0:T(8,128)(2,1)} custom-call(bf16[6,8,128,128]{3,2,1,0:T(8,128)(2,1)S(1)} %get-tuple-element.138.pre_grad, bf16[6,1,128,128]{3,2,1,0:T(8,128)(2,1)S(1)} %collective-permute-done.10.ahead, bf16[6,1,128,128]{3,2,1,0:T(8,128)(2,1)S(1)} %collective-permute-done.11.across, bf16[1152,256]{1,0:T(8,128)(2,1)S(1)} %turned_weights.1.wts), custom_call_target="tpu_custom_call" | custom-call | flops 603979776 | bytes 786432 | tf_op jit(solution)/shard_map/image_gradient/pallas_call | solution.py:587
  62.4 2.0 %collective-permute-done.12.received = f32[288,128]{1,0:T(8,128)S(1)} collective-permute-done((f32[288,128]{1,0:T(8,128)S(1)}, f32[288,128]{1,0:T(8,128)S(1)}, u32[]{:S(2)}, u32[]{:S(2)}) %collective-permute-start.12) | collective-permute-done | bytes 147488 | tf_op jit(solution)/shard_map/ppermute | solution.py:669
  64.5 1.6 %collective-permute-start.13 = (f32[144,128]{1,0:T(8,128)S(1)}, f32[144,128]{1,0:T(8,128)S(1)}, u32[]{:S(2)}, u32[]{:S(2)}) collective-permute-start(f32[144,128]{1,0:T(8,128)S(1)} %get-tuple-element.113), channel_id=1, source_target_pairs={{0,8},{1,9},{2,10},{3,11},{4,12},{5,13},{6,14},{7,15},{8,0},{9,1},... | collective-permute-start | bytes 221192 | tf_op jit(solution)/shard_map/ppermute | solution.py:669
  66.1 1.6 %image_gradient.6.rest_0_ = bf16[6,8,128,256]{3,2,1,0:T(8,128)(2,1)} custom-call(bf16[6,8,128,128]{3,2,1,0:T(8,128)(2,1)S(1)} %get-tuple-element.138.pre_grad, bf16[6,1,128,128]{3,2,1,0:T(8,128)(2,1)S(1)} %collective-permute-done.10.ahead, bf16[6,1,128,128]{3,2,1,0:T(8,128)(2,1)S(1)} %collective-permute-done.11.across, ...), custom_call_target="tpu_custom_call", output_to_operand_aliasing={{}: (4, {})} | custom-call | flops 603979776 | bytes 786432 | tf_op jit(solution)/shard_map/image_gradient/pallas_call | solution.py:587
  67.8 1.7 %collective-permute-done.13 = f32[144,128]{1,0:T(8,128)S(1)} collective-permute-done((f32[144,128]{1,0:T(8,128)S(1)}, f32[144,128]{1,0:T(8,128)S(1)}, u32[]{:S(2)}, u32[]{:S(2)}) %collective-permute-start.13) | collective-permute-done | bytes 73760 | tf_op jit(solution)/shard_map/ppermute | solution.py:669
  69.5 2.9 %collective-permute-start.14 = (f32[144,128]{1,0:T(8,128)S(1)}, f32[144,128]{1,0:T(8,128)S(1)}, u32[]{:S(2)}, u32[]{:S(2)}) collective-permute-start(f32[144,128]{1,0:T(8,128)S(1)} %add.26), channel_id=1, source_target_pairs={{0,16},{1,17},{2,18},{3,19},{4,20},{5,21},{6,22},{7,23},{8,24},{9,... | collective-permute-start | bytes 221192 | tf_op jit(solution)/shard_map/ppermute | solution.py:669
  72.4 2.5 %image_gradient.7.rest_0_ = bf16[6,8,128,256]{3,2,1,0:T(8,128)(2,1)} custom-call(bf16[6,8,128,128]{3,2,1,0:T(8,128)(2,1)S(1)} %get-tuple-element.138.pre_grad, bf16[6,1,128,128]{3,2,1,0:T(8,128)(2,1)S(1)} %collective-permute-done.10.ahead, bf16[6,1,128,128]{3,2,1,0:T(8,128)(2,1)S(1)} %collective-permute-done.11.across, ...), custom_call_target="tpu_custom_call", output_to_operand_aliasing={{}: (4, {})} | custom-call | flops 1207959552 | bytes 1572864 | tf_op jit(solution)/shard_map/image_gradient/pallas_call | solution.py:587
  77.2 1.6 %image_gradient.8.rest_0_ = bf16[6,8,128,256]{3,2,1,0:T(8,128)(2,1)} custom-call(bf16[6,8,128,128]{3,2,1,0:T(8,128)(2,1)S(1)} %get-tuple-element.138.pre_grad, bf16[6,1,128,128]{3,2,1,0:T(8,128)(2,1)S(1)} %collective-permute-done.10.ahead, bf16[6,1,128,128]{3,2,1,0:T(8,128)(2,1)S(1)} %collective-permute-done.11.across, ...), custom_call_target="tpu_custom_call", output_to_operand_aliasing={{}: (4, {})} | custom-call | flops 603979776 | bytes 786432 | tf_op jit(solution)/shard_map/image_gradient/pallas_call | solution.py:587
  78.8 1.6 %collective-permute-done.15.received = bf16[144,128]{1,0:T(8,128)(2,1)S(1)} collective-permute-done((bf16[144,128]{1,0:T(8,128)(2,1)S(1)}, bf16[144,128]{1,0:T(8,128)(2,1)S(1)}, u32[]{:S(2)}, u32[]{:S(2)}) %collective-permute-start.15) | collective-permute-done | bytes 36896 | tf_op jit(solution)/shard_map/ppermute | solution.py:669
  82.0 1.6 %image_gradient.9 = bf16[6,8,128,256]{3,2,1,0:T(8,128)(2,1)} custom-call(bf16[6,8,128,128]{3,2,1,0:T(8,128)(2,1)S(1)} %get-tuple-element.138.pre_grad, bf16[6,1,128,128]{3,2,1,0:T(8,128)(2,1)S(1)} %collective-permute-done.10.ahead, bf16[6,1,128,128]{3,2,1,0:T(8,128)(2,1)S(1)} %collective-permute-done.11.across, ...), custom_call_target="tpu_custom_call", output_to_operand_aliasing={{}: (4, {})} | custom-call | flops 603979776 | bytes 786432 | tf_op jit(solution)/shard_map/image_gradient/pallas_call | solution.py:587
  83.7 1.7 %collective-permute-done.16.received = bf16[288,128]{1,0:T(8,128)(2,1)S(1)} collective-permute-done((bf16[288,128]{1,0:T(8,128)(2,1)S(1)}, bf16[288,128]{1,0:T(8,128)(2,1)S(1)}, u32[]{:S(2)}, u32[]{:S(2)}) %collective-permute-start.16) | collective-permute-done | bytes 73760 | tf_op jit(solution)/shard_map/ppermute | solution.py:669
  86.4 4.2 %collective-permute-done.17.received = bf16[576,128]{1,0:T(8,128)(2,1)S(1)} collective-permute-done((bf16[576,128]{1,0:T(8,128)(2,1)S(1)}, bf16[576,128]{1,0:T(8,128)(2,1)S(1)}, u32[]{:S(2)}, u32[]{:S(2)}) %collective-permute-start.17) | collective-permute-done | bytes 147488 | tf_op jit(solution)/shard_map/ppermute | solution.py:669
  92.3 1.6 %finish.1 = f32[2304,128]{1,0:T(8,128)} custom-call(bf16[1152,128]{1,0:T(8,128)(2,1)S(1)} %join.5.value, bf16[1152,128]{1,0:T(8,128)(2,1)S(1)} %collective-permute-done.18.received), custom_call_target="tpu_custom_call" | custom-call | tf_op jit(solution)/shard_map/finish/pallas_call | solution.py:647
  (48 shorter events, 18.6 us)
Async XLA Ops:
  1.8 11.1 %collective-permute-start = (bf16[6,1,128,256]{3,2,1,0:T(8,128)(2,1)S(1)}, bf16[6,1,128,256]{3,2,1,0:T(8,128)(2,1)S(1)}, u32[]{:S(2)}, u32[]{:S(2)}) collective-permute-start(bf16[6,1,128,256]{3,2,1,0:T(8,128)(2,1)S(1)} %get-tuple-element.75), channel_id=1, source_target_pairs={{0,1},{2,3},{1,0},{3,2},{4,5},{6,7},{5,4},{7,6},{8,9},{10,11},{9,8... | collective-permute-start | bytes 1179656 | tf_op jit(solution)/shard_map/ppermute | solution.py:664
  2.4 10.6 %copy-start.1 = (bf16[6,8,128,128]{3,2,1,0:T(8,128)(2,1)S(1)}, bf16[6,8,128,128]{3,2,1,0:T(8,128)(2,1)}, u32[]{:S(2)}) copy-start(bf16[6,8,128,128]{3,2,1,0:T(8,128)(2,1)} %ups.3) | copy-start | bytes 4718596
  2.4 10.6 %copy-start.2 = (bf16[3,3,256,128]{3,2,1,0:T(8,128)(2,1)S(1)}, bf16[3,3,256,128]{3,2,1,0:T(8,128)(2,1)}, u32[]{:S(2)}) copy-start(bf16[3,3,256,128]{3,2,1,0:T(8,128)(2,1)} %kern.4) | copy-start | bytes 1769476
  2.4 10.6 %collective-permute-start.1 = (bf16[6,1,128,256]{3,2,1,0:T(8,128)(2,1)S(1)}, bf16[6,1,128,256]{3,2,1,0:T(8,128)(2,1)S(1)}, u32[]{:S(2)}, u32[]{:S(2)}) collective-permute-start(bf16[6,1,128,256]{3,2,1,0:T(8,128)(2,1)S(1)} %get-tuple-element.76), channel_id=1, source_target_pairs={{1,2},{2,1},{5,6},{6,5},{9,10},{10,9},{13,14},{14,13},{17,18},{18,... | collective-permute-start | bytes 1179656 | tf_op jit(solution)/shard_map/ppermute | solution.py:664
  13.0 23.9 %copy-start = (bf16[6,8,128,256]{3,2,1,0:T(8,128)(2,1)S(1)}, bf16[6,8,128,256]{3,2,1,0:T(8,128)(2,1)}, u32[]{:S(2)}) copy-start(bf16[6,8,128,256]{3,2,1,0:T(8,128)(2,1)} %img.3) | copy-start | bytes 9437188
  13.0 23.9 %copy-start.3 = (f32[2,64,64]{2,1,0:T(8,128)S(1)}, f32[2,64,64]{2,1,0:T(8,128)}, u32[]{:S(2)}) copy-start(f32[2,64,64]{2,1,0:T(8,128)} %colors.1) | copy-start | bytes 98308
  13.0 23.9 %copy-start.4 = (f32[128]{0:T(128)S(1)}, f32[128]{0:T(128)}, u32[]{:S(2)}) copy-start(f32[128]{0:T(128)} %param.8) | copy-start | bytes 1540
  14.2 4.7 %collective-permute-start.2 = (f32[72,128]{1,0:T(8,128)S(1)}, f32[72,128]{1,0:T(8,128)S(1)}, u32[]{:S(2)}, u32[]{:S(2)}) collective-permute-start(f32[72,128]{1,0:T(8,128)S(1)} %get-tuple-element.81), channel_id=1, source_target_pairs={{0,1},{1,0},{2,3},{3,2},{4,5},{5,4},{6,7},{7,6},{8,9},{9,8},{10,11... | collective-permute-start | bytes 110600 | tf_op jit(solution)/shard_map/ppermute | solution.py:669
  18.9 4.0 %collective-permute-start.3 = (f32[72,128]{1,0:T(8,128)S(1)}, f32[72,128]{1,0:T(8,128)S(1)}, u32[]{:S(2)}, u32[]{:S(2)}) collective-permute-start(f32[72,128]{1,0:T(8,128)S(1)} %add.21), channel_id=1, source_target_pairs={{0,2},{1,5},{2,0},{3,7},{4,6},{5,1},{6,4},{7,3},{8,10},{9,13},{10,... | collective-permute-start | bytes 110600 | tf_op jit(solution)/shard_map/ppermute | solution.py:669
  22.9 4.0 %collective-permute-start.4 = (f32[72,128]{1,0:T(8,128)S(1)}, f32[72,128]{1,0:T(8,128)S(1)}, u32[]{:S(2)}, u32[]{:S(2)}) collective-permute-start(f32[72,128]{1,0:T(8,128)S(1)} %add.22), channel_id=1, source_target_pairs={{0,4},{1,3},{2,6},{3,1},{4,0},{5,7},{6,2},{7,5},{8,12},{9,11},{10,... | collective-permute-start | bytes 110600 | tf_op jit(solution)/shard_map/ppermute | solution.py:669
  26.8 4.0 %collective-permute-start.5 = (f32[72,128]{1,0:T(8,128)S(1)}, f32[72,128]{1,0:T(8,128)S(1)}, u32[]{:S(2)}, u32[]{:S(2)}) collective-permute-start(f32[72,128]{1,0:T(8,128)S(1)} %add.23), channel_id=1, source_target_pairs={{0,8},{1,9},{2,10},{3,11},{4,12},{5,13},{6,14},{7,15},{8,0},{9,1},... | collective-permute-start | bytes 110600 | tf_op jit(solution)/shard_map/ppermute | solution.py:669
  30.8 4.9 %collective-permute-start.6 = (f32[72,128]{1,0:T(8,128)S(1)}, f32[72,128]{1,0:T(8,128)S(1)}, u32[]{:S(2)}, u32[]{:S(2)}) collective-permute-start(f32[72,128]{1,0:T(8,128)S(1)} %add.24), channel_id=1, source_target_pairs={{0,16},{1,17},{2,18},{3,19},{4,20},{5,21},{6,22},{7,23},{8,24},{9,... | collective-permute-start | bytes 110600 | tf_op jit(solution)/shard_map/ppermute | solution.py:669
  35.7 1.2 %collective-permute-start.7 = (f32[72,128]{1,0:T(8,128)S(1)}, f32[72,128]{1,0:T(8,128)S(1)}, u32[]{:S(2)}, u32[]{:S(2)}) collective-permute-start(f32[72,128]{1,0:T(8,128)S(1)} %add.25.own), channel_id=1, source_target_pairs={{0,1},{1,0},{2,3},{3,2},{4,5},{5,4},{6,7},{7,6},{8,9},{9,8},{10,11... | collective-permute-start | bytes 110600 | tf_op jit(solution)/shard_map/ppermute | solution.py:669
  50.3 2.0 %collective-permute-start.8 = (f32[1152,128]{1,0:T(8,128)S(1)}, f32[1152,128]{1,0:T(8,128)S(1)}, u32[]{:S(2)}, u32[]{:S(2)}) collective-permute-start(f32[1152,128]{1,0:T(8,128)S(1)} %get-tuple-element.89), channel_id=1, source_target_pairs={{0,1},{1,0},{2,3},{3,2},{4,5},{5,4},{6,7},{7,6},{8,9},{9,8},{10,11... | collective-permute-start | bytes 1769480 | tf_op jit(solution)/shard_map/ppermute | solution.py:669
  52.4 6.8 %collective-permute-start.9 = (f32[576,128]{1,0:T(8,128)S(1)}, f32[576,128]{1,0:T(8,128)S(1)}, u32[]{:S(2)}, u32[]{:S(2)}) collective-permute-start(f32[576,128]{1,0:T(8,128)S(1)} %get-tuple-element.94), channel_id=1, source_target_pairs={{0,2},{1,5},{2,0},{3,7},{4,6},{5,1},{6,4},{7,3},{8,10},{9,13},{10,... | collective-permute-start | bytes 884744 | tf_op jit(solution)/shard_map/ppermute | solution.py:669
  52.9 1.9 %collective-permute-start.10 = (bf16[6,1,128,128]{3,2,1,0:T(8,128)(2,1)S(1)}, bf16[6,1,128,128]{3,2,1,0:T(8,128)(2,1)S(1)}, u32[]{:S(2)}, u32[]{:S(2)}) collective-permute-start(bf16[6,1,128,128]{3,2,1,0:T(8,128)(2,1)S(1)} %get-tuple-element.95), channel_id=1, source_target_pairs={{0,1},{2,3},{1,0},{3,2},{4,5},{6,7},{5,4},{7,6},{8,9},{10,11},{9,8... | collective-permute-start | bytes 589832 | tf_op jit(solution)/shard_map/ppermute | solution.py:664
  53.8 1.1 %collective-permute-start.11 = (bf16[6,1,128,128]{3,2,1,0:T(8,128)(2,1)S(1)}, bf16[6,1,128,128]{3,2,1,0:T(8,128)(2,1)S(1)}, u32[]{:S(2)}, u32[]{:S(2)}) collective-permute-start(bf16[6,1,128,128]{3,2,1,0:T(8,128)(2,1)S(1)} %get-tuple-element.96), channel_id=1, source_target_pairs={{1,2},{2,1},{5,6},{6,5},{9,10},{10,9},{13,14},{14,13},{17,18},{18,... | collective-permute-start | bytes 589832 | tf_op jit(solution)/shard_map/ppermute | solution.py:664
  59.2 5.2 %collective-permute-start.12 = (f32[288,128]{1,0:T(8,128)S(1)}, f32[288,128]{1,0:T(8,128)S(1)}, u32[]{:S(2)}, u32[]{:S(2)}) collective-permute-start(f32[288,128]{1,0:T(8,128)S(1)} %get-tuple-element.104), channel_id=1, source_target_pairs={{0,4},{1,3},{2,6},{3,1},{4,0},{5,7},{6,2},{7,5},{8,12},{9,11},{10,... | collective-permute-start | bytes 442376 | tf_op jit(solution)/shard_map/ppermute | solution.py:669
  64.5 5.0 %collective-permute-start.13 = (f32[144,128]{1,0:T(8,128)S(1)}, f32[144,128]{1,0:T(8,128)S(1)}, u32[]{:S(2)}, u32[]{:S(2)}) collective-permute-start(f32[144,128]{1,0:T(8,128)S(1)} %get-tuple-element.113), channel_id=1, source_target_pairs={{0,8},{1,9},{2,10},{3,11},{4,12},{5,13},{6,14},{7,15},{8,0},{9,1},... | collective-permute-start | bytes 221192 | tf_op jit(solution)/shard_map/ppermute | solution.py:669
  69.5 6.9 %collective-permute-start.14 = (f32[144,128]{1,0:T(8,128)S(1)}, f32[144,128]{1,0:T(8,128)S(1)}, u32[]{:S(2)}, u32[]{:S(2)}) collective-permute-start(f32[144,128]{1,0:T(8,128)S(1)} %add.26), channel_id=1, source_target_pairs={{0,16},{1,17},{2,18},{3,19},{4,20},{5,21},{6,22},{7,23},{8,24},{9,... | collective-permute-start | bytes 221192 | tf_op jit(solution)/shard_map/ppermute | solution.py:669
  76.4 4.0 %collective-permute-start.15 = (bf16[144,128]{1,0:T(8,128)(2,1)S(1)}, bf16[144,128]{1,0:T(8,128)(2,1)S(1)}, u32[]{:S(2)}, u32[]{:S(2)}) collective-permute-start(bf16[144,128]{1,0:T(8,128)(2,1)S(1)} %add_convert_fusion.value), channel_id=1, source_target_pairs={{0,8},{1,9},{2,10},{3,11},{4,12},{5,13},{6,14},{7,15},{8,0},{9,1},... | collective-permute-start | bytes 110600 | tf_op jit(solution)/shard_map/ppermute | solution.py:669
  80.5 4.9 %collective-permute-start.16 = (bf16[288,128]{1,0:T(8,128)(2,1)S(1)}, bf16[288,128]{1,0:T(8,128)(2,1)S(1)}, u32[]{:S(2)}, u32[]{:S(2)}) collective-permute-start(bf16[288,128]{1,0:T(8,128)(2,1)S(1)} %join.3.value), channel_id=1, source_target_pairs={{0,4},{1,3},{2,6},{3,1},{4,0},{5,7},{6,2},{7,5},{8,12},{9,11},{10,... | collective-permute-start | bytes 221192 | tf_op jit(solution)/shard_map/ppermute | solution.py:669
  85.4 5.2 %collective-permute-start.17 = (bf16[576,128]{1,0:T(8,128)(2,1)S(1)}, bf16[576,128]{1,0:T(8,128)(2,1)S(1)}, u32[]{:S(2)}, u32[]{:S(2)}) collective-permute-start(bf16[576,128]{1,0:T(8,128)(2,1)S(1)} %join.4.value), channel_id=1, source_target_pairs={{0,2},{1,5},{2,0},{3,7},{4,6},{5,1},{6,4},{7,3},{8,10},{9,13},{10,... | collective-permute-start | bytes 442376 | tf_op jit(solution)/shard_map/ppermute | solution.py:669
  90.7 1.6 %collective-permute-start.18 = (bf16[1152,128]{1,0:T(8,128)(2,1)S(1)}, bf16[1152,128]{1,0:T(8,128)(2,1)S(1)}, u32[]{:S(2)}, u32[]{:S(2)}) collective-permute-start(bf16[1152,128]{1,0:T(8,128)(2,1)S(1)} %join.5.value), channel_id=1, source_target_pairs={{0,1},{1,0},{2,3},{3,2},{4,5},{5,4},{6,7},{7,6},{8,9},{9,8},{10,11... | collective-permute-start | bytes 884744 | tf_op jit(solution)/shard_map/ppermute | solution.py:669

commit v2 on v1

--- a/solution.py
+++ b/solution.py
@@ -69,6 +69,30 @@
     return prod[:, cout : 2 * cout].reshape(shape) + left + right
 
 
+def paired_rows(padded, wts, cout):
+    rows, width, cin = padded.shape[0] - 2, *padded.shape[1:]
+    pairs = rows // 2
+    parts = [
+        jnp.concatenate([padded[2 * k + a : 2 * k + a + 1] for k in range(pairs)], axis=0)
+        for a in range(4)
+    ]
+    wide = jnp.concatenate(parts, axis=2).reshape(pairs * width, 4 * cin)
+    outer = dot(wide[:, : 3 * cin], wts[: 3 * cin])
+    shared = dot(wide, wts[3 * cin : 7 * cin])
+    inner = dot(wide[:, cin:], wts[7 * cin :])
+    shape = (pairs, width, cout)
+
+    def added_up(left, middle, right):
+        _, before = shifted(left.reshape(shape))
+        after, _ = shifted(right.reshape(shape))
+        return middle.reshape(shape) + before + after
+
+    first = added_up(outer[:, :cout], outer[:, cout:], shared[:, :cout])
+    second = added_up(shared[:, cout:], inner[:, :cout], inner[:, cout:])
+    ordered = [part[k : k + 1] for k in range(pairs) for part in (first, second)]
+    return jnp.concatenate(ordered, axis=0)
+
+
 def column(row):
     size = row.shape[1]
     return jnp.broadcast_to(row, (size, size)).T
@@ -102,9 +126,15 @@
 
     @pl.when(step == 0)
     def _():
-        for a in range(3):
-            for c in range(3):
-                wts[a * cin : (a + 1) * cin, c * cout : (c + 1) * cout] = kern[a, c]
+        blank = jnp.zeros((cin, cout), BF16)
+        blocks = [(kern[a, 0], kern[a, 1]) for a in range(3)]
+        blocks += [
+            (kern[a, 2] if a < 3 else blank, kern[a - 1, 0] if a > 0 else blank) for a in range(4)
+        ]
+        blocks += [(kern[a, 1], kern[a, 2]) for a in range(3)]
+        for index, (one, two) in enumerate(blocks):
+            wts[index * cin : (index + 1) * cin, :cout] = one
+            wts[index * cin : (index + 1) * cin, cout:] = two
         acc[...] = jnp.zeros_like(acc)
         sums[...] = jnp.zeros_like(sums)
         held[...] = jnp.zeros_like(held)
@@ -112,10 +142,8 @@
     acc[...] += statistics(held[...])
     blank = jnp.zeros((1, width, cin), BF16)
     padded = jnp.concatenate([blank, img[0], blank], axis=0)
-    wide = jnp.concatenate([padded[a : a + rows] for a in range(3)], axis=2)
-    prod = dot(wide.reshape(rows * width, 3 * cin), wts[...])
-    pre = merged(prod, (rows, width, cout))
-    pre_out[0] = pre
+    pre = paired_rows(padded, wts, cout)
+    pre_out[step] = pre
     mid = pre[1 : rows - 1].reshape(inner, cout)
     mean = jnp.sum(mid, axis=0, keepdims=True) / inner
     shift = jnp.where(step == 0, mean, sums[2:3])
@@ -139,43 +167,38 @@
     return jnp.where(even, across, ahead), jnp.where(even, ahead, across)
 
 
-def slice_kernel(first, final, ahead, across):
-    across[...], ahead[...] = sides(final[...], first[...])
-
-
-def edge_kernel(
-    total,
-    stage,
-    ahead,
-    across,
-    pre_top,
-    pre_bot,
-    ups_top,
-    ups_bot,
-    kern,
-    acc,
-    sums,
-    low,
-    high,
-    keep,
-    send,
-    stats,
-):
+def slice_kernel(images, ahead, across, sems):
+    last = images.shape[1] - 1
+    even = is_even()
+    copies = [
+        pltpu.make_async_copy(images.at[:, pl.ds(row, 1)], target, sems.at[index])
+        for index, (row, target) in enumerate(
+            ((jnp.where(even, last, 0), ahead), (jnp.where(even, 0, last), across))
+        )
+    ]
+    for copy in copies:
+        copy.start()
+    for copy in copies:
+        copy.wait()
+
+
+def edge_kernel(total, stage, ahead, across, pre, ups, kern, acc, sums, low, high, keep, send, stats):
     count, _, width, cin = ahead.shape
     cout = kern.shape[3]
+    last = pre.shape[1] - 1
     top, bot = sides(ahead[...], across[...])
     pixels = count * width
     shape = (count, width, cout)
     edges = []
-    for a, source, part, out in ((0, top, pre_top, low), (2, bot, pre_bot, high)):
+    for a, source, row, out in ((0, top, 0, low), (2, bot, last, high)):
         taps = jnp.concatenate([kern[a, c] for c in range(3)], axis=1)
-        value = merged(dot(source.reshape(pixels, cin), taps), shape) + part[:, 0]
+        value = merged(dot(source.reshape(pixels, cin), taps), shape) + pre[:, row]
         out[:, 0] = value
         edges.append(value.reshape(pixels, cout))
     shift = sums[2:3]
     delta = jnp.concatenate(edges, axis=0) - shift
     up = jnp.concatenate(
-        [ups_top[...].reshape(pixels, cout), ups_bot[...].reshape(pixels, cout)], axis=0
+        [ups[:, 0].reshape(pixels, cout), ups[:, last].reshape(pixels, cout)], axis=0
     )
     big, small = split(delta)
     gram = acc[...] + statistics(jnp.concatenate([small, big, up], axis=1))
@@ -267,99 +290,129 @@
     return average, mixed, symmetric / total_pix, bias, offset, color_sum
 
 
-def backward_kernel(
+def moment_kernel(image, pre, low, high, ups, img, ahead, across, sums, *rest):
+    acc, maps = rest[-2:]
+    rows, width, cin = img.shape[1:]
+    cout = pre.shape[3]
+    pixels = rows * width
+    top, bot = sides(ahead[image], across[image])
+    padded = jnp.concatenate([top, img[image], bot], axis=0)
+    turned = padded.reshape((rows + 2) * width, cin).T
+    full = jnp.concatenate([low[image], pre[image, 1 : rows - 1], high[image]], axis=0)
+    columns = []
+    for value in (ups[image], (full - sums[2:3]).astype(BF16)):
+        after, before = shifted(value.astype(F32))
+        columns += [after.astype(BF16), value, before.astype(BF16)]
+    right = jnp.concatenate(columns, axis=2).reshape(pixels, 6 * cout)
+    left = jnp.concatenate([turned[:, a * width : a * width + pixels] for a in range(3)], axis=0)
+    product = dot(left, right)
+    tiles = [turned[:, row * width : (row + 1) * width].astype(F32) for row in range(rows + 2)]
+    middle = functools.reduce(jnp.add, tiles[2:rows])
+    outer = ((0, 1), (1, rows), (rows, rows + 1))
+    totals = jnp.concatenate([middle + tiles[one] + tiles[two] for one, two in outer], axis=0)
+    if len(rest) == 4:
+        product = rest[0][...] + product
+        totals = rest[1][...] + totals
+    acc[...] = product
+    maps[...] = totals
+
+
+def whitening_kernel(
     total_pix,
     stage,
     own,
     other,
     colors,
     offset,
-    pre,
-    low,
-    high,
-    ups,
-    img,
-    ahead,
-    across,
-    colored,
-    pre_grad,
-    edge_ahead,
-    edge_across,
+    sums,
+    acc,
+    maps,
     keep,
     send,
     grad_colors,
+    mats,
+    paint,
+    paint_rows,
     stats,
-    mats,
-    rowsbuf,
-    acc,
-    turned,
 ):
-    step = pl.program_id(0)
-    last = pl.num_programs(0) - 1
-    rows, width, cin = img.shape[1:]
-    cout = pre.shape[3]
+    cout = 2 * colors.shape[1]
     half = cout // 2
-    pixels = rows * width
+    cin = acc.shape[0] // 3
     scaling = 1.0 / math.sqrt(total_pix)
-
-    @pl.when(step == 0)
-    def _():
-        join_kernel(stage, own, other, stats)
-        average, mixed, symmetric, bias, offs, color_sum = whitening(
-            stats[...], spread(colors[...]), offset[...], total_pix, half
-        )
-        zero = jnp.zeros((cout, cout), BF16)
-        mixed_h, mixed_l = split(mixed)
-        color_h, color_l = split(mixed.T)
-        sym_h, sym_l = split(symmetric)
-        for index, (one, two) in enumerate(
-            ((sym_h, color_h), (sym_h, color_h), (sym_l, color_l), (mixed_h, zero), (mixed_l, zero))
-        ):
-            mats[index * cout : (index + 1) * cout, :cout] = one
-            mats[index * cout : (index + 1) * cout, cout:] = two
-        rowsbuf[0:1, :cout] = average
-        rowsbuf[1:2, :cout] = bias
-        rowsbuf[1:2, cout:] = offs
-        scaled = color_sum * scaling
-        grad_colors[0] = scaled[:half, :half]
-        grad_colors[1] = pltpu.roll(scaled[half:], half, 1)[:, :half]
-        acc[...] = jnp.zeros_like(acc)
-        turned[...] = jnp.zeros_like(turned)
-
-    top, bot = sides(ahead[0], across[0])
-    padded = jnp.concatenate([top, img[0], bot], axis=0)
+    join_kernel(stage, own, other, stats)
+    average, mixed, symmetric, bias, offs, color_sum = whitening(
+        stats[...], spread(colors[...]), offset[...], total_pix, half
+    )
+    blank = jnp.zeros((cout, cout), BF16)
+    mixed_h, mixed_l = split(mixed)
+    color_h, color_l = split(mixed.T)
+    sym_h, sym_l = split(symmetric)
+    for target, blocks in (
+        (mats, ((sym_h, sym_l), (mixed_h, mixed_l), (sym_h, blank))),
+        (paint, ((color_h, color_l), (color_h, blank))),
+    ):
+        for index, (one, two) in enumerate(blocks):
+            target[index * cout : (index + 1) * cout, :cout] = one
+            target[index * cout : (index + 1) * cout, cout:] = two
+    paint_rows[...] = jnp.zeros_like(paint_rows)
+    paint_rows[0:1] = average
+    paint_rows[1:2] = offs
+    paint_rows[2:3] = bias
+    scaled = color_sum * scaling
+    grad_colors[0] = scaled[:half, :half]
+    grad_colors[1] = pltpu.roll(scaled[half:], half, 1)[:, :half]
+
+    moved = jnp.broadcast_to(sums[2:3] - average, (8, cout))
+    constant = (bias + dot3(moved, symmetric)[0:1]) * scaling
+    tall_h = jnp.concatenate([mixed_h, sym_h], axis=0)
+    tall_l = jnp.concatenate([mixed_l, sym_l], axis=0)
+    right = jnp.concatenate(
+        [
+            jnp.concatenate([tall_h, tall_l], axis=1),
+            jnp.concatenate([tall_h, jnp.zeros_like(tall_l)], axis=1),
+        ],
+        axis=0,
+    )
+    lane = lax.broadcasted_iota(jnp.int32, (cin, maps.shape[1]), 1)
+    seen = (lane < maps.shape[1] - 1, lane >= 0, lane > 0)
+    parts = []
     for a in range(3):
-        acc[a] += dot(turned[...], padded[a : a + rows].reshape(pixels, cin))
-    full = jnp.concatenate([low[0], pre[0, 1 : rows - 1], high[0]], axis=0)
-    centred = full.reshape(pixels, cout) - rowsbuf[0:1, :cout]
-    big, small = split(centred)
-    up = ups[0].reshape(pixels, cout)
-    result = dot(jnp.concatenate([big, small, big, up, up], axis=1), mats[...]) + rowsbuf[1:2]
-    colored[0] = result[:, cout:].astype(BF16).reshape(rows, width, cout)
-    grad = result[:, :cout].astype(BF16)
+        place = slice(a * cin, (a + 1) * cin)
+        for c in range(3):
+            pair = [acc[place, (k + c) * cout : (k + c + 1) * cout] for k in (0, 3)]
+            left = jnp.concatenate(split(jnp.concatenate(pair, axis=1)), axis=1)
+            result = dot(left, right)
+            total = jnp.sum(jnp.where(seen[c], maps[place], 0.0), axis=1, keepdims=True)
+            result = (result[:, :cout] + result[:, cout:]) * scaling + total * constant
+            parts += [result[: cin // 2], result[cin // 2 :]]
+    upper = is_upper(stage)
+    for index in range(9):
+        place = slice(index * cin // 2, (index + 1) * cin // 2)
+        keep[place] = jnp.where(upper, parts[9 + index], parts[index])
+        send[place] = jnp.where(upper, parts[index], parts[9 + index])
+
+
+def centred_halves(image, pre, low, high, average):
+    rows, width, cout = pre.shape[1:]
+    full = jnp.concatenate([low[image], pre[image, 1 : rows - 1], high[image]], axis=0)
+    return split(full.reshape(rows * width, cout) - average)
+
+
+def pixel_kernel(
+    pre, low, high, ups, mats, paint, paint_rows, colored, pre_grad, edge_ahead, edge_across
+):
+    image = pl.program_id(0)
+    rows, width, cout = pre.shape[1:]
+    big, small = centred_halves(image, pre, low, high, paint_rows[0:1])
+    up = ups[image].reshape(rows * width, cout)
+    result = dot(jnp.concatenate([big, up, small], axis=1), mats[...])
+    grad = (result[:, :cout] + result[:, cout:] + paint_rows[2:3]).astype(BF16)
     shaped = grad.reshape(rows, width, cout)
-    pre_grad[0] = shaped
-    edge_across[0], edge_ahead[0] = sides(shaped[rows - 1 :], shaped[:1])
-    after, before = shifted(shaped.astype(F32))
-    after = after.astype(BF16).reshape(pixels, cout)
-    before = before.astype(BF16).reshape(pixels, cout)
-    turned[:cout] = after.T
-    turned[cout : 2 * cout] = grad.T
-    turned[2 * cout :] = before.T
-
-    @pl.when(step == last)
-    def _():
-        upper = is_upper(stage)
-        parts = [
-            acc[tap // 3, tap % 3 * cout : (tap % 3 + 1) * cout, piece * cin // 2 : (piece + 1) * cin // 2].T
-            * scaling
-            for tap in range(9)
-            for piece in range(2)
-        ]
-        for index in range(9):
-            place = slice(index * cin // 2, (index + 1) * cin // 2)
-            keep[place] = jnp.where(upper, parts[9 + index], parts[index])
-            send[place] = jnp.where(upper, parts[index], parts[9 + index])
+    pre_grad[image] = shaped
+    edge_across[image], edge_ahead[image] = sides(shaped[rows - 1 :], shaped[:1])
+    result = dot(jnp.concatenate([big, small], axis=1), paint[...])
+    result = result[:, :cout] + result[:, cout:] + paint_rows[1:2]
+    colored[0] = result.astype(BF16).reshape(rows, width, cout)
 
 
 def turn_kernel(kern, out):
@@ -370,12 +423,13 @@
             out[tap : tap + cout] = kern[a, c].T
 
 
-def image_kernel(pre_grad, ahead, across, wts, *rest):
+def image_kernel(first, pre_grad, ahead, across, wts, *rest):
     out = rest[-1]
-    top, bot = sides(ahead[0], across[0])
+    image = pl.program_id(0) + first
+    top, bot = sides(ahead[image], across[image])
     rows, width, cout = pre_grad.shape[1:]
     cin = wts.shape[1]
-    exact = jnp.concatenate([top, pre_grad[0], bot], axis=0).astype(F32)
+    exact = jnp.concatenate([top, pre_grad[image], bot], axis=0).astype(F32)
     after, before = shifted(exact)
     taps = [value.astype(BF16) for value in (after, exact, before)]
     wide = jnp.concatenate(
@@ -401,13 +455,19 @@
     out[part:] = jnp.where(upper, value[...], received[...])
 
 
-def finish_kernel(stage, value, received, out):
-    size = out.shape[0]
-    steps = value.shape[0] // size
-    step = pl.program_id(0)
-    place = pl.ds(pl.multiple_of(step % steps * size, size), size)
-    own = is_upper(stage) == (step >= steps)
-    out[...] = jnp.where(own, value[place], received[place]).astype(F32)
+def finish_kernel(stage, own, value, *rest):
+    out, held, sems = rest[-3:]
+    count, size = held.shape[:2]
+    upper = is_upper(stage) if own else jnp.logical_not(is_upper(stage))
+    start = jnp.where(upper, count * size, 0)
+    copies = []
+    for index in range(count):
+        held[index] = value[index * size : (index + 1) * size].astype(F32)
+        place = pl.ds(pl.multiple_of(start + index * size, size), size)
+        copies.append(pltpu.make_async_copy(held.at[index], out.at[place], sems.at[index]))
+        copies[-1].start()
+    for copy in copies:
+        copy.wait()
 
 
 def image_spec(shape, place=lambda b: b):
@@ -424,10 +484,6 @@
 
 def resident():
     return pl.BlockSpec(memory_space=pltpu.VMEM)
-
-
-def row_spec(shape, row):
-    return pl.BlockSpec((shape[0], 1, *shape[2:]), lambda b: (0, row, 0, 0))
 
 
 def forward(images, kernel, upstream):
@@ -443,7 +499,7 @@
             image_spec(upstream.shape),
         ],
         out_specs=[
-            image_spec(pre_shape),
+            resident(),
             whole_spec((2 * cout, 2 * cout)),
             whole_spec((8, cout)),
         ],
@@ -453,7 +509,7 @@
             jax.ShapeDtypeStruct((8, cout), F32),
         ],
         scratch_shapes=[
-            pltpu.VMEM((3 * cin, 3 * cout), BF16),
+            pltpu.VMEM((10 * cin, 2 * cout), BF16),
             pltpu.VMEM(((rows - 2) * width, 3 * cout), BF16),
         ],
         compiler_params=pltpu.CompilerParams(vmem_limit_bytes=20 * MIB),
@@ -470,25 +526,13 @@
 
 def edges(stage, top, bot, pre, upstream, kernel, acc, sums):
     count, rows, width, cout = pre.shape
+    part = (cout + 16) // 2
     edge = (count, 1, width, cout)
-
-    part = (cout + 16) // 2
     shapes = [edge, edge, (part, cout), (part, cout)]
     return pl.pallas_call(
         functools.partial(edge_kernel, count * rows * width, stage),
-        grid=(1,),
-        in_specs=[
-            resident(),
-            resident(),
-            row_spec(pre.shape, 0),
-            row_spec(pre.shape, rows - 1),
-            row_spec(upstream.shape, 0),
-            row_spec(upstream.shape, rows - 1),
-            resident(),
-            resident(),
-            resident(),
-        ],
-        out_specs=[whole_spec(edge), whole_spec(edge), resident(), resident()],
+        in_specs=[resident()] * 7,
+        out_specs=[resident()] * 4,
         out_shape=[jax.ShapeDtypeStruct(shape, F32) for shape in shapes],
         scratch_shapes=[pltpu.VMEM((2 * part, cout), F32)],
         compiler_params=pltpu.CompilerParams(vmem_limit_bytes=12 * MIB),
@@ -498,64 +542,74 @@
             transcendentals=0,
         ),
         name="forward_edges",
-    )(top, bot, pre, pre, upstream, upstream, kernel, acc, sums)
-
-
-def backward(total_pix, stage, own, other, colors, offset, pre, low, high, upstream, images, top, bot):
-    count, rows, width, cin = images.shape
+    )(top, bot, pre, upstream, kernel, acc, sums)
+
+
+def moments(image, pre, low, high, upstream, images, top, bot, sums, *sofar):
+    width, cin = images.shape[2:]
     cout = upstream.shape[3]
-    half = cout // 2
-    edge = (count, 1, width, cout)
-
-    def here(b):
-        return jnp.minimum(b, count - 1)
-
-    def behind(b):
-        return jnp.maximum(b - 1, 0)
-
-    out_shapes = [
-        (upstream.shape, BF16),
-        (upstream.shape, BF16),
-        (edge, BF16),
-        (edge, BF16),
+    rows = images.shape[1]
+    operands = (pre, low, high, upstream, images, top, bot, sums, *sofar)
+    return pl.pallas_call(
+        functools.partial(moment_kernel, image),
+        in_specs=[resident()] * len(operands),
+        out_specs=[resident()] * 2,
+        out_shape=[
+            jax.ShapeDtypeStruct((3 * cin, 6 * cout), F32),
+            jax.ShapeDtypeStruct((3 * cin, width), F32),
+        ],
+        input_output_aliases={8: 0, 9: 1} if sofar else {},
+        compiler_params=pltpu.CompilerParams(vmem_limit_bytes=20 * MIB),
+        cost_estimate=pl.CostEstimate(
+            flops=2 * rows * width * 18 * cin * cout, bytes_accessed=8 * MIB, transcendentals=0
+        ),
+        name="moments",
+    )(*operands)
+
+
+def whitened(total_pix, stage, own, other, colors, offset, sums, acc, maps):
+    half = colors.shape[1]
+    cout = 2 * half
+    cin = acc.shape[0] // 3
+    shapes = [
         ((9 * cin // 2, cout), F32),
         ((9 * cin // 2, cout), F32),
         ((2, half, half), F32),
+        ((3 * cout, 2 * cout), BF16),
+        ((2 * cout, 2 * cout), BF16),
+        ((8, cout), F32),
     ]
     return pl.pallas_call(
-        functools.partial(backward_kernel, total_pix, stage),
-        grid=(count + 1,),
-        in_specs=[
-            resident(),
-            resident(),
-            resident(),
-            resident(),
-            image_spec(pre.shape, here),
-            image_spec(low.shape, here),
-            image_spec(high.shape, here),
-            image_spec(upstream.shape, here),
-            image_spec(images.shape, behind),
-            image_spec(top.shape, behind),
-            image_spec(bot.shape, behind),
-        ],
-        out_specs=[image_spec(shape, here) for shape, _ in out_shapes[:4]]
-        + [resident(), resident(), resident()],
-        out_shape=[jax.ShapeDtypeStruct(shape, dtype) for shape, dtype in out_shapes],
-        scratch_shapes=[
-            pltpu.VMEM((cout + 16, cout), F32),
-            pltpu.VMEM((5 * cout, 2 * cout), BF16),
-            pltpu.VMEM((8, 2 * cout), F32),
-            pltpu.VMEM((3, 3 * cout, cin), F32),
-            pltpu.VMEM((3 * cout, rows * width), BF16),
-        ],
+        functools.partial(whitening_kernel, total_pix, stage),
+        in_specs=[resident()] * 7,
+        out_specs=[resident()] * len(shapes),
+        out_shape=[jax.ShapeDtypeStruct(shape, dtype) for shape, dtype in shapes],
+        scratch_shapes=[pltpu.VMEM((cout + 16, cout), F32)],
         compiler_params=pltpu.CompilerParams(vmem_limit_bytes=20 * MIB),
         cost_estimate=pl.CostEstimate(
-            flops=2 * count * rows * width * 11 * cin * cout,
-            bytes_accessed=2 * images.size + 10 * upstream.size,
+            flops=2 * 9 * cin * 8 * cout * cout, bytes_accessed=8 * MIB, transcendentals=0
+        ),
+        name="whitening",
+    )(own, other, colors, offset, sums, acc, maps)
+
+
+def pixels(pre, low, high, upstream, mats, paint, paint_rows):
+    count, rows, width, cout = pre.shape
+    shapes = [pre.shape, pre.shape, (count, 1, width, cout), (count, 1, width, cout)]
+    return pl.pallas_call(
+        pixel_kernel,
+        grid=(count,),
+        in_specs=[resident()] * 7,
+        out_specs=[image_spec(pre.shape)] + [resident()] * 3,
+        out_shape=[jax.ShapeDtypeStruct(shape, BF16) for shape in shapes],
+        compiler_params=pltpu.CompilerParams(vmem_limit_bytes=16 * MIB),
+        cost_estimate=pl.CostEstimate(
+            flops=2 * count * rows * width * 12 * cout * cout,
+            bytes_accessed=10 * pre.size,
             transcendentals=0,
         ),
-        name="whitening_backward",
-    )(own, other, colors, offset, pre, low, high, upstream, images, top, bot)
+        name="pixels",
+    )(pre, low, high, upstream, mats, paint, paint_rows)
 
 
 def turned_weights(kernel):
@@ -577,15 +631,14 @@
         return b + first
 
     operands = [pre_grad, top, bot, turned]
-    in_specs = [image_spec(part.shape, place) for part in operands[:3]]
-    in_specs.append(whole_spec(turned.shape))
+    in_specs = [resident()] * 4
     aliases = {}
     if out is not None:
         operands.append(out)
         in_specs.append(pl.BlockSpec(memory_space=pl.ANY))
         aliases = {4: 0}
     return pl.pallas_call(
-        image_kernel,
+        functools.partial(image_kernel, first),
         grid=(count,),
         in_specs=in_specs,
         out_specs=image_spec(shape, place),
@@ -603,17 +656,15 @@
 
 def sliced(images):
     count, rows, width, cin = images.shape
-    shape = (count, 1, width, cin)
-    source = in_hbm(images)
     return pl.pallas_call(
         slice_kernel,
-        grid=(1,),
-        in_specs=[row_spec(images.shape, 0), row_spec(images.shape, rows - 1)],
+        in_specs=[pl.BlockSpec(memory_space=pltpu.HBM)],
         out_specs=[resident(), resident()],
-        out_shape=[jax.ShapeDtypeStruct(shape, BF16)] * 2,
-        compiler_params=pltpu.CompilerParams(vmem_limit_bytes=8 * MIB),
+        out_shape=[jax.ShapeDtypeStruct((count, 1, width, cin), BF16)] * 2,
+        scratch_shapes=[pltpu.SemaphoreType.DMA((2,))],
+        compiler_params=pltpu.CompilerParams(vmem_limit_bytes=4 * MIB),
         name="edge_rows",
-    )(source, source)
+    )(in_hbm(images))
 
 
 def small_call(kernel, name, *operands, out):
@@ -641,18 +692,25 @@
     )[0]
 
 
-def finish(value, received, stage):
+def finish(stage, value, out=None):
     part, lanes = value.shape
-    size = part // 2
-    return pl.pallas_call(
-        functools.partial(finish_kernel, stage),
-        grid=(4,),
-        in_specs=[resident(), resident()],
-        out_specs=pl.BlockSpec((size, lanes), lambda b: (b, 0)),
+    operands, aliases = (value,), {}
+    if out is not None:
+        operands, aliases = (value, out), {1: 0}
+    space = pl.BlockSpec(memory_space=pltpu.HBM)
+    return pl.pallas_call(
+        functools.partial(finish_kernel, stage, out is None),
+        in_specs=[resident(), space][: len(operands)],
+        out_specs=space,
         out_shape=jax.ShapeDtypeStruct((2 * part, lanes), F32),
-        compiler_params=pltpu.CompilerParams(vmem_limit_bytes=8 * MIB),
+        scratch_shapes=[
+            pltpu.VMEM((2, part // 2, lanes), F32),
+            pltpu.SemaphoreType.DMA((2,)),
+        ],
+        input_output_aliases=aliases,
+        compiler_params=pltpu.CompilerParams(vmem_limit_bytes=4 * MIB),
         name="finish",
-    )(value, received)
+    )(*operands)
 
 
 def halos(ahead, across):
@@ -685,29 +743,40 @@
     top, bot = halos(*sliced(images))
     pre, acc, sums = forward(images, kernel, upstream)
     low, high, value, send = edges(plan[0], top, bot, pre, upstream, kernel, acc, sums)
-    value = value + exchange(send, devices, plan[0])
-    for stage in plan[1:-1]:
-        value = value + exchange(value, devices, stage)
-    received, turned = beside(value, devices, plan[-1], turned_weights, (kernel,))
-    value = value + received
-    received = exchange(value, devices, plan[0])
-    colored, pre_grad, edge_ahead, edge_across, value, send, grad_colors = backward(
+    state = {"next": 0, "moments": (), "grad": None}
+
+    def summed(send, stage):
+        image = state["next"]
+        if image >= count:
+            return exchange(send, devices, stage)
+        state["next"] = image + 1
+        operands = (pre, low, high, upstream, images, top, bot, sums, *state["moments"])
+        received, state["moments"] = beside(
+            send, devices, stage, functools.partial(moments, image), operands
+        )
+        return received
+
+    value = value + summed(send, plan[0])
+    for stage in plan[1:]:
+        value = value + summed(value, stage)
+    received = summed(value, plan[0])
+    for image in range(state["next"], count):
+        state["moments"] = moments(
+            image, pre, low, high, upstream, images, top, bot, sums, *state["moments"]
+        )
+    value, send, grad_colors, mats, paint, paint_rows = whitened(
         total_pix,
         plan[0],
         value,
         received,
         colors,
         offset.reshape(1, cout),
-        pre,
-        low,
-        high,
-        upstream,
-        images,
-        top,
-        bot,
-    )
-    shares = [1, 1, 2, 1, 1]
-    state = {"next": 0, "grad": None}
+        sums,
+        *state["moments"],
+    )
+    received, turned = beside(send, devices, plan[0], turned_weights, (kernel,))
+    state["next"] = 0
+    shares = [1, 2, 1, 1, 1]
 
     def transfer(send, stage):
         first = state["next"]
@@ -724,7 +793,6 @@
         return received
 
     cuts = []
-    received = exchange(send, devices, plan[0])
     for stage in plan[1:]:
         if value.shape[0] % 32 == 0 and value.shape[0] > 144:
             value, send = fold(value, received, stage)
@@ -732,6 +800,10 @@
         else:
             value = send = value + received
         if stage == plan[1]:
+            received, (colored, pre_grad, edge_ahead, edge_across) = beside(
+                send, devices, stage, pixels, (pre, low, high, upstream, mats, paint, paint_rows)
+            )
+        elif stage == plan[2]:
             received, (grad_top, grad_bot) = beside(
                 send, devices, stage, halos, (edge_ahead, edge_across)
             )
@@ -740,8 +812,15 @@
     value = (value + received).astype(BF16)
     for stage in reversed(cuts):
         value = join(value, transfer(value, stage), stage)
-    grad_kernel = finish(value, exchange(value, devices, plan[0]), plan[0])
-    return colored, state["grad"], grad_kernel.reshape(3, 3, cin, cout), grad_colors
+    received, result = beside(
+        value, devices, plan[0], functools.partial(finish, plan[0]), (value,)
+    )
+    first = state["next"]
+    if first < count:
+        operands = (pre_grad, grad_top, grad_bot, turned, state["grad"])
+        state["grad"] = image_gradient(first, count - first, *operands)
+    grad_kernel = finish(plan[0], received, result).reshape(3, 3, cin, cout)
+    return colored, state["grad"], grad_kernel, grad_colors
 
 
 def solution(mesh):

time: 94.1 us -> 86.1 us (0.915)
  waiting for transfers between devices: 33.4 us -> 15.2 us
  starting transfers between devices: 23 us -> 29.6 us
  Pallas kernels: 36.7 us -> 39.9 us
    ppermute x15, waiting for transfers between devices: 33 us -> 15.2 us  [exchange(): return lax.ppermute(value, AXES, pairs)]
    ppermute x15, starting transfers between devices: 20.1 us -> 27.6 us  [exchange(): return lax.ppermute(value, AXES, pairs)]
    pallas_call x8 -> x16, Pallas kernels: 25.3 us -> 29.1 us  [the longest x6 9.51 us: moments(): pl.pallas_call(functools.partial(moment_kernel, image), in_specs=[residen...]
  transfers between devices with their start and end apart: 19 -> 19, of which waited for: 16 -> 13; matrix products, arithmetic and copies ran while one was open for 0% -> 0% of each run, Pallas kernels for 20% -> 39%
where the time goes in v2:
time: 86.1 us; the launch traced here: 85.9 us
  Pallas kernels  39.9 us (46%)
  starting transfers between devices  29.6 us (34%)
  waiting for transfers between devices  15.2 us (18%)
  between operations  1.06 us (1%)
    ppermute x15, starting transfers between devices, exchange(): return lax.ppermute(value, AXES, pairs)  27.6 us
    ppermute x15, waiting for transfers between devices, exchange(): return lax.ppermute(value, AXES, pairs)  15.2 us
    pallas_call x6, Pallas kernels, moments(): pl.pallas_call(functools.partial(moment_kernel, image), in_specs=[residen...  9.51 us
    pallas_call x1, Pallas kernels, forward(): pl.pallas_call(forward_kernel, grid=(count,), in_specs=[image_spec(images...  9.27 us
    pallas_call x5, Pallas kernels, image_gradient(): pl.pallas_call(functools.partial(image_kernel, first), grid=(count,), in_...  9.11 us
    pallas_call x1, Pallas kernels, pixels(): pl.pallas_call(pixel_kernel, grid=(count,), in_specs=[resident()] * 7, ou...  4.37 us
    pallas_call x1, Pallas kernels, whitened(): pl.pallas_call(functools.partial(whitening_kernel, total_pix, stage), in_...  3.24 us
  transfers between devices with their start and end apart: 19, of which 13 were waited for; matrix products, arithmetic and copies ran while one was open for 0% of the time, Pallas kernels for 39%

profile of v2, /device:TPU:0, one launch (start us, length us, event | category | flops | bytes accessed | tf_op | source)
XLA Modules:
  0.0 85.9 jit_solution(15428151935551413277)
XLA Ops:
  3.1 9.3 %forward_inner.1 = (f32[6,8,128,128]{3,2,1,0:T(8,128)S(1)}, f32[256,256]{1,0:T(8,128)S(1)}, f32[8,128]{1,0:T(8,128)S(1)}) custom-call(bf16[6,8,128,256]{3,2,1,0:T(8,128)(2,1)} %img.7, bf16[3,3,256,128]{3,2,1,0:T(8,128)(2,1)} %kern.4, bf16[6,8,128,128]{3,2,1,0:T(8,128)(2,1)} %ups.10), custom_call_target="tpu_custom_call" | custom-call | flops 3623878656 | bytes 7864320 | tf_op jit(solution)/shard_map/forward_inner/pallas_call | solution.py:493
  13.5 3.9 %collective-permute-start.2 = (f32[72,128]{1,0:T(8,128)S(1)}, f32[72,128]{1,0:T(8,128)S(1)}, u32[]{:S(2)}, u32[]{:S(2)}) collective-permute-start(f32[72,128]{1,0:T(8,128)S(1)} %get-tuple-element.198), channel_id=1, source_target_pairs={{0,1},{1,0},{2,3},{3,2},{4,5},{5,4},{6,7},{7,6},{8,9},{9,8},{10,11... | collective-permute-start | bytes 110600 | tf_op jit(solution)/shard_map/ppermute | solution.py:727
  19.6 1.6 %moments.7 = (f32[768,768]{1,0:T(8,128)S(1)}, f32[768,128]{1,0:T(8,128)S(1)}) custom-call(f32[6,8,128,128]{3,2,1,0:T(8,128)S(1)} %get-tuple-element.302.pre, f32[6,1,128,128]{3,2,1,0:T(8,128)S(1)} %get-tuple-element.303.low, f32[6,1,128,128]{3,2,1,0:T(8,128)S(1)} %get-tuple-element.304.high, ...), custom_call_target="tpu_custom_call", output_to_operand_aliasing={{0}: (8, {}), {1}: (9, {})} | custom-call | flops 1207959552 | bytes 8388608 | tf_op jit(solution)/shard_map/moments/pallas_call | solution.py:553
  21.2 1.7 %collective-permute-done.3 = f32[72,128]{1,0:T(8,128)S(1)} collective-permute-done((f32[72,128]{1,0:T(8,128)S(1)}, f32[72,128]{1,0:T(8,128)S(1)}, u32[]{:S(2)}, u32[]{:S(2)}) %collective-permute-start.3) | collective-permute-done | bytes 36896 | tf_op jit(solution)/shard_map/ppermute | solution.py:727
  24.4 1.6 %moments.8 = (f32[768,768]{1,0:T(8,128)S(1)}, f32[768,128]{1,0:T(8,128)S(1)}) custom-call(f32[6,8,128,128]{3,2,1,0:T(8,128)S(1)} %get-tuple-element.302.pre, f32[6,1,128,128]{3,2,1,0:T(8,128)S(1)} %get-tuple-element.303.low, f32[6,1,128,128]{3,2,1,0:T(8,128)S(1)} %get-tuple-element.304.high, ...), custom_call_target="tpu_custom_call", output_to_operand_aliasing={{0}: (8, {}), {1}: (9, {})} | custom-call | flops 1207959552 | bytes 8388608 | tf_op jit(solution)/shard_map/moments/pallas_call | solution.py:553
  26.9 1.6 %collective-permute-start.5 = (f32[72,128]{1,0:T(8,128)S(1)}, f32[72,128]{1,0:T(8,128)S(1)}, u32[]{:S(2)}, u32[]{:S(2)}) collective-permute-start(f32[72,128]{1,0:T(8,128)S(1)} %add.23), channel_id=1, source_target_pairs={{0,8},{1,9},{2,10},{3,11},{4,12},{5,13},{6,14},{7,15},{8,0},{9,1},... | collective-permute-start | bytes 110600 | tf_op jit(solution)/shard_map/ppermute | solution.py:727
  28.5 1.6 %moments.9 = (f32[768,768]{1,0:T(8,128)S(1)}, f32[768,128]{1,0:T(8,128)S(1)}) custom-call(f32[6,8,128,128]{3,2,1,0:T(8,128)S(1)} %get-tuple-element.302.pre, f32[6,1,128,128]{3,2,1,0:T(8,128)S(1)} %get-tuple-element.303.low, f32[6,1,128,128]{3,2,1,0:T(8,128)S(1)} %get-tuple-element.304.high, ...), custom_call_target="tpu_custom_call", output_to_operand_aliasing={{0}: (8, {}), {1}: (9, {})} | custom-call | flops 1207959552 | bytes 8388608 | tf_op jit(solution)/shard_map/moments/pallas_call | solution.py:553
  30.9 2.6 %collective-permute-start.6 = (f32[72,128]{1,0:T(8,128)S(1)}, f32[72,128]{1,0:T(8,128)S(1)}, u32[]{:S(2)}, u32[]{:S(2)}) collective-permute-start(f32[72,128]{1,0:T(8,128)S(1)} %add.24), channel_id=1, source_target_pairs={{0,16},{1,17},{2,18},{3,19},{4,20},{5,21},{6,22},{7,23},{8,24},{9,... | collective-permute-start | bytes 110600 | tf_op jit(solution)/shard_map/ppermute | solution.py:727
  33.5 1.6 %moments.10 = (f32[768,768]{1,0:T(8,128)S(1)}, f32[768,128]{1,0:T(8,128)S(1)}) custom-call(f32[6,8,128,128]{3,2,1,0:T(8,128)S(1)} %get-tuple-element.302.pre, f32[6,1,128,128]{3,2,1,0:T(8,128)S(1)} %get-tuple-element.303.low, f32[6,1,128,128]{3,2,1,0:T(8,128)S(1)} %get-tuple-element.304.high, ...), custom_call_target="tpu_custom_call", output_to_operand_aliasing={{0}: (8, {}), {1}: (9, {})} | custom-call | flops 1207959552 | bytes 8388608 | tf_op jit(solution)/shard_map/moments/pallas_call | solution.py:553
  35.8 1.6 %moments.11 = (f32[768,768]{1,0:T(8,128)S(1)}, f32[768,128]{1,0:T(8,128)S(1)}) custom-call(f32[6,8,128,128]{3,2,1,0:T(8,128)S(1)} %get-tuple-element.302.pre, f32[6,1,128,128]{3,2,1,0:T(8,128)S(1)} %get-tuple-element.303.low, f32[6,1,128,128]{3,2,1,0:T(8,128)S(1)} %get-tuple-element.304.high, ...), custom_call_target="tpu_custom_call", output_to_operand_aliasing={{0}: (8, {}), {1}: (9, {})} | custom-call | flops 1207959552 | bytes 8388608 | tf_op jit(solution)/shard_map/moments/pallas_call | solution.py:553
  37.5 3.2 %whitening.1 = (f32[1152,128]{1,0:T(8,128)S(1)}, f32[1152,128]{1,0:T(8,128)S(1)}, f32[2,64,64]{2,1,0:T(8,128)}, bf16[384,256]{1,0:T(8,128)(2,1)S(1)}, bf16[256,2...) custom-call(f32[72,128]{1,0:T(8,128)S(1)} %add.25.own, f32[72,128]{1,0:T(8,128)S(1)} %collective-permute-done.7.other, ...), custom_call_target="tpu_custom_call" | custom-call | flops 603979776 | bytes 8388608 | tf_op jit(solution)/shard_map/whitening/pallas_call | solution.py:582
  44.1 4.4 %pixels.1 = (bf16[6,8,128,128]{3,2,1,0:T(8,128)(2,1)}, bf16[6,8,128,128]{3,2,1,0:T(8,128)(2,1)S(1)}, bf16[6,1,128,128]{3,2,1,0:T(8,128)(2,1)S(1)}, bf16[6,1,128,128]{3,2,1,0:T(8,128)(2,1)S(1)}) custom-call(f32[6,8,128,128]{3,2,1,0:T(8,128)S(1)} %get-tuple-element.302.pre, f32[6,1,128,128]{3,2,1,0:T(8,128)S(1)} %get-tuple-element.303.low, ...), custom_call_target="tpu_custom_call" | custom-call | flops 2415919104 | bytes 7864320 | tf_op jit(solution)/shard_map/pixels/pallas_call | solution.py:599
  50.5 1.6 %collective-permute-start.10 = (f32[288,128]{1,0:T(8,128)S(1)}, f32[288,128]{1,0:T(8,128)S(1)}, u32[]{:S(2)}, u32[]{:S(2)}) collective-permute-start(f32[288,128]{1,0:T(8,128)S(1)} %get-tuple-element.320), channel_id=1, source_target_pairs={{0,4},{1,3},{2,6},{3,1},{4,0},{5,7},{6,2},{7,5},{8,12},{9,11},{10,... | collective-permute-start | bytes 442376 | tf_op jit(solution)/shard_map/ppermute | solution.py:727
  52.1 3.6 %collective-permute-done.10.received = f32[288,128]{1,0:T(8,128)S(1)} collective-permute-done((f32[288,128]{1,0:T(8,128)S(1)}, f32[288,128]{1,0:T(8,128)S(1)}, u32[]{:S(2)}, u32[]{:S(2)}) %collective-permute-start.10) | collective-permute-done | bytes 147488 | tf_op jit(solution)/shard_map/ppermute | solution.py:727
  55.7 1.7 %collective-permute-start.13 = (f32[144,128]{1,0:T(8,128)S(1)}, f32[144,128]{1,0:T(8,128)S(1)}, u32[]{:S(2)}, u32[]{:S(2)}) collective-permute-start(f32[144,128]{1,0:T(8,128)S(1)} %get-tuple-element.330), channel_id=1, source_target_pairs={{0,8},{1,9},{2,10},{3,11},{4,12},{5,13},{6,14},{7,15},{8,0},{9,1},... | collective-permute-start | bytes 221192 | tf_op jit(solution)/shard_map/ppermute | solution.py:727
  57.4 1.6 %image_gradient.5.rest_0_ = bf16[6,8,128,256]{3,2,1,0:T(8,128)(2,1)} custom-call(bf16[6,8,128,128]{3,2,1,0:T(8,128)(2,1)S(1)} %get-tuple-element.362.pre_grad, bf16[6,1,128,128]{3,2,1,0:T(8,128)(2,1)S(1)} %collective-permute-done.11.ahead, bf16[6,1,128,128]{3,2,1,0:T(8,128)(2,1)S(1)} %collective-permute-done.12.across, bf16[1152,256]{1,0:T(8,128)(2,1)S(1)} %turned_weights.1.wts), custom_call_target="tpu_custom_call" | custom-call | flops 603979776 | bytes 786432 | tf_op jit(solution)/shard_map/image_gradient/pallas_call | solution.py:640
  60.2 2.7 %collective-permute-start.14 = (f32[144,128]{1,0:T(8,128)S(1)}, f32[144,128]{1,0:T(8,128)S(1)}, u32[]{:S(2)}, u32[]{:S(2)}) collective-permute-start(f32[144,128]{1,0:T(8,128)S(1)} %add.26), channel_id=1, source_target_pairs={{0,16},{1,17},{2,18},{3,19},{4,20},{5,21},{6,22},{7,23},{8,24},{9,... | collective-permute-start | bytes 221192 | tf_op jit(solution)/shard_map/ppermute | solution.py:727
  62.9 2.5 %image_gradient.6.rest_0_ = bf16[6,8,128,256]{3,2,1,0:T(8,128)(2,1)} custom-call(bf16[6,8,128,128]{3,2,1,0:T(8,128)(2,1)S(1)} %get-tuple-element.362.pre_grad, bf16[6,1,128,128]{3,2,1,0:T(8,128)(2,1)S(1)} %collective-permute-done.11.ahead, bf16[6,1,128,128]{3,2,1,0:T(8,128)(2,1)S(1)} %collective-permute-done.12.across, ...), custom_call_target="tpu_custom_call", output_to_operand_aliasing={{}: (4, {})} | custom-call | flops 1207959552 | bytes 1572864 | tf_op jit(solution)/shard_map/image_gradient/pallas_call | solution.py:640
  65.5 2.8 %collective-permute-start.15 = (bf16[144,128]{1,0:T(8,128)(2,1)S(1)}, bf16[144,128]{1,0:T(8,128)(2,1)S(1)}, u32[]{:S(2)}, u32[]{:S(2)}) collective-permute-start(bf16[144,128]{1,0:T(8,128)(2,1)S(1)} %add_convert_fusion.value), channel_id=1, source_target_pairs={{0,8},{1,9},{2,10},{3,11},{4,12},{5,13},{6,14},{7,15},{8,0},{9,1},... | collective-permute-start | bytes 110600 | tf_op jit(solution)/shard_map/ppermute | solution.py:727
  68.3 1.6 %image_gradient.7.rest_0_ = bf16[6,8,128,256]{3,2,1,0:T(8,128)(2,1)} custom-call(bf16[6,8,128,128]{3,2,1,0:T(8,128)(2,1)S(1)} %get-tuple-element.362.pre_grad, bf16[6,1,128,128]{3,2,1,0:T(8,128)(2,1)S(1)} %collective-permute-done.11.ahead, bf16[6,1,128,128]{3,2,1,0:T(8,128)(2,1)S(1)} %collective-permute-done.12.across, ...), custom_call_target="tpu_custom_call", output_to_operand_aliasing={{}: (4, {})} | custom-call | flops 603979776 | bytes 786432 | tf_op jit(solution)/shard_map/image_gradient/pallas_call | solution.py:640
  70.3 1.5 %collective-permute-start.16 = (bf16[288,128]{1,0:T(8,128)(2,1)S(1)}, bf16[288,128]{1,0:T(8,128)(2,1)S(1)}, u32[]{:S(2)}, u32[]{:S(2)}) collective-permute-start(bf16[288,128]{1,0:T(8,128)(2,1)S(1)} %join.3.value), channel_id=1, source_target_pairs={{0,4},{1,3},{2,6},{3,1},{4,0},{5,7},{6,2},{7,5},{8,12},{9,11},{10,... | collective-permute-start | bytes 221192 | tf_op jit(solution)/shard_map/ppermute | solution.py:727
  71.8 1.6 %image_gradient.8.rest_0_ = bf16[6,8,128,256]{3,2,1,0:T(8,128)(2,1)} custom-call(bf16[6,8,128,128]{3,2,1,0:T(8,128)(2,1)S(1)} %get-tuple-element.362.pre_grad, bf16[6,1,128,128]{3,2,1,0:T(8,128)(2,1)S(1)} %collective-permute-done.11.ahead, bf16[6,1,128,128]{3,2,1,0:T(8,128)(2,1)S(1)} %collective-permute-done.12.across, ...), custom_call_target="tpu_custom_call", output_to_operand_aliasing={{}: (4, {})} | custom-call | flops 603979776 | bytes 786432 | tf_op jit(solution)/shard_map/image_gradient/pallas_call | solution.py:640
  74.7 5.3 %collective-permute-start.17 = (bf16[576,128]{1,0:T(8,128)(2,1)S(1)}, bf16[576,128]{1,0:T(8,128)(2,1)S(1)}, u32[]{:S(2)}, u32[]{:S(2)}) collective-permute-start(bf16[576,128]{1,0:T(8,128)(2,1)S(1)} %join.4.value), channel_id=1, source_target_pairs={{0,2},{1,5},{2,0},{3,7},{4,6},{5,1},{6,4},{7,3},{8,10},{9,13},{10,... | collective-permute-start | bytes 442376 | tf_op jit(solution)/shard_map/ppermute | solution.py:727
  80.0 1.6 %image_gradient.9 = bf16[6,8,128,256]{3,2,1,0:T(8,128)(2,1)} custom-call(bf16[6,8,128,128]{3,2,1,0:T(8,128)(2,1)S(1)} %get-tuple-element.362.pre_grad, bf16[6,1,128,128]{3,2,1,0:T(8,128)(2,1)S(1)} %collective-permute-done.11.ahead, bf16[6,1,128,128]{3,2,1,0:T(8,128)(2,1)S(1)} %collective-permute-done.12.across, ...), custom_call_target="tpu_custom_call", output_to_operand_aliasing={{}: (4, {})} | custom-call | flops 603979776 | bytes 786432 | tf_op jit(solution)/shard_map/image_gradient/pallas_call | solution.py:640
  (56 shorter events, 21.8 us)
Async XLA Ops:
  1.8 10.6 %collective-permute-start = (bf16[6,1,128,256]{3,2,1,0:T(8,128)(2,1)S(1)}, bf16[6,1,128,256]{3,2,1,0:T(8,128)(2,1)S(1)}, u32[]{:S(2)}, u32[]{:S(2)}) collective-permute-start(bf16[6,1,128,256]{3,2,1,0:T(8,128)(2,1)S(1)} %get-tuple-element.189), channel_id=1, source_target_pairs={{0,1},{2,3},{1,0},{3,2},{4,5},{6,7},{5,4},{7,6},{8,9},{10,11},{9,8... | collective-permute-start | bytes 1179656 | tf_op jit(solution)/shard_map/ppermute | solution.py:722
  2.3 10.1 %copy-start.1 = (bf16[6,8,128,128]{3,2,1,0:T(8,128)(2,1)S(1)}, bf16[6,8,128,128]{3,2,1,0:T(8,128)(2,1)}, u32[]{:S(2)}) copy-start(bf16[6,8,128,128]{3,2,1,0:T(8,128)(2,1)} %ups.10) | copy-start | bytes 4718596
  2.3 10.1 %copy-start.2 = (bf16[3,3,256,128]{3,2,1,0:T(8,128)(2,1)S(1)}, bf16[3,3,256,128]{3,2,1,0:T(8,128)(2,1)}, u32[]{:S(2)}) copy-start(bf16[3,3,256,128]{3,2,1,0:T(8,128)(2,1)} %kern.4) | copy-start | bytes 1769476
  2.3 10.1 %collective-permute-start.1 = (bf16[6,1,128,256]{3,2,1,0:T(8,128)(2,1)S(1)}, bf16[6,1,128,256]{3,2,1,0:T(8,128)(2,1)S(1)}, u32[]{:S(2)}, u32[]{:S(2)}) collective-permute-start(bf16[6,1,128,256]{3,2,1,0:T(8,128)(2,1)S(1)} %get-tuple-element.190), channel_id=1, source_target_pairs={{1,2},{2,1},{5,6},{6,5},{9,10},{10,9},{13,14},{14,13},{17,18},{18,... | collective-permute-start | bytes 1179656 | tf_op jit(solution)/shard_map/ppermute | solution.py:722
  12.4 5.0 %copy-start = (bf16[6,8,128,256]{3,2,1,0:T(8,128)(2,1)S(1)}, bf16[6,8,128,256]{3,2,1,0:T(8,128)(2,1)}, u32[]{:S(2)}) copy-start(bf16[6,8,128,256]{3,2,1,0:T(8,128)(2,1)} %img.7) | copy-start | bytes 9437188
  13.5 5.3 %collective-permute-start.2 = (f32[72,128]{1,0:T(8,128)S(1)}, f32[72,128]{1,0:T(8,128)S(1)}, u32[]{:S(2)}, u32[]{:S(2)}) collective-permute-start(f32[72,128]{1,0:T(8,128)S(1)} %get-tuple-element.198), channel_id=1, source_target_pairs={{0,1},{1,0},{2,3},{3,2},{4,5},{5,4},{6,7},{7,6},{8,9},{9,8},{10,11... | collective-permute-start | bytes 110600 | tf_op jit(solution)/shard_map/ppermute | solution.py:727
  18.9 4.0 %collective-permute-start.3 = (f32[72,128]{1,0:T(8,128)S(1)}, f32[72,128]{1,0:T(8,128)S(1)}, u32[]{:S(2)}, u32[]{:S(2)}) collective-permute-start(f32[72,128]{1,0:T(8,128)S(1)} %add.21), channel_id=1, source_target_pairs={{0,2},{1,5},{2,0},{3,7},{4,6},{5,1},{6,4},{7,3},{8,10},{9,13},{10,... | collective-permute-start | bytes 110600 | tf_op jit(solution)/shard_map/ppermute | solution.py:727
  22.9 4.0 %collective-permute-start.4 = (f32[72,128]{1,0:T(8,128)S(1)}, f32[72,128]{1,0:T(8,128)S(1)}, u32[]{:S(2)}, u32[]{:S(2)}) collective-permute-start(f32[72,128]{1,0:T(8,128)S(1)} %add.22), channel_id=1, source_target_pairs={{0,4},{1,3},{2,6},{3,1},{4,0},{5,7},{6,2},{7,5},{8,12},{9,11},{10,... | collective-permute-start | bytes 110600 | tf_op jit(solution)/shard_map/ppermute | solution.py:727
  26.9 4.0 %collective-permute-start.5 = (f32[72,128]{1,0:T(8,128)S(1)}, f32[72,128]{1,0:T(8,128)S(1)}, u32[]{:S(2)}, u32[]{:S(2)}) collective-permute-start(f32[72,128]{1,0:T(8,128)S(1)} %add.23), channel_id=1, source_target_pairs={{0,8},{1,9},{2,10},{3,11},{4,12},{5,13},{6,14},{7,15},{8,0},{9,1},... | collective-permute-start | bytes 110600 | tf_op jit(solution)/shard_map/ppermute | solution.py:727
  30.9 4.9 %collective-permute-start.6 = (f32[72,128]{1,0:T(8,128)S(1)}, f32[72,128]{1,0:T(8,128)S(1)}, u32[]{:S(2)}, u32[]{:S(2)}) collective-permute-start(f32[72,128]{1,0:T(8,128)S(1)} %add.24), channel_id=1, source_target_pairs={{0,16},{1,17},{2,18},{3,19},{4,20},{5,21},{6,22},{7,23},{8,24},{9,... | collective-permute-start | bytes 110600 | tf_op jit(solution)/shard_map/ppermute | solution.py:727
  35.7 1.7 %copy-start.3 = (f32[2,64,64]{2,1,0:T(8,128)S(1)}, f32[2,64,64]{2,1,0:T(8,128)}, u32[]{:S(2)}) copy-start(f32[2,64,64]{2,1,0:T(8,128)} %colors.1) | copy-start | bytes 98308
  35.7 1.7 %copy-start.4 = (f32[128]{0:T(128)S(1)}, f32[128]{0:T(128)}, u32[]{:S(2)}) copy-start(f32[128]{0:T(128)} %param.8) | copy-start | bytes 1540
  35.7 1.7 %collective-permute-start.7 = (f32[72,128]{1,0:T(8,128)S(1)}, f32[72,128]{1,0:T(8,128)S(1)}, u32[]{:S(2)}, u32[]{:S(2)}) collective-permute-start(f32[72,128]{1,0:T(8,128)S(1)} %add.25.own), channel_id=1, source_target_pairs={{0,1},{1,0},{2,3},{3,2},{4,5},{5,4},{6,7},{7,6},{8,9},{9,8},{10,11... | collective-permute-start | bytes 110600 | tf_op jit(solution)/shard_map/ppermute | solution.py:727
  40.7 2.1 %collective-permute-start.8 = (f32[1152,128]{1,0:T(8,128)S(1)}, f32[1152,128]{1,0:T(8,128)S(1)}, u32[]{:S(2)}, u32[]{:S(2)}) collective-permute-start(f32[1152,128]{1,0:T(8,128)S(1)} %get-tuple-element.294), channel_id=1, source_target_pairs={{0,1},{1,0},{2,3},{3,2},{4,5},{5,4},{6,7},{7,6},{8,9},{9,8},{10,11... | collective-permute-start | bytes 1769480 | tf_op jit(solution)/shard_map/ppermute | solution.py:727
  42.9 6.8 %collective-permute-start.9 = (f32[576,128]{1,0:T(8,128)S(1)}, f32[576,128]{1,0:T(8,128)S(1)}, u32[]{:S(2)}, u32[]{:S(2)}) collective-permute-start(f32[576,128]{1,0:T(8,128)S(1)} %get-tuple-element.301), channel_id=1, source_target_pairs={{0,2},{1,5},{2,0},{3,7},{4,6},{5,1},{6,4},{7,3},{8,10},{9,13},{10,... | collective-permute-start | bytes 884744 | tf_op jit(solution)/shard_map/ppermute | solution.py:727
  49.7 6.0 %collective-permute-start.11 = (bf16[6,1,128,128]{3,2,1,0:T(8,128)(2,1)S(1)}, bf16[6,1,128,128]{3,2,1,0:T(8,128)(2,1)S(1)}, u32[]{:S(2)}, u32[]{:S(2)}) collective-permute-start(bf16[6,1,128,128]{3,2,1,0:T(8,128)(2,1)S(1)} %get-tuple-element.321), channel_id=1, source_target_pairs={{0,1},{2,3},{1,0},{3,2},{4,5},{6,7},{5,4},{7,6},{8,9},{10,11},{9,8... | collective-permute-start | bytes 589832 | tf_op jit(solution)/shard_map/ppermute | solution.py:722
  49.8 5.9 %collective-permute-start.12 = (bf16[6,1,128,128]{3,2,1,0:T(8,128)(2,1)S(1)}, bf16[6,1,128,128]{3,2,1,0:T(8,128)(2,1)S(1)}, u32[]{:S(2)}, u32[]{:S(2)}) collective-permute-start(bf16[6,1,128,128]{3,2,1,0:T(8,128)(2,1)S(1)} %get-tuple-element.322), channel_id=1, source_target_pairs={{1,2},{2,1},{5,6},{6,5},{9,10},{10,9},{13,14},{14,13},{17,18},{18,... | collective-permute-start | bytes 589832 | tf_op jit(solution)/shard_map/ppermute | solution.py:722
  50.5 5.2 %collective-permute-start.10 = (f32[288,128]{1,0:T(8,128)S(1)}, f32[288,128]{1,0:T(8,128)S(1)}, u32[]{:S(2)}, u32[]{:S(2)}) collective-permute-start(f32[288,128]{1,0:T(8,128)S(1)} %get-tuple-element.320), channel_id=1, source_target_pairs={{0,4},{1,3},{2,6},{3,1},{4,0},{5,7},{6,2},{7,5},{8,12},{9,11},{10,... | collective-permute-start | bytes 442376 | tf_op jit(solution)/shard_map/ppermute | solution.py:727
  55.7 4.4 %collective-permute-start.13 = (f32[144,128]{1,0:T(8,128)S(1)}, f32[144,128]{1,0:T(8,128)S(1)}, u32[]{:S(2)}, u32[]{:S(2)}) collective-permute-start(f32[144,128]{1,0:T(8,128)S(1)} %get-tuple-element.330), channel_id=1, source_target_pairs={{0,8},{1,9},{2,10},{3,11},{4,12},{5,13},{6,14},{7,15},{8,0},{9,1},... | collective-permute-start | bytes 221192 | tf_op jit(solution)/shard_map/ppermute | solution.py:727
  60.2 5.3 %collective-permute-start.14 = (f32[144,128]{1,0:T(8,128)S(1)}, f32[144,128]{1,0:T(8,128)S(1)}, u32[]{:S(2)}, u32[]{:S(2)}) collective-permute-start(f32[144,128]{1,0:T(8,128)S(1)} %add.26), channel_id=1, source_target_pairs={{0,16},{1,17},{2,18},{3,19},{4,20},{5,21},{6,22},{7,23},{8,24},{9,... | collective-permute-start | bytes 221192 | tf_op jit(solution)/shard_map/ppermute | solution.py:727
  65.5 4.7 %collective-permute-start.15 = (bf16[144,128]{1,0:T(8,128)(2,1)S(1)}, bf16[144,128]{1,0:T(8,128)(2,1)S(1)}, u32[]{:S(2)}, u32[]{:S(2)}) collective-permute-start(bf16[144,128]{1,0:T(8,128)(2,1)S(1)} %add_convert_fusion.value), channel_id=1, source_target_pairs={{0,8},{1,9},{2,10},{3,11},{4,12},{5,13},{6,14},{7,15},{8,0},{9,1},... | collective-permute-start | bytes 110600 | tf_op jit(solution)/shard_map/ppermute | solution.py:727
  70.3 4.4 %collective-permute-start.16 = (bf16[288,128]{1,0:T(8,128)(2,1)S(1)}, bf16[288,128]{1,0:T(8,128)(2,1)S(1)}, u32[]{:S(2)}, u32[]{:S(2)}) collective-permute-start(bf16[288,128]{1,0:T(8,128)(2,1)S(1)} %join.3.value), channel_id=1, source_target_pairs={{0,4},{1,3},{2,6},{3,1},{4,0},{5,7},{6,2},{7,5},{8,12},{9,11},{10,... | collective-permute-start | bytes 221192 | tf_op jit(solution)/shard_map/ppermute | solution.py:727
  74.7 8.4 %collective-permute-start.17 = (bf16[576,128]{1,0:T(8,128)(2,1)S(1)}, bf16[576,128]{1,0:T(8,128)(2,1)S(1)}, u32[]{:S(2)}, u32[]{:S(2)}) collective-permute-start(bf16[576,128]{1,0:T(8,128)(2,1)S(1)} %join.4.value), channel_id=1, source_target_pairs={{0,2},{1,5},{2,0},{3,7},{4,6},{5,1},{6,4},{7,3},{8,10},{9,13},{10,... | collective-permute-start | bytes 442376 | tf_op jit(solution)/shard_map/ppermute | solution.py:727
  83.2 1.6 %collective-permute-start.18 = (bf16[1152,128]{1,0:T(8,128)(2,1)S(1)}, bf16[1152,128]{1,0:T(8,128)(2,1)S(1)}, u32[]{:S(2)}, u32[]{:S(2)}) collective-permute-start(bf16[1152,128]{1,0:T(8,128)(2,1)S(1)} %join.5.value), channel_id=1, source_target_pairs={{0,1},{1,0},{2,3},{3,2},{4,5},{5,4},{6,7},{7,6},{8,9},{9,8},{10,11... | collective-permute-start | bytes 884744 | tf_op jit(solution)/shard_map/ppermute | solution.py:727

commit v3 on v2

--- a/solution.py
+++ b/solution.py
@@ -117,15 +117,27 @@
     return dot(held[:, third:], held[:, : 2 * third], ((0,), (0,)))
 
 
-def forward_kernel(img, kern, ups, pre_out, acc, sums, wts, held):
+def forward_kernel(
+    first, img, kern, upstream, pre_out, acc, sums, maps, ups, wts, held, map_sems, up_sems
+):
     step = pl.program_id(0)
     last = pl.num_programs(0) - 1
-    rows, width, cin = img.shape[1:]
+    count, rows, width, cin = img.shape
     cout = kern.shape[3]
     inner = (rows - 2) * width
 
+    def map_copy(image):
+        return pltpu.make_async_copy(img.at[image], maps.at[image], map_sems.at[image])
+
+    def up_copy(image):
+        return pltpu.make_async_copy(upstream.at[image], ups.at[image], up_sems.at[image])
+
     @pl.when(step == 0)
     def _():
+        up_copy(0).start()
+        for image in range(1, count):
+            map_copy(image).start()
+            up_copy(image).start()
         blank = jnp.zeros((cin, cout), BF16)
         blocks = [(kern[a, 0], kern[a, 1]) for a in range(3)]
         blocks += [
@@ -139,9 +151,13 @@
         sums[...] = jnp.zeros_like(sums)
         held[...] = jnp.zeros_like(held)
 
+    @pl.when(step > 0)
+    def _():
+        map_copy(step).wait()
+
     acc[...] += statistics(held[...])
     blank = jnp.zeros((1, width, cin), BF16)
-    padded = jnp.concatenate([blank, img[0], blank], axis=0)
+    padded = jnp.concatenate([blank, maps[step], blank], axis=0)
     pre = paired_rows(padded, wts, cout)
     pre_out[step] = pre
     mid = pre[1 : rows - 1].reshape(inner, cout)
@@ -149,7 +165,8 @@
     shift = jnp.where(step == 0, mean, sums[2:3])
     sums[2:3] = shift
     delta = mid - shift
-    up = ups[0, 1 : rows - 1].reshape(inner, cout)
+    up_copy(step).wait()
+    up = ups[step, 1 : rows - 1].reshape(inner, cout)
     high, low = split(delta)
     held[:, :cout] = low
     held[:, cout : 2 * cout] = high
@@ -167,14 +184,18 @@
     return jnp.where(even, across, ahead), jnp.where(even, ahead, across)
 
 
-def slice_kernel(images, ahead, across, sems):
+def fetch_kernel(images, kern, ahead, across, taps, maps, sems):
     last = images.shape[1] - 1
     even = is_even()
+    pairs = (
+        (images.at[:, pl.ds(jnp.where(even, last, 0), 1)], ahead),
+        (images.at[:, pl.ds(jnp.where(even, 0, last), 1)], across),
+        (kern, taps),
+        (images.at[0], maps.at[0]),
+    )
     copies = [
-        pltpu.make_async_copy(images.at[:, pl.ds(row, 1)], target, sems.at[index])
-        for index, (row, target) in enumerate(
-            ((jnp.where(even, last, 0), ahead), (jnp.where(even, 0, last), across))
-        )
+        pltpu.make_async_copy(source, target, sems.at[index])
+        for index, (source, target) in enumerate(pairs)
     ]
     for copy in copies:
         copy.start()
@@ -290,8 +311,7 @@
     return average, mixed, symmetric / total_pix, bias, offset, color_sum
 
 
-def moment_kernel(image, pre, low, high, ups, img, ahead, across, sums, *rest):
-    acc, maps = rest[-2:]
+def image_moments(image, pre, low, high, ups, img, ahead, across, sums):
     rows, width, cin = img.shape[1:]
     cout = pre.shape[3]
     pixels = rows * width
@@ -305,16 +325,20 @@
         columns += [after.astype(BF16), value, before.astype(BF16)]
     right = jnp.concatenate(columns, axis=2).reshape(pixels, 6 * cout)
     left = jnp.concatenate([turned[:, a * width : a * width + pixels] for a in range(3)], axis=0)
-    product = dot(left, right)
     tiles = [turned[:, row * width : (row + 1) * width].astype(F32) for row in range(rows + 2)]
     middle = functools.reduce(jnp.add, tiles[2:rows])
     outer = ((0, 1), (1, rows), (rows, rows + 1))
     totals = jnp.concatenate([middle + tiles[one] + tiles[two] for one, two in outer], axis=0)
-    if len(rest) == 4:
-        product = rest[0][...] + product
-        totals = rest[1][...] + totals
-    acc[...] = product
-    maps[...] = totals
+    return dot(left, right), totals
+
+
+def moment_kernel(first, count, *refs):
+    acc, maps = refs[-2:]
+    found = [image_moments(first + index, *refs[:8]) for index in range(count)]
+    if len(refs) == 12:
+        found.append((refs[8][...], refs[9][...]))
+    acc[...] = functools.reduce(jnp.add, [product for product, _ in found])
+    maps[...] = functools.reduce(jnp.add, [totals for _, totals in found])
 
 
 def whitening_kernel(
@@ -398,19 +422,35 @@
     return split(full.reshape(rows * width, cout) - average)
 
 
-def pixel_kernel(
-    pre, low, high, ups, mats, paint, paint_rows, colored, pre_grad, edge_ahead, edge_across
-):
+def edge_gradient_kernel(low, high, ups, mats, paint_rows, edge_ahead, edge_across):
+    count, _, width, cout = low.shape
+    last = ups.shape[1] - 1
+    pre = jnp.concatenate([low[:, 0], high[:, 0]], axis=0).reshape(2 * count * width, cout)
+    up = jnp.concatenate([ups[:, 0], ups[:, last]], axis=0).reshape(2 * count * width, cout)
+    grad = pre_gradient(*split(pre - paint_rows[0:1]), up, mats, paint_rows)
+    shaped = grad.reshape(2 * count, width, cout)
+    edge_across[:, 0], edge_ahead[:, 0] = sides(shaped[count:], shaped[:count])
+
+
+def pre_gradient(big, small, up, mats, paint_rows):
+    cout = up.shape[1]
+    result = dot(jnp.concatenate([big, up, small], axis=1), mats[...])
+    return (result[:, :cout] + result[:, cout:] + paint_rows[2:3]).astype(BF16)
+
+
+def gradient_kernel(pre, low, high, ups, mats, paint_rows, pre_grad):
     image = pl.program_id(0)
     rows, width, cout = pre.shape[1:]
     big, small = centred_halves(image, pre, low, high, paint_rows[0:1])
     up = ups[image].reshape(rows * width, cout)
-    result = dot(jnp.concatenate([big, up, small], axis=1), mats[...])
-    grad = (result[:, :cout] + result[:, cout:] + paint_rows[2:3]).astype(BF16)
-    shaped = grad.reshape(rows, width, cout)
-    pre_grad[image] = shaped
-    edge_across[image], edge_ahead[image] = sides(shaped[rows - 1 :], shaped[:1])
-    result = dot(jnp.concatenate([big, small], axis=1), paint[...])
+    grad = pre_gradient(big, small, up, mats, paint_rows)
+    pre_grad[image] = grad.reshape(rows, width, cout)
+
+
+def paint_kernel(pre, low, high, paint, paint_rows, colored):
+    rows, width, cout = pre.shape[1:]
+    halves = centred_halves(pl.program_id(0), pre, low, high, paint_rows[0:1])
+    result = dot(jnp.concatenate(halves, axis=1), paint[...])
     result = result[:, :cout] + result[:, cout:] + paint_rows[1:2]
     colored[0] = result.astype(BF16).reshape(rows, width, cout)
 
@@ -486,32 +526,30 @@
     return pl.BlockSpec(memory_space=pltpu.VMEM)
 
 
-def forward(images, kernel, upstream):
+def forward(first, images, taps, upstream):
     count, rows, width, cin = images.shape
-    cout = kernel.shape[3]
-    pre_shape = (count, rows, width, cout)
+    cout = taps.shape[3]
+    shapes = [
+        ((count, rows, width, cout), F32),
+        ((2 * cout, 2 * cout), F32),
+        ((8, cout), F32),
+        (images.shape, BF16),
+        (upstream.shape, BF16),
+    ]
+    space = pl.BlockSpec(memory_space=pltpu.HBM)
     return pl.pallas_call(
         forward_kernel,
         grid=(count,),
-        in_specs=[
-            image_spec(images.shape),
-            whole_spec(kernel.shape),
-            image_spec(upstream.shape),
-        ],
-        out_specs=[
-            resident(),
-            whole_spec((2 * cout, 2 * cout)),
-            whole_spec((8, cout)),
-        ],
-        out_shape=[
-            jax.ShapeDtypeStruct(pre_shape, F32),
-            jax.ShapeDtypeStruct((2 * cout, 2 * cout), F32),
-            jax.ShapeDtypeStruct((8, cout), F32),
-        ],
+        in_specs=[resident(), space, resident(), space],
+        out_specs=[resident()] * len(shapes),
+        out_shape=[jax.ShapeDtypeStruct(shape, dtype) for shape, dtype in shapes],
         scratch_shapes=[
             pltpu.VMEM((10 * cin, 2 * cout), BF16),
             pltpu.VMEM(((rows - 2) * width, 3 * cout), BF16),
+            pltpu.SemaphoreType.DMA((count,)),
+            pltpu.SemaphoreType.DMA((count,)),
         ],
+        input_output_aliases={0: 3},
         compiler_params=pltpu.CompilerParams(vmem_limit_bytes=20 * MIB),
         cost_estimate=pl.CostEstimate(
             flops=2 * count * rows * width * 9 * cin * cout,
@@ -519,9 +557,7 @@
             transcendentals=0,
         ),
         name="forward_inner",
-    )(
-        in_hbm(images), in_hbm(kernel), in_hbm(upstream)
-    )
+    )(first, in_hbm(images), taps, in_hbm(upstream))
 
 
 def edges(stage, top, bot, pre, upstream, kernel, acc, sums):
@@ -545,13 +581,13 @@
     )(top, bot, pre, upstream, kernel, acc, sums)
 
 
-def moments(image, pre, low, high, upstream, images, top, bot, sums, *sofar):
+def moments(first, count, pre, low, high, upstream, images, top, bot, sums, *sofar):
     width, cin = images.shape[2:]
     cout = upstream.shape[3]
     rows = images.shape[1]
     operands = (pre, low, high, upstream, images, top, bot, sums, *sofar)
     return pl.pallas_call(
-        functools.partial(moment_kernel, image),
+        functools.partial(moment_kernel, first, count),
         in_specs=[resident()] * len(operands),
         out_specs=[resident()] * 2,
         out_shape=[
@@ -559,9 +595,9 @@
             jax.ShapeDtypeStruct((3 * cin, width), F32),
         ],
         input_output_aliases={8: 0, 9: 1} if sofar else {},
-        compiler_params=pltpu.CompilerParams(vmem_limit_bytes=20 * MIB),
+        compiler_params=pltpu.CompilerParams(vmem_limit_bytes=28 * MIB),
         cost_estimate=pl.CostEstimate(
-            flops=2 * rows * width * 18 * cin * cout, bytes_accessed=8 * MIB, transcendentals=0
+            flops=2 * count * rows * width * 18 * cin * cout, bytes_accessed=8 * MIB, transcendentals=0
         ),
         name="moments",
     )(*operands)
@@ -593,23 +629,51 @@
     )(own, other, colors, offset, sums, acc, maps)
 
 
-def pixels(pre, low, high, upstream, mats, paint, paint_rows):
+def edge_gradients(low, high, upstream, mats, paint_rows):
+    return pl.pallas_call(
+        edge_gradient_kernel,
+        in_specs=[resident()] * 5,
+        out_specs=[resident()] * 2,
+        out_shape=[jax.ShapeDtypeStruct(low.shape, BF16)] * 2,
+        compiler_params=pltpu.CompilerParams(vmem_limit_bytes=16 * MIB),
+        name="edge_gradients",
+    )(low, high, upstream, mats, paint_rows)
+
+
+def gradients(pre, low, high, upstream, mats, paint_rows):
     count, rows, width, cout = pre.shape
-    shapes = [pre.shape, pre.shape, (count, 1, width, cout), (count, 1, width, cout)]
-    return pl.pallas_call(
-        pixel_kernel,
+    return pl.pallas_call(
+        gradient_kernel,
         grid=(count,),
-        in_specs=[resident()] * 7,
-        out_specs=[image_spec(pre.shape)] + [resident()] * 3,
-        out_shape=[jax.ShapeDtypeStruct(shape, BF16) for shape in shapes],
+        in_specs=[resident()] * 6,
+        out_specs=resident(),
+        out_shape=jax.ShapeDtypeStruct(pre.shape, BF16),
         compiler_params=pltpu.CompilerParams(vmem_limit_bytes=16 * MIB),
         cost_estimate=pl.CostEstimate(
-            flops=2 * count * rows * width * 12 * cout * cout,
-            bytes_accessed=10 * pre.size,
+            flops=2 * count * rows * width * 6 * cout * cout,
+            bytes_accessed=8 * pre.size,
             transcendentals=0,
         ),
-        name="pixels",
-    )(pre, low, high, upstream, mats, paint, paint_rows)
+        name="pre_gradient",
+    )(pre, low, high, upstream, mats, paint_rows)
+
+
+def painted(pre, low, high, paint, paint_rows):
+    count, rows, width, cout = pre.shape
+    return pl.pallas_call(
+        paint_kernel,
+        grid=(count,),
+        in_specs=[resident()] * 5,
+        out_specs=image_spec(pre.shape),
+        out_shape=jax.ShapeDtypeStruct(pre.shape, BF16),
+        compiler_params=pltpu.CompilerParams(vmem_limit_bytes=16 * MIB),
+        cost_estimate=pl.CostEstimate(
+            flops=2 * count * rows * width * 4 * cout * cout,
+            bytes_accessed=6 * pre.size,
+            transcendentals=0,
+        ),
+        name="colored",
+    )(pre, low, high, paint, paint_rows)
 
 
 def turned_weights(kernel):
@@ -654,17 +718,21 @@
     )(*operands)
 
 
-def sliced(images):
+def fetched(images, kernel):
     count, rows, width, cin = images.shape
-    return pl.pallas_call(
-        slice_kernel,
-        in_specs=[pl.BlockSpec(memory_space=pltpu.HBM)],
-        out_specs=[resident(), resident()],
-        out_shape=[jax.ShapeDtypeStruct((count, 1, width, cin), BF16)] * 2,
-        scratch_shapes=[pltpu.SemaphoreType.DMA((2,))],
+    edge = (count, 1, width, cin)
+    space = pl.BlockSpec(memory_space=pltpu.HBM)
+    return pl.pallas_call(
+        fetch_kernel,
+        in_specs=[space, space],
+        out_specs=[resident()] * 4,
+        out_shape=[
+            jax.ShapeDtypeStruct(shape, BF16) for shape in (edge, edge, kernel.shape, images.shape)
+        ],
+        scratch_shapes=[pltpu.SemaphoreType.DMA((4,))],
         compiler_params=pltpu.CompilerParams(vmem_limit_bytes=4 * MIB),
         name="edge_rows",
-    )(in_hbm(images))
+    )(in_hbm(images), in_hbm(kernel))
 
 
 def small_call(kernel, name, *operands, out):
@@ -740,30 +808,32 @@
     devices = lax.axis_size("dp") * lax.axis_size("rows")
     total_pix = count * rows * width * devices
     plan = stages(devices)
-    top, bot = halos(*sliced(images))
-    pre, acc, sums = forward(images, kernel, upstream)
+    ahead, across, kernel, maps = fetched(images, kernel)
+    top, bot = halos(ahead, across)
+    pre, acc, sums, images, upstream = forward(maps, images, kernel, upstream)
     low, high, value, send = edges(plan[0], top, bot, pre, upstream, kernel, acc, sums)
     state = {"next": 0, "moments": (), "grad": None}
 
-    def summed(send, stage):
-        image = state["next"]
-        if image >= count:
+    def summed(send, stage, many):
+        first = state["next"]
+        many = min(many, count - first)
+        if many < 1:
             return exchange(send, devices, stage)
-        state["next"] = image + 1
+        state["next"] = first + many
         operands = (pre, low, high, upstream, images, top, bot, sums, *state["moments"])
         received, state["moments"] = beside(
-            send, devices, stage, functools.partial(moments, image), operands
+            send, devices, stage, functools.partial(moments, first, many), operands
         )
         return received
 
-    value = value + summed(send, plan[0])
+    value = value + summed(send, plan[0], 0)
     for stage in plan[1:]:
-        value = value + summed(value, stage)
-    received = summed(value, plan[0])
-    for image in range(state["next"], count):
-        state["moments"] = moments(
-            image, pre, low, high, upstream, images, top, bot, sums, *state["moments"]
-        )
+        value = value + summed(value, stage, 2 if stage == plan[1] else 1)
+    received = summed(value, plan[0], 1)
+    first = state["next"]
+    if first < count:
+        operands = (pre, low, high, upstream, images, top, bot, sums, *state["moments"])
+        state["moments"] = moments(first, count - first, *operands)
     value, send, grad_colors, mats, paint, paint_rows = whitened(
         total_pix,
         plan[0],
@@ -774,7 +844,13 @@
         sums,
         *state["moments"],
     )
-    received, turned = beside(send, devices, plan[0], turned_weights, (kernel,))
+    received, (edge_ahead, edge_across, turned) = beside(
+        send,
+        devices,
+        plan[0],
+        lambda kernel, *operands: (*edge_gradients(*operands), turned_weights(kernel)),
+        (kernel, low, high, upstream, mats, paint_rows),
+    )
     state["next"] = 0
     shares = [1, 2, 1, 1, 1]
 
@@ -800,12 +876,16 @@
         else:
             value = send = value + received
         if stage == plan[1]:
-            received, (colored, pre_grad, edge_ahead, edge_across) = beside(
-                send, devices, stage, pixels, (pre, low, high, upstream, mats, paint, paint_rows)
+            send, edge_ahead, edge_across = lax.optimization_barrier(
+                (send, edge_ahead, edge_across)
+            )
+            grad_top, grad_bot = halos(edge_ahead, edge_across)
+            received, pre_grad = beside(
+                send, devices, stage, gradients, (pre, low, high, upstream, mats, paint_rows)
             )
         elif stage == plan[2]:
-            received, (grad_top, grad_bot) = beside(
-                send, devices, stage, halos, (edge_ahead, edge_across)
+            received, colored = beside(
+                send, devices, stage, painted, (pre, low, high, paint, paint_rows)
             )
         else:
             received = transfer(send, stage)

time: 86.1 us -> 80.7 us (0.937)
  starting transfers between devices: 29.6 us -> 25.2 us
  waiting for transfers between devices: 15.2 us -> 12.4 us
  Pallas kernels: 39.9 us -> 41.8 us
    ppermute x15, starting transfers between devices: 27.6 us -> 22.6 us  [exchange(): return lax.ppermute(value, AXES, pairs)]
    ppermute x15, waiting for transfers between devices: 15.2 us -> 12.4 us  [exchange(): return lax.ppermute(value, AXES, pairs)]
    pallas_call x9 -> x10, Pallas kernels: 24.3 us -> 26.3 us  [the longest x5 9.96 us: moments(): pl.pallas_call(functools.partial(moment_kernel, first, count), in_specs=[...]
  transfers between devices with their start and end apart: 19 -> 19, of which waited for: 13 -> 13; matrix products, arithmetic and copies ran while one was open for 0% -> 0% of each run, Pallas kernels for 39% -> 43%
where the time goes in v3:
time: 80.7 us; the launch traced here: 80.5 us
  Pallas kernels  41.8 us (52%)
  starting transfers between devices  25.2 us (31%)
  waiting for transfers between devices  12.4 us (15%)
  between operations  1.03 us (1%)
    ppermute x15, starting transfers between devices, exchange(): return lax.ppermute(value, AXES, pairs)  22.6 us
    ppermute x15, waiting for transfers between devices, exchange(): return lax.ppermute(value, AXES, pairs)  12.4 us
    pallas_call x5, Pallas kernels, moments(): pl.pallas_call(functools.partial(moment_kernel, first, count), in_specs=[...  9.96 us
    pallas_call x5, Pallas kernels, image_gradient(): pl.pallas_call(functools.partial(image_kernel, first), grid=(count,), in_...  9.1 us
    pallas_call x1, Pallas kernels, forward(): pl.pallas_call(forward_kernel, grid=(count,), in_specs=[resident(), space...  8.02 us
    pallas_call x1, Pallas kernels, painted(): pl.pallas_call(paint_kernel, grid=(count,), in_specs=[resident()] * 5, ou...  3.41 us
    pallas_call x1, Pallas kernels, whitened(): pl.pallas_call(functools.partial(whitening_kernel, total_pix, stage), in_...  3.23 us
    pallas_call x1, Pallas kernels, gradients(): pl.pallas_call(gradient_kernel, grid=(count,), in_specs=[resident()] * 6,...  2.63 us
  transfers between devices with their start and end apart: 19, of which 13 were waited for; matrix products, arithmetic and copies ran while one was open for 0% of the time, Pallas kernels for 43%

profile of v3, /device:TPU:0, one launch (start us, length us, event | category | flops | bytes accessed | tf_op | source)
XLA Modules:
  0.0 80.5 jit_solution(2405634531296247477)
XLA Ops:
  3.3 8.0 %forward_inner.1 = (f32[6,8,128,128]{3,2,1,0:T(8,128)S(1)}, f32[256,256]{1,0:T(8,128)S(1)}, f32[8,128]{1,0:T(8,128)S(1)}, bf16[6,8,128,256]{3,2,1,0:T(8,128)(2,1)S(1)}, bf16[6,8,128,128]{3,2,1,0:T(8,128)(2,1)S(1)}) custom-call(bf16[6,8,128,256]{3,2,1,0:T(8,128)(2,1)S(1)} %get-tuple-element.185.first, ...), custom_call_target="tpu_custom_call", output_to_operand_aliasing={{3}: (0, {})} | custom-call | flops 3623878656 | bytes 7864320 | tf_op jit(solution)/shard_map/forward_inner/pallas_call | solution.py:540
  12.5 4.0 %collective-permute-start.2 = (f32[72,128]{1,0:T(8,128)S(1)}, f32[72,128]{1,0:T(8,128)S(1)}, u32[]{:S(2)}, u32[]{:S(2)}) collective-permute-start(f32[72,128]{1,0:T(8,128)S(1)} %get-tuple-element.192), channel_id=1, source_target_pairs={{0,1},{1,0},{2,3},{3,2},{4,5},{5,4},{6,7},{7,6},{8,9},{9,8},{10,11... | collective-permute-start | bytes 110600 | tf_op jit(solution)/shard_map/ppermute | solution.py:795
  17.6 2.7 %moments.5 = (f32[768,768]{1,0:T(8,128)S(1)}, f32[768,128]{1,0:T(8,128)S(1)}) custom-call(f32[6,8,128,128]{3,2,1,0:T(8,128)S(1)} %get-tuple-element.304.pre.refs_0_, f32[6,1,128,128]{3,2,1,0:T(8,128)S(1)} %get-tuple-element.305.refs_1_.low, f32[6,1,128,128]{3,2,1,0:T(8,128)S(1)} %get-tuple-element.306.refs_2_.high, ...), custom_call_target="tpu_custom_call" | custom-call | flops 2415919104 | bytes 8388608 | tf_op jit(solution)/shard_map/moments/pallas_call | solution.py:589
  22.7 1.8 %moments.6 = (f32[768,768]{1,0:T(8,128)S(1)}, f32[768,128]{1,0:T(8,128)S(1)}) custom-call(f32[6,8,128,128]{3,2,1,0:T(8,128)S(1)} %get-tuple-element.304.pre.refs_0_, f32[6,1,128,128]{3,2,1,0:T(8,128)S(1)} %get-tuple-element.305.refs_1_.low, f32[6,1,128,128]{3,2,1,0:T(8,128)S(1)} %get-tuple-element.306.refs_2_.high, ...), custom_call_target="tpu_custom_call", output_to_operand_aliasing={{0}: (8, {}), {1}: (9, {})} | custom-call | flops 1207959552 | bytes 8388608 | tf_op jit(solution)/shard_map/moments/pallas_call | solution.py:589
  26.8 1.8 %moments.7 = (f32[768,768]{1,0:T(8,128)S(1)}, f32[768,128]{1,0:T(8,128)S(1)}) custom-call(f32[6,8,128,128]{3,2,1,0:T(8,128)S(1)} %get-tuple-element.304.pre.refs_0_, f32[6,1,128,128]{3,2,1,0:T(8,128)S(1)} %get-tuple-element.305.refs_1_.low, f32[6,1,128,128]{3,2,1,0:T(8,128)S(1)} %get-tuple-element.306.refs_2_.high, ...), custom_call_target="tpu_custom_call", output_to_operand_aliasing={{0}: (8, {}), {1}: (9, {})} | custom-call | flops 1207959552 | bytes 8388608 | tf_op jit(solution)/shard_map/moments/pallas_call | solution.py:589
  29.2 2.6 %collective-permute-start.6 = (f32[72,128]{1,0:T(8,128)S(1)}, f32[72,128]{1,0:T(8,128)S(1)}, u32[]{:S(2)}, u32[]{:S(2)}) collective-permute-start(f32[72,128]{1,0:T(8,128)S(1)} %add.24), channel_id=1, source_target_pairs={{0,16},{1,17},{2,18},{3,19},{4,20},{5,21},{6,22},{7,23},{8,24},{9,... | collective-permute-start | bytes 110600 | tf_op jit(solution)/shard_map/ppermute | solution.py:795
  31.8 1.8 %moments.8 = (f32[768,768]{1,0:T(8,128)S(1)}, f32[768,128]{1,0:T(8,128)S(1)}) custom-call(f32[6,8,128,128]{3,2,1,0:T(8,128)S(1)} %get-tuple-element.304.pre.refs_0_, f32[6,1,128,128]{3,2,1,0:T(8,128)S(1)} %get-tuple-element.305.refs_1_.low, f32[6,1,128,128]{3,2,1,0:T(8,128)S(1)} %get-tuple-element.306.refs_2_.high, ...), custom_call_target="tpu_custom_call", output_to_operand_aliasing={{0}: (8, {}), {1}: (9, {})} | custom-call | flops 1207959552 | bytes 8388608 | tf_op jit(solution)/shard_map/moments/pallas_call | solution.py:589
  34.2 1.8 %moments.9 = (f32[768,768]{1,0:T(8,128)S(1)}, f32[768,128]{1,0:T(8,128)S(1)}) custom-call(f32[6,8,128,128]{3,2,1,0:T(8,128)S(1)} %get-tuple-element.304.pre.refs_0_, f32[6,1,128,128]{3,2,1,0:T(8,128)S(1)} %get-tuple-element.305.refs_1_.low, f32[6,1,128,128]{3,2,1,0:T(8,128)S(1)} %get-tuple-element.306.refs_2_.high, ...), custom_call_target="tpu_custom_call", output_to_operand_aliasing={{0}: (8, {}), {1}: (9, {})} | custom-call | flops 1207959552 | bytes 8388608 | tf_op jit(solution)/shard_map/moments/pallas_call | solution.py:589
  36.0 3.2 %whitening.1 = (f32[1152,128]{1,0:T(8,128)S(1)}, f32[1152,128]{1,0:T(8,128)S(1)}, f32[2,64,64]{2,1,0:T(8,128)}, bf16[384,256]{1,0:T(8,128)(2,1)S(1)}, bf16[256,2...) custom-call(f32[72,128]{1,0:T(8,128)S(1)} %add.25.own, f32[72,128]{1,0:T(8,128)S(1)} %collective-permute-done.7.other, ...), custom_call_target="tpu_custom_call" | custom-call | flops 603979776 | bytes 8388608 | tf_op jit(solution)/shard_map/whitening/pallas_call | solution.py:618
  43.8 2.6 %pre_gradient.1.pre_grad = bf16[6,8,128,128]{3,2,1,0:T(8,128)(2,1)S(1)} custom-call(f32[6,8,128,128]{3,2,1,0:T(8,128)S(1)} %get-tuple-element.304.pre.refs_0_, f32[6,1,128,128]{3,2,1,0:T(8,128)S(1)} %get-tuple-element.305.refs_1_.low, f32[6,1,128,128]{3,2,1,0:T(8,128)S(1)} %get-tuple-element.306.refs_2_.high, ...), custom_call_target="tpu_custom_call" | custom-call | flops 1207959552 | bytes 6291456 | tf_op jit(solution)/shard_map/pre_gradient/pallas_call | solution.py:645
  46.4 1.8 %collective-permute-done.9.received = f32[576,128]{1,0:T(8,128)S(1)} collective-permute-done((f32[576,128]{1,0:T(8,128)S(1)}, f32[576,128]{1,0:T(8,128)S(1)}, u32[]{:S(2)}, u32[]{:S(2)}) %collective-permute-start.9) | collective-permute-done | bytes 294944 | tf_op jit(solution)/shard_map/ppermute | solution.py:795
  49.9 3.4 %colored.1 = bf16[6,8,128,128]{3,2,1,0:T(8,128)(2,1)} custom-call(f32[6,8,128,128]{3,2,1,0:T(8,128)S(1)} %get-tuple-element.304.pre.refs_0_, f32[6,1,128,128]{3,2,1,0:T(8,128)S(1)} %get-tuple-element.305.refs_1_.low, f32[6,1,128,128]{3,2,1,0:T(8,128)S(1)} %get-tuple-element.306.refs_2_.high, bf16[256,256]{1,0:T(8,128)(2,1)S(1)} %get-tuple-element.307.paint, ...), custom_call_target="tpu_custom_call" | custom-call | flops 805306368 | bytes 4718592 | tf_op jit(solution)/shard_map/colored/pallas_call | solution.py:663
  53.5 1.6 %collective-permute-start.13 = (f32[144,128]{1,0:T(8,128)S(1)}, f32[144,128]{1,0:T(8,128)S(1)}, u32[]{:S(2)}, u32[]{:S(2)}) collective-permute-start(f32[144,128]{1,0:T(8,128)S(1)} %get-tuple-element.318), channel_id=1, source_target_pairs={{0,8},{1,9},{2,10},{3,11},{4,12},{5,13},{6,14},{7,15},{8,0},{9,1},... | collective-permute-start | bytes 221192 | tf_op jit(solution)/shard_map/ppermute | solution.py:795
  55.2 1.6 %image_gradient.5.rest_0_ = bf16[6,8,128,256]{3,2,1,0:T(8,128)(2,1)} custom-call(bf16[6,8,128,128]{3,2,1,0:T(8,128)(2,1)S(1)} %pre_gradient.1.pre_grad, bf16[6,1,128,128]{3,2,1,0:T(8,128)(2,1)S(1)} %collective-permute-done.11.ahead, bf16[6,1,128,128]{3,2,1,0:T(8,128)(2,1)S(1)} %collective-permute-done.12.across, bf16[1152,256]{1,0:T(8,128)(2,1)S(1)} %turned_weights.1.wts), custom_call_target="tpu_custom_call" | custom-call | flops 603979776 | bytes 786432 | tf_op jit(solution)/shard_map/image_gradient/pallas_call | solution.py:704
  58.0 2.9 %collective-permute-start.14 = (f32[144,128]{1,0:T(8,128)S(1)}, f32[144,128]{1,0:T(8,128)S(1)}, u32[]{:S(2)}, u32[]{:S(2)}) collective-permute-start(f32[144,128]{1,0:T(8,128)S(1)} %add.26), channel_id=1, source_target_pairs={{0,16},{1,17},{2,18},{3,19},{4,20},{5,21},{6,22},{7,23},{8,24},{9,... | collective-permute-start | bytes 221192 | tf_op jit(solution)/shard_map/ppermute | solution.py:795
  60.9 2.5 %image_gradient.6.rest_0_ = bf16[6,8,128,256]{3,2,1,0:T(8,128)(2,1)} custom-call(bf16[6,8,128,128]{3,2,1,0:T(8,128)(2,1)S(1)} %pre_gradient.1.pre_grad, bf16[6,1,128,128]{3,2,1,0:T(8,128)(2,1)S(1)} %collective-permute-done.11.ahead, bf16[6,1,128,128]{3,2,1,0:T(8,128)(2,1)S(1)} %collective-permute-done.12.across, ...), custom_call_target="tpu_custom_call", output_to_operand_aliasing={{}: (4, {})} | custom-call | flops 1207959552 | bytes 1572864 | tf_op jit(solution)/shard_map/image_gradient/pallas_call | solution.py:704
  63.4 1.7 %collective-permute-start.15 = (bf16[144,128]{1,0:T(8,128)(2,1)S(1)}, bf16[144,128]{1,0:T(8,128)(2,1)S(1)}, u32[]{:S(2)}, u32[]{:S(2)}) collective-permute-start(bf16[144,128]{1,0:T(8,128)(2,1)S(1)} %add_convert_fusion.value), channel_id=1, source_target_pairs={{0,8},{1,9},{2,10},{3,11},{4,12},{5,13},{6,14},{7,15},{8,0},{9,1},... | collective-permute-start | bytes 110600 | tf_op jit(solution)/shard_map/ppermute | solution.py:795
  65.1 1.6 %image_gradient.7.rest_0_ = bf16[6,8,128,256]{3,2,1,0:T(8,128)(2,1)} custom-call(bf16[6,8,128,128]{3,2,1,0:T(8,128)(2,1)S(1)} %pre_gradient.1.pre_grad, bf16[6,1,128,128]{3,2,1,0:T(8,128)(2,1)S(1)} %collective-permute-done.11.ahead, bf16[6,1,128,128]{3,2,1,0:T(8,128)(2,1)S(1)} %collective-permute-done.12.across, ...), custom_call_target="tpu_custom_call", output_to_operand_aliasing={{}: (4, {})} | custom-call | flops 603979776 | bytes 786432 | tf_op jit(solution)/shard_map/image_gradient/pallas_call | solution.py:704
  67.4 1.8 %collective-permute-start.16 = (bf16[288,128]{1,0:T(8,128)(2,1)S(1)}, bf16[288,128]{1,0:T(8,128)(2,1)S(1)}, u32[]{:S(2)}, u32[]{:S(2)}) collective-permute-start(bf16[288,128]{1,0:T(8,128)(2,1)S(1)} %join.3.value), channel_id=1, source_target_pairs={{0,4},{1,3},{2,6},{3,1},{4,0},{5,7},{6,2},{7,5},{8,12},{9,11},{10,... | collective-permute-start | bytes 221192 | tf_op jit(solution)/shard_map/ppermute | solution.py:795
  69.2 1.6 %image_gradient.8.rest_0_ = bf16[6,8,128,256]{3,2,1,0:T(8,128)(2,1)} custom-call(bf16[6,8,128,128]{3,2,1,0:T(8,128)(2,1)S(1)} %pre_gradient.1.pre_grad, bf16[6,1,128,128]{3,2,1,0:T(8,128)(2,1)S(1)} %collective-permute-done.11.ahead, bf16[6,1,128,128]{3,2,1,0:T(8,128)(2,1)S(1)} %collective-permute-done.12.across, ...), custom_call_target="tpu_custom_call", output_to_operand_aliasing={{}: (4, {})} | custom-call | flops 603979776 | bytes 786432 | tf_op jit(solution)/shard_map/image_gradient/pallas_call | solution.py:704
  70.9 1.7 %collective-permute-done.16.received = bf16[288,128]{1,0:T(8,128)(2,1)S(1)} collective-permute-done((bf16[288,128]{1,0:T(8,128)(2,1)S(1)}, bf16[288,128]{1,0:T(8,128)(2,1)S(1)}, u32[]{:S(2)}, u32[]{:S(2)}) %collective-permute-start.16) | collective-permute-done | bytes 73760 | tf_op jit(solution)/shard_map/ppermute | solution.py:795
  72.6 1.7 %collective-permute-start.17 = (bf16[576,128]{1,0:T(8,128)(2,1)S(1)}, bf16[576,128]{1,0:T(8,128)(2,1)S(1)}, u32[]{:S(2)}, u32[]{:S(2)}) collective-permute-start(bf16[576,128]{1,0:T(8,128)(2,1)S(1)} %join.4.value), channel_id=1, source_target_pairs={{0,2},{1,5},{2,0},{3,7},{4,6},{5,1},{6,4},{7,3},{8,10},{9,13},{10,... | collective-permute-start | bytes 442376 | tf_op jit(solution)/shard_map/ppermute | solution.py:795
  74.2 1.6 %image_gradient.9 = bf16[6,8,128,256]{3,2,1,0:T(8,128)(2,1)} custom-call(bf16[6,8,128,128]{3,2,1,0:T(8,128)(2,1)S(1)} %pre_gradient.1.pre_grad, bf16[6,1,128,128]{3,2,1,0:T(8,128)(2,1)S(1)} %collective-permute-done.11.ahead, bf16[6,1,128,128]{3,2,1,0:T(8,128)(2,1)S(1)} %collective-permute-done.12.across, ...), custom_call_target="tpu_custom_call", output_to_operand_aliasing={{}: (4, {})} | custom-call | flops 603979776 | bytes 786432 | tf_op jit(solution)/shard_map/image_gradient/pallas_call | solution.py:704
  75.9 1.9 %collective-permute-done.17.received = bf16[576,128]{1,0:T(8,128)(2,1)S(1)} collective-permute-done((bf16[576,128]{1,0:T(8,128)(2,1)S(1)}, bf16[576,128]{1,0:T(8,128)(2,1)S(1)}, u32[]{:S(2)}, u32[]{:S(2)}) %collective-permute-start.17) | collective-permute-done | bytes 147488 | tf_op jit(solution)/shard_map/ppermute | solution.py:795
  (51 shorter events, 21.6 us)
Async XLA Ops:
  2.1 9.2 %collective-permute-start = (bf16[6,1,128,256]{3,2,1,0:T(8,128)(2,1)S(1)}, bf16[6,1,128,256]{3,2,1,0:T(8,128)(2,1)S(1)}, u32[]{:S(2)}, u32[]{:S(2)}) collective-permute-start(bf16[6,1,128,256]{3,2,1,0:T(8,128)(2,1)S(1)} %get-tuple-element.183), channel_id=1, source_target_pairs={{0,1},{2,3},{1,0},{3,2},{4,5},{6,7},{5,4},{7,6},{8,9},{10,11},{9,8... | collective-permute-start | bytes 1179656 | tf_op jit(solution)/shard_map/ppermute | solution.py:790
  2.7 8.7 %collective-permute-start.1 = (bf16[6,1,128,256]{3,2,1,0:T(8,128)(2,1)S(1)}, bf16[6,1,128,256]{3,2,1,0:T(8,128)(2,1)S(1)}, u32[]{:S(2)}, u32[]{:S(2)}) collective-permute-start(bf16[6,1,128,256]{3,2,1,0:T(8,128)(2,1)S(1)} %get-tuple-element.184), channel_id=1, source_target_pairs={{1,2},{2,1},{5,6},{6,5},{9,10},{10,9},{13,14},{14,13},{17,18},{18,... | collective-permute-start | bytes 1179656 | tf_op jit(solution)/shard_map/ppermute | solution.py:790
  12.5 4.8 %collective-permute-start.2 = (f32[72,128]{1,0:T(8,128)S(1)}, f32[72,128]{1,0:T(8,128)S(1)}, u32[]{:S(2)}, u32[]{:S(2)}) collective-permute-start(f32[72,128]{1,0:T(8,128)S(1)} %get-tuple-element.192), channel_id=1, source_target_pairs={{0,1},{1,0},{2,3},{3,2},{4,5},{5,4},{6,7},{7,6},{8,9},{9,8},{10,11... | collective-permute-start | bytes 110600 | tf_op jit(solution)/shard_map/ppermute | solution.py:795
  17.3 4.0 %collective-permute-start.3 = (f32[72,128]{1,0:T(8,128)S(1)}, f32[72,128]{1,0:T(8,128)S(1)}, u32[]{:S(2)}, u32[]{:S(2)}) collective-permute-start(f32[72,128]{1,0:T(8,128)S(1)} %add.21), channel_id=1, source_target_pairs={{0,2},{1,5},{2,0},{3,7},{4,6},{5,1},{6,4},{7,3},{8,10},{9,13},{10,... | collective-permute-start | bytes 110600 | tf_op jit(solution)/shard_map/ppermute | solution.py:795
  21.3 4.0 %collective-permute-start.4 = (f32[72,128]{1,0:T(8,128)S(1)}, f32[72,128]{1,0:T(8,128)S(1)}, u32[]{:S(2)}, u32[]{:S(2)}) collective-permute-start(f32[72,128]{1,0:T(8,128)S(1)} %add.22), channel_id=1, source_target_pairs={{0,4},{1,3},{2,6},{3,1},{4,0},{5,7},{6,2},{7,5},{8,12},{9,11},{10,... | collective-permute-start | bytes 110600 | tf_op jit(solution)/shard_map/ppermute | solution.py:795
  25.2 4.0 %collective-permute-start.5 = (f32[72,128]{1,0:T(8,128)S(1)}, f32[72,128]{1,0:T(8,128)S(1)}, u32[]{:S(2)}, u32[]{:S(2)}) collective-permute-start(f32[72,128]{1,0:T(8,128)S(1)} %add.23), channel_id=1, source_target_pairs={{0,8},{1,9},{2,10},{3,11},{4,12},{5,13},{6,14},{7,15},{8,0},{9,1},... | collective-permute-start | bytes 110600 | tf_op jit(solution)/shard_map/ppermute | solution.py:795
  29.2 4.9 %collective-permute-start.6 = (f32[72,128]{1,0:T(8,128)S(1)}, f32[72,128]{1,0:T(8,128)S(1)}, u32[]{:S(2)}, u32[]{:S(2)}) collective-permute-start(f32[72,128]{1,0:T(8,128)S(1)} %add.24), channel_id=1, source_target_pairs={{0,16},{1,17},{2,18},{3,19},{4,20},{5,21},{6,22},{7,23},{8,24},{9,... | collective-permute-start | bytes 110600 | tf_op jit(solution)/shard_map/ppermute | solution.py:795
  34.1 1.9 %copy-start = (f32[2,64,64]{2,1,0:T(8,128)S(1)}, f32[2,64,64]{2,1,0:T(8,128)}, u32[]{:S(2)}) copy-start(f32[2,64,64]{2,1,0:T(8,128)} %colors.1) | copy-start | bytes 98308
  34.1 1.9 %copy-start.1 = (f32[128]{0:T(128)S(1)}, f32[128]{0:T(128)}, u32[]{:S(2)}) copy-start(f32[128]{0:T(128)} %param.8) | copy-start | bytes 1540
  34.1 1.9 %collective-permute-start.7 = (f32[72,128]{1,0:T(8,128)S(1)}, f32[72,128]{1,0:T(8,128)S(1)}, u32[]{:S(2)}, u32[]{:S(2)}) collective-permute-start(f32[72,128]{1,0:T(8,128)S(1)} %add.25.own), channel_id=1, source_target_pairs={{0,1},{1,0},{2,3},{3,2},{4,5},{5,4},{6,7},{7,6},{8,9},{9,8},{10,11... | collective-permute-start | bytes 110600 | tf_op jit(solution)/shard_map/ppermute | solution.py:795
  39.3 2.1 %collective-permute-start.8 = (f32[1152,128]{1,0:T(8,128)S(1)}, f32[1152,128]{1,0:T(8,128)S(1)}, u32[]{:S(2)}, u32[]{:S(2)}) collective-permute-start(f32[1152,128]{1,0:T(8,128)S(1)} %get-tuple-element.278), channel_id=1, source_target_pairs={{0,1},{1,0},{2,3},{3,2},{4,5},{5,4},{6,7},{7,6},{8,9},{9,8},{10,11... | collective-permute-start | bytes 1769480 | tf_op jit(solution)/shard_map/ppermute | solution.py:795
  41.5 6.8 %collective-permute-start.9 = (f32[576,128]{1,0:T(8,128)S(1)}, f32[576,128]{1,0:T(8,128)S(1)}, u32[]{:S(2)}, u32[]{:S(2)}) collective-permute-start(f32[576,128]{1,0:T(8,128)S(1)} %get-tuple-element.293), channel_id=1, source_target_pairs={{0,2},{1,5},{2,0},{3,7},{4,6},{5,1},{6,4},{7,3},{8,10},{9,13},{10,... | collective-permute-start | bytes 884744 | tf_op jit(solution)/shard_map/ppermute | solution.py:795
  42.4 11.1 %collective-permute-start.11 = (bf16[6,1,128,128]{3,2,1,0:T(8,128)(2,1)S(1)}, bf16[6,1,128,128]{3,2,1,0:T(8,128)(2,1)S(1)}, u32[]{:S(2)}, u32[]{:S(2)}) collective-permute-start(bf16[6,1,128,128]{3,2,1,0:T(8,128)(2,1)S(1)} %get-tuple-element.315), channel_id=1, source_target_pairs={{0,1},{2,3},{1,0},{3,2},{4,5},{6,7},{5,4},{7,6},{8,9},{10,11},{9,8... | collective-permute-start | bytes 589832 | tf_op jit(solution)/shard_map/ppermute | solution.py:790
  43.1 10.4 %collective-permute-start.12 = (bf16[6,1,128,128]{3,2,1,0:T(8,128)(2,1)S(1)}, bf16[6,1,128,128]{3,2,1,0:T(8,128)(2,1)S(1)}, u32[]{:S(2)}, u32[]{:S(2)}) collective-permute-start(bf16[6,1,128,128]{3,2,1,0:T(8,128)(2,1)S(1)} %get-tuple-element.316), channel_id=1, source_target_pairs={{1,2},{2,1},{5,6},{6,5},{9,10},{10,9},{13,14},{14,13},{17,18},{18,... | collective-permute-start | bytes 589832 | tf_op jit(solution)/shard_map/ppermute | solution.py:790
  48.3 5.2 %collective-permute-start.10 = (f32[288,128]{1,0:T(8,128)S(1)}, f32[288,128]{1,0:T(8,128)S(1)}, u32[]{:S(2)}, u32[]{:S(2)}) collective-permute-start(f32[288,128]{1,0:T(8,128)S(1)} %get-tuple-element.303), channel_id=1, source_target_pairs={{0,4},{1,3},{2,6},{3,1},{4,0},{5,7},{6,2},{7,5},{8,12},{9,11},{10,... | collective-permute-start | bytes 442376 | tf_op jit(solution)/shard_map/ppermute | solution.py:795
  53.5 4.4 %collective-permute-start.13 = (f32[144,128]{1,0:T(8,128)S(1)}, f32[144,128]{1,0:T(8,128)S(1)}, u32[]{:S(2)}, u32[]{:S(2)}) collective-permute-start(f32[144,128]{1,0:T(8,128)S(1)} %get-tuple-element.318), channel_id=1, source_target_pairs={{0,8},{1,9},{2,10},{3,11},{4,12},{5,13},{6,14},{7,15},{8,0},{9,1},... | collective-permute-start | bytes 221192 | tf_op jit(solution)/shard_map/ppermute | solution.py:795
  58.0 5.4 %collective-permute-start.14 = (f32[144,128]{1,0:T(8,128)S(1)}, f32[144,128]{1,0:T(8,128)S(1)}, u32[]{:S(2)}, u32[]{:S(2)}) collective-permute-start(f32[144,128]{1,0:T(8,128)S(1)} %add.26), channel_id=1, source_target_pairs={{0,16},{1,17},{2,18},{3,19},{4,20},{5,21},{6,22},{7,23},{8,24},{9,... | collective-permute-start | bytes 221192 | tf_op jit(solution)/shard_map/ppermute | solution.py:795
  63.4 4.0 %collective-permute-start.15 = (bf16[144,128]{1,0:T(8,128)(2,1)S(1)}, bf16[144,128]{1,0:T(8,128)(2,1)S(1)}, u32[]{:S(2)}, u32[]{:S(2)}) collective-permute-start(bf16[144,128]{1,0:T(8,128)(2,1)S(1)} %add_convert_fusion.value), channel_id=1, source_target_pairs={{0,8},{1,9},{2,10},{3,11},{4,12},{5,13},{6,14},{7,15},{8,0},{9,1},... | collective-permute-start | bytes 110600 | tf_op jit(solution)/shard_map/ppermute | solution.py:795
  67.4 5.1 %collective-permute-start.16 = (bf16[288,128]{1,0:T(8,128)(2,1)S(1)}, bf16[288,128]{1,0:T(8,128)(2,1)S(1)}, u32[]{:S(2)}, u32[]{:S(2)}) collective-permute-start(bf16[288,128]{1,0:T(8,128)(2,1)S(1)} %join.3.value), channel_id=1, source_target_pairs={{0,4},{1,3},{2,6},{3,1},{4,0},{5,7},{6,2},{7,5},{8,12},{9,11},{10,... | collective-permute-start | bytes 221192 | tf_op jit(solution)/shard_map/ppermute | solution.py:795
  72.6 5.2 %collective-permute-start.17 = (bf16[576,128]{1,0:T(8,128)(2,1)S(1)}, bf16[576,128]{1,0:T(8,128)(2,1)S(1)}, u32[]{:S(2)}, u32[]{:S(2)}) collective-permute-start(bf16[576,128]{1,0:T(8,128)(2,1)S(1)} %join.4.value), channel_id=1, source_target_pairs={{0,2},{1,5},{2,0},{3,7},{4,6},{5,1},{6,4},{7,3},{8,10},{9,13},{10,... | collective-permute-start | bytes 442376 | tf_op jit(solution)/shard_map/ppermute | solution.py:795
  77.9 1.6 %collective-permute-start.18 = (bf16[1152,128]{1,0:T(8,128)(2,1)S(1)}, bf16[1152,128]{1,0:T(8,128)(2,1)S(1)}, u32[]{:S(2)}, u32[]{:S(2)}) collective-permute-start(bf16[1152,128]{1,0:T(8,128)(2,1)S(1)} %join.5.value), channel_id=1, source_target_pairs={{0,1},{1,0},{2,3},{3,2},{4,5},{5,4},{6,7},{7,6},{8,9},{9,8},{10,11... | collective-permute-start | bytes 884744 | tf_op jit(solution)/shard_map/ppermute | solution.py:795

commit v4 on v3

--- a/solution.py
+++ b/solution.py
@@ -33,7 +33,7 @@
     bits = [1 << i for i in range(devices.bit_length() - 1)]
     plan = [(bit, bit) for bit in bits]
     if len(bits) > 2:
-        plan[1:3] = [(2, 4), (4, 2)]
+        plan[1:3] = [(4, 2), (2, 4)]
     return plan
 
 
@@ -150,22 +150,22 @@
         acc[...] = jnp.zeros_like(acc)
         sums[...] = jnp.zeros_like(sums)
         held[...] = jnp.zeros_like(held)
+        sample = paired_rows(maps[0, 0:4], wts, cout).reshape(2 * width, cout)
+        sums[2:3] = jnp.sum(sample, axis=0, keepdims=True) / (2 * width)
 
     @pl.when(step > 0)
     def _():
         map_copy(step).wait()
 
+    up_copy(step).wait()
+    shift = sums[2:3]
     acc[...] += statistics(held[...])
     blank = jnp.zeros((1, width, cin), BF16)
     padded = jnp.concatenate([blank, maps[step], blank], axis=0)
     pre = paired_rows(padded, wts, cout)
     pre_out[step] = pre
     mid = pre[1 : rows - 1].reshape(inner, cout)
-    mean = jnp.sum(mid, axis=0, keepdims=True) / inner
-    shift = jnp.where(step == 0, mean, sums[2:3])
-    sums[2:3] = shift
     delta = mid - shift
-    up_copy(step).wait()
     up = ups[step, 1 : rows - 1].reshape(inner, cout)
     high, low = split(delta)
     held[:, :cout] = low
@@ -180,8 +180,16 @@
 
 
 def sides(ahead, across):
+    place = lax.axis_index("rows")
     even = is_even()
+    outermost = jnp.where(even, place == 0, place == lax.axis_size("rows") - 1)
+    across = jnp.where(outermost, jnp.zeros_like(across), across)
     return jnp.where(even, across, ahead), jnp.where(even, ahead, across)
+
+
+def edge_choice(first, final):
+    even = is_even()
+    return jnp.where(even, final, first), jnp.where(even, first, final)
 
 
 def fetch_kernel(images, kern, ahead, across, taps, maps, sems):
@@ -429,7 +437,7 @@
     up = jnp.concatenate([ups[:, 0], ups[:, last]], axis=0).reshape(2 * count * width, cout)
     grad = pre_gradient(*split(pre - paint_rows[0:1]), up, mats, paint_rows)
     shaped = grad.reshape(2 * count, width, cout)
-    edge_across[:, 0], edge_ahead[:, 0] = sides(shaped[count:], shaped[:count])
+    edge_ahead[:, 0], edge_across[:, 0] = edge_choice(shaped[:count], shaped[count:])
 
 
 def pre_gradient(big, small, up, mats, paint_rows):
@@ -782,12 +790,17 @@
 
 
 def halos(ahead, across):
-    count = lax.axis_size("rows")
-    pairs = []
-    for first in (0, 1):
-        found = [(i, i + 1) for i in range(first, count - 1, 2)]
-        pairs.append(found + [(i, j) for j, i in found])
-    return lax.ppermute(ahead, "rows", pairs[0]), lax.ppermute(across, "rows", pairs[1])
+    count, groups = lax.axis_size("rows"), lax.axis_size("dp")
+    offset = 2 if groups % 4 == 0 else 1 if groups % 2 == 0 else 0
+    pairs = ([], [])
+    for group in range(groups):
+        for place in range(count):
+            for first in (0, 1):
+                partner = place + 1 if place % 2 == first else place - 1
+                inside = 0 <= partner < count
+                other = (group, partner) if inside else (group ^ offset, place)
+                pairs[first].append((group * count + place, other[0] * count + other[1]))
+    return lax.ppermute(ahead, AXES, pairs[0]), lax.ppermute(across, AXES, pairs[1])
 
 
 def exchange(value, devices, stage):
@@ -817,7 +830,7 @@
     def summed(send, stage, many):
         first = state["next"]
         many = min(many, count - first)
-        if many < 1:
+        if many == 0:
             return exchange(send, devices, stage)
         state["next"] = first + many
         operands = (pre, low, high, upstream, images, top, bot, sums, *state["moments"])
@@ -826,10 +839,10 @@
         )
         return received
 
-    value = value + summed(send, plan[0], 0)
+    value = value + exchange(send, devices, plan[0])
     for stage in plan[1:]:
-        value = value + summed(value, stage, 2 if stage == plan[1] else 1)
-    received = summed(value, plan[0], 1)
+        value = value + summed(value, stage, 2 if stage in plan[2:4] else 1)
+    received = exchange(value, devices, plan[0])
     first = state["next"]
     if first < count:
         operands = (pre, low, high, upstream, images, top, bot, sums, *state["moments"])
@@ -852,7 +865,7 @@
         (kernel, low, high, upstream, mats, paint_rows),
     )
     state["next"] = 0
-    shares = [1, 2, 1, 1, 1]
+    shares = [1, 1, 1, 1, 2]
 
     def transfer(send, stage):
         first = state["next"]

time: 80.7 us -> 80.1 us (level)
  starting transfers between devices: 25.2 us -> 20.9 us
  waiting for transfers between devices: 12.4 us -> 16.7 us
    ppermute x15, starting transfers between devices: 22.6 us -> 16.7 us  [exchange(): return lax.ppermute(value, AXES, pairs)]
    ppermute x15, waiting for transfers between devices: 12.4 us -> 16.7 us  [exchange(): return lax.ppermute(value, AXES, pairs)]
    ppermute x4, starting transfers between devices: 2.59 us -> 4.21 us  [the longest x2 3.68 us: halos(): lax.ppermute(across, AXES, pairs[1])]
    pallas_call x5 -> x4, Pallas kernels: 9.96 us -> 9.19 us  [moments(): pl.pallas_call(functools.partial(moment_kernel, first, count), in_specs=[...]
  transfers between devices with their start and end apart: 19 -> 19, of which waited for: 13 -> 14; matrix products, arithmetic and copies ran while one was open for 0% -> 0% of each run, Pallas kernels for 43% -> 43%
where the time goes in v4:
time: 80.1 us; the launch traced here: 80 us
  Pallas kernels  41.3 us (52%)
  starting transfers between devices  20.9 us (26%)
  waiting for transfers between devices  16.7 us (21%)
  between operations  1 us (1%)
    ppermute x15, starting transfers between devices, exchange(): return lax.ppermute(value, AXES, pairs)  16.7 us
    ppermute x15, waiting for transfers between devices, exchange(): return lax.ppermute(value, AXES, pairs)  16.7 us
    pallas_call x4, Pallas kernels, moments(): pl.pallas_call(functools.partial(moment_kernel, first, count), in_specs=[...  9.19 us
    pallas_call x5, Pallas kernels, image_gradient(): pl.pallas_call(functools.partial(image_kernel, first), grid=(count,), in_...  9.1 us
    pallas_call x1, Pallas kernels, forward(): pl.pallas_call(forward_kernel, grid=(count,), in_specs=[resident(), space...  8.43 us
    ppermute x2, starting transfers between devices, halos(): lax.ppermute(across, AXES, pairs[1])  3.68 us
    pallas_call x1, Pallas kernels, painted(): pl.pallas_call(paint_kernel, grid=(count,), in_specs=[resident()] * 5, ou...  3.41 us
    pallas_call x1, Pallas kernels, whitened(): pl.pallas_call(functools.partial(whitening_kernel, total_pix, stage), in_...  3.23 us
  transfers between devices with their start and end apart: 19, of which 14 were waited for; matrix products, arithmetic and copies ran while one was open for 0% of the time, Pallas kernels for 43%

profile of v4, /device:TPU:0, one launch (start us, length us, event | category | flops | bytes accessed | tf_op | source)
XLA Modules:
  0.0 80.0 jit_solution(4950569387886973672)
XLA Ops:
  0.6 1.5 %edge_rows.1 = (bf16[6,1,128,256]{3,2,1,0:T(8,128)(2,1)S(1)}, bf16[6,1,128,256]{3,2,1,0:T(8,128)(2,1)S(1)}, bf16[3,3,256,128]{3,2,1,0:T(8,128)(2,1)S(1)}, bf16[6,8,128,256]{3,2,1,0:T(8,128)(2,1)S(1)}) custom-call(bf16[6,8,128,256]{3,2,1,0:T(8,128)(2,1)} %img.1, bf16[3,3,256,128]{3,2,1,0:T(8,128)(2,1)} %kern.1), custom_call_target="tpu_custom_call" | custom-call | tf_op jit(solution)/shard_map/edge_rows/pallas_call | solution.py:733
  2.7 2.6 %collective-permute-start.1 = (bf16[6,1,128,256]{3,2,1,0:T(8,128)(2,1)S(1)}, bf16[6,1,128,256]{3,2,1,0:T(8,128)(2,1)S(1)}, u32[]{:S(2)}, u32[]{:S(2)}) collective-permute-start(bf16[6,1,128,256]{3,2,1,0:T(8,128)(2,1)S(1)} %get-tuple-element.168), channel_id=1, source_target_pairs={{0,8},{1,2},{2,1},{3,11},{4,12},{5,6},{6,5},{7,15},{8,0},{9,10},{1... | collective-permute-start | bytes 1179656 | tf_op jit(solution)/shard_map/ppermute | solution.py:803
  5.3 8.4 %forward_inner.1 = (f32[6,8,128,128]{3,2,1,0:T(8,128)S(1)}, f32[256,256]{1,0:T(8,128)S(1)}, f32[8,128]{1,0:T(8,128)S(1)}, bf16[6,8,128,256]{3,2,1,0:T(8,128)(2,1)S(1)}, bf16[6,8,128,128]{3,2,1,0:T(8,128)(2,1)S(1)}) custom-call(bf16[6,8,128,256]{3,2,1,0:T(8,128)(2,1)S(1)} %get-tuple-element.169.first, ...), custom_call_target="tpu_custom_call", output_to_operand_aliasing={{3}: (0, {})} | custom-call | flops 3623878656 | bytes 7864320 | tf_op jit(solution)/shard_map/forward_inner/pallas_call | solution.py:548
  16.1 1.5 %collective-permute-start.3 = (f32[72,128]{1,0:T(8,128)S(1)}, f32[72,128]{1,0:T(8,128)S(1)}, u32[]{:S(2)}, u32[]{:S(2)}) collective-permute-start(f32[72,128]{1,0:T(8,128)S(1)} %add.21), channel_id=1, source_target_pairs={{0,4},{1,3},{2,6},{3,1},{4,0},{5,7},{6,2},{7,5},{8,12},{9,11},{10,... | collective-permute-start | bytes 110600 | tf_op jit(solution)/shard_map/ppermute | solution.py:808
  17.6 1.5 %moments.4 = (f32[768,768]{1,0:T(8,128)S(1)}, f32[768,128]{1,0:T(8,128)S(1)}) custom-call(f32[6,8,128,128]{3,2,1,0:T(8,128)S(1)} %get-tuple-element.272.pre.refs_0_, f32[6,1,128,128]{3,2,1,0:T(8,128)S(1)} %get-tuple-element.273.refs_1_.low, f32[6,1,128,128]{3,2,1,0:T(8,128)S(1)} %get-tuple-element.274.refs_2_.high, ...), custom_call_target="tpu_custom_call" | custom-call | flops 1207959552 | bytes 8388608 | tf_op jit(solution)/shard_map/moments/pallas_call | solution.py:597
  21.4 2.9 %moments.5 = (f32[768,768]{1,0:T(8,128)S(1)}, f32[768,128]{1,0:T(8,128)S(1)}) custom-call(f32[6,8,128,128]{3,2,1,0:T(8,128)S(1)} %get-tuple-element.272.pre.refs_0_, f32[6,1,128,128]{3,2,1,0:T(8,128)S(1)} %get-tuple-element.273.refs_1_.low, f32[6,1,128,128]{3,2,1,0:T(8,128)S(1)} %get-tuple-element.274.refs_2_.high, ...), custom_call_target="tpu_custom_call", output_to_operand_aliasing={{0}: (8, {}), {1}: (9, {})} | custom-call | flops 2415919104 | bytes 8388608 | tf_op jit(solution)/shard_map/moments/pallas_call | solution.py:597
  25.4 2.9 %moments.6 = (f32[768,768]{1,0:T(8,128)S(1)}, f32[768,128]{1,0:T(8,128)S(1)}) custom-call(f32[6,8,128,128]{3,2,1,0:T(8,128)S(1)} %get-tuple-element.272.pre.refs_0_, f32[6,1,128,128]{3,2,1,0:T(8,128)S(1)} %get-tuple-element.273.refs_1_.low, f32[6,1,128,128]{3,2,1,0:T(8,128)S(1)} %get-tuple-element.274.refs_2_.high, ...), custom_call_target="tpu_custom_call", output_to_operand_aliasing={{0}: (8, {}), {1}: (9, {})} | custom-call | flops 2415919104 | bytes 8388608 | tf_op jit(solution)/shard_map/moments/pallas_call | solution.py:597
  28.4 2.6 %collective-permute-start.6 = (f32[72,128]{1,0:T(8,128)S(1)}, f32[72,128]{1,0:T(8,128)S(1)}, u32[]{:S(2)}, u32[]{:S(2)}) collective-permute-start(f32[72,128]{1,0:T(8,128)S(1)} %add.24), channel_id=1, source_target_pairs={{0,16},{1,17},{2,18},{3,19},{4,20},{5,21},{6,22},{7,23},{8,24},{9,... | collective-permute-start | bytes 110600 | tf_op jit(solution)/shard_map/ppermute | solution.py:808
  31.1 1.8 %moments.7 = (f32[768,768]{1,0:T(8,128)S(1)}, f32[768,128]{1,0:T(8,128)S(1)}) custom-call(f32[6,8,128,128]{3,2,1,0:T(8,128)S(1)} %get-tuple-element.272.pre.refs_0_, f32[6,1,128,128]{3,2,1,0:T(8,128)S(1)} %get-tuple-element.273.refs_1_.low, f32[6,1,128,128]{3,2,1,0:T(8,128)S(1)} %get-tuple-element.274.refs_2_.high, ...), custom_call_target="tpu_custom_call", output_to_operand_aliasing={{0}: (8, {}), {1}: (9, {})} | custom-call | flops 1207959552 | bytes 8388608 | tf_op jit(solution)/shard_map/moments/pallas_call | solution.py:597
  34.6 3.2 %whitening.1 = (f32[1152,128]{1,0:T(8,128)S(1)}, f32[1152,128]{1,0:T(8,128)S(1)}, f32[2,64,64]{2,1,0:T(8,128)}, bf16[384,256]{1,0:T(8,128)(2,1)S(1)}, bf16[256,2...) custom-call(f32[72,128]{1,0:T(8,128)S(1)} %add.25.own, f32[72,128]{1,0:T(8,128)S(1)} %collective-permute-done.7.other, ...), custom_call_target="tpu_custom_call" | custom-call | flops 603979776 | bytes 8388608 | tf_op jit(solution)/shard_map/whitening/pallas_call | solution.py:626
  39.9 1.6 %collective-permute-start.9 = (f32[576,128]{1,0:T(8,128)S(1)}, f32[576,128]{1,0:T(8,128)S(1)}, u32[]{:S(2)}, u32[]{:S(2)}) collective-permute-start(f32[576,128]{1,0:T(8,128)S(1)} %get-tuple-element.261), channel_id=1, source_target_pairs={{0,4},{1,3},{2,6},{3,1},{4,0},{5,7},{6,2},{7,5},{8,12},{9,11},{10,... | collective-permute-start | bytes 884744 | tf_op jit(solution)/shard_map/ppermute | solution.py:808
  42.5 2.6 %pre_gradient.1.pre_grad = bf16[6,8,128,128]{3,2,1,0:T(8,128)(2,1)S(1)} custom-call(f32[6,8,128,128]{3,2,1,0:T(8,128)S(1)} %get-tuple-element.272.pre.refs_0_, f32[6,1,128,128]{3,2,1,0:T(8,128)S(1)} %get-tuple-element.273.refs_1_.low, f32[6,1,128,128]{3,2,1,0:T(8,128)S(1)} %get-tuple-element.274.refs_2_.high, ...), custom_call_target="tpu_custom_call" | custom-call | flops 1207959552 | bytes 6291456 | tf_op jit(solution)/shard_map/pre_gradient/pallas_call | solution.py:653
  45.1 1.6 %collective-permute-done.9.received = f32[576,128]{1,0:T(8,128)S(1)} collective-permute-done((f32[576,128]{1,0:T(8,128)S(1)}, f32[576,128]{1,0:T(8,128)S(1)}, u32[]{:S(2)}, u32[]{:S(2)}) %collective-permute-start.9) | collective-permute-done | bytes 294944 | tf_op jit(solution)/shard_map/ppermute | solution.py:808
  47.8 3.4 %colored.1 = bf16[6,8,128,128]{3,2,1,0:T(8,128)(2,1)} custom-call(f32[6,8,128,128]{3,2,1,0:T(8,128)S(1)} %get-tuple-element.272.pre.refs_0_, f32[6,1,128,128]{3,2,1,0:T(8,128)S(1)} %get-tuple-element.273.refs_1_.low, f32[6,1,128,128]{3,2,1,0:T(8,128)S(1)} %get-tuple-element.274.refs_2_.high, bf16[256,256]{1,0:T(8,128)(2,1)S(1)} %get-tuple-element.275.paint, ...), custom_call_target="tpu_custom_call" | custom-call | flops 805306368 | bytes 4718592 | tf_op jit(solution)/shard_map/colored/pallas_call | solution.py:671
  53.1 1.6 %image_gradient.5.rest_0_ = bf16[6,8,128,256]{3,2,1,0:T(8,128)(2,1)} custom-call(bf16[6,8,128,128]{3,2,1,0:T(8,128)(2,1)S(1)} %pre_gradient.1.pre_grad, bf16[6,1,128,128]{3,2,1,0:T(8,128)(2,1)S(1)} %collective-permute-done.11.ahead, bf16[6,1,128,128]{3,2,1,0:T(8,128)(2,1)S(1)} %collective-permute-done.12.across, bf16[1152,256]{1,0:T(8,128)(2,1)S(1)} %turned_weights.1.wts), custom_call_target="tpu_custom_call" | custom-call | flops 603979776 | bytes 786432 | tf_op jit(solution)/shard_map/image_gradient/pallas_call | solution.py:712
  54.7 1.7 %collective-permute-done.13 = f32[144,128]{1,0:T(8,128)S(1)} collective-permute-done((f32[144,128]{1,0:T(8,128)S(1)}, f32[144,128]{1,0:T(8,128)S(1)}, u32[]{:S(2)}, u32[]{:S(2)}) %collective-permute-start.13) | collective-permute-done | bytes 73760 | tf_op jit(solution)/shard_map/ppermute | solution.py:808
  56.4 3.2 %collective-permute-start.14 = (f32[144,128]{1,0:T(8,128)S(1)}, f32[144,128]{1,0:T(8,128)S(1)}, u32[]{:S(2)}, u32[]{:S(2)}) collective-permute-start(f32[144,128]{1,0:T(8,128)S(1)} %add.26), channel_id=1, source_target_pairs={{0,16},{1,17},{2,18},{3,19},{4,20},{5,21},{6,22},{7,23},{8,24},{9,... | collective-permute-start | bytes 221192 | tf_op jit(solution)/shard_map/ppermute | solution.py:808
  59.6 1.6 %image_gradient.6.rest_0_ = bf16[6,8,128,256]{3,2,1,0:T(8,128)(2,1)} custom-call(bf16[6,8,128,128]{3,2,1,0:T(8,128)(2,1)S(1)} %pre_gradient.1.pre_grad, bf16[6,1,128,128]{3,2,1,0:T(8,128)(2,1)S(1)} %collective-permute-done.11.ahead, bf16[6,1,128,128]{3,2,1,0:T(8,128)(2,1)S(1)} %collective-permute-done.12.across, ...), custom_call_target="tpu_custom_call", output_to_operand_aliasing={{}: (4, {})} | custom-call | flops 603979776 | bytes 786432 | tf_op jit(solution)/shard_map/image_gradient/pallas_call | solution.py:712
  61.3 1.5 %collective-permute-done.14 = f32[144,128]{1,0:T(8,128)S(1)} collective-permute-done((f32[144,128]{1,0:T(8,128)S(1)}, f32[144,128]{1,0:T(8,128)S(1)}, u32[]{:S(2)}, u32[]{:S(2)}) %collective-permute-start.14) | collective-permute-done | bytes 73760 | tf_op jit(solution)/shard_map/ppermute | solution.py:808
  63.6 1.6 %image_gradient.7.rest_0_ = bf16[6,8,128,256]{3,2,1,0:T(8,128)(2,1)} custom-call(bf16[6,8,128,128]{3,2,1,0:T(8,128)(2,1)S(1)} %pre_gradient.1.pre_grad, bf16[6,1,128,128]{3,2,1,0:T(8,128)(2,1)S(1)} %collective-permute-done.11.ahead, bf16[6,1,128,128]{3,2,1,0:T(8,128)(2,1)S(1)} %collective-permute-done.12.across, ...), custom_call_target="tpu_custom_call", output_to_operand_aliasing={{}: (4, {})} | custom-call | flops 603979776 | bytes 786432 | tf_op jit(solution)/shard_map/image_gradient/pallas_call | solution.py:712
  65.2 1.6 %collective-permute-done.15.received = bf16[144,128]{1,0:T(8,128)(2,1)S(1)} collective-permute-done((bf16[144,128]{1,0:T(8,128)(2,1)S(1)}, bf16[144,128]{1,0:T(8,128)(2,1)S(1)}, u32[]{:S(2)}, u32[]{:S(2)}) %collective-permute-start.15) | collective-permute-done | bytes 36896 | tf_op jit(solution)/shard_map/ppermute | solution.py:808
  67.7 1.6 %image_gradient.8.rest_0_ = bf16[6,8,128,256]{3,2,1,0:T(8,128)(2,1)} custom-call(bf16[6,8,128,128]{3,2,1,0:T(8,128)(2,1)S(1)} %pre_gradient.1.pre_grad, bf16[6,1,128,128]{3,2,1,0:T(8,128)(2,1)S(1)} %collective-permute-done.11.ahead, bf16[6,1,128,128]{3,2,1,0:T(8,128)(2,1)S(1)} %collective-permute-done.12.across, ...), custom_call_target="tpu_custom_call", output_to_operand_aliasing={{}: (4, {})} | custom-call | flops 603979776 | bytes 786432 | tf_op jit(solution)/shard_map/image_gradient/pallas_call | solution.py:712
  69.3 2.7 %collective-permute-done.16.received = bf16[288,128]{1,0:T(8,128)(2,1)S(1)} collective-permute-done((bf16[288,128]{1,0:T(8,128)(2,1)S(1)}, bf16[288,128]{1,0:T(8,128)(2,1)S(1)}, u32[]{:S(2)}, u32[]{:S(2)}) %collective-permute-start.16) | collective-permute-done | bytes 73760 | tf_op jit(solution)/shard_map/ppermute | solution.py:808
  73.4 2.5 %image_gradient.9 = bf16[6,8,128,256]{3,2,1,0:T(8,128)(2,1)} custom-call(bf16[6,8,128,128]{3,2,1,0:T(8,128)(2,1)S(1)} %pre_gradient.1.pre_grad, bf16[6,1,128,128]{3,2,1,0:T(8,128)(2,1)S(1)} %collective-permute-done.11.ahead, bf16[6,1,128,128]{3,2,1,0:T(8,128)(2,1)S(1)} %collective-permute-done.12.across, ...), custom_call_target="tpu_custom_call", output_to_operand_aliasing={{}: (4, {})} | custom-call | flops 1207959552 | bytes 1572864 | tf_op jit(solution)/shard_map/image_gradient/pallas_call | solution.py:712
  (50 shorter events, 21.0 us)
Async XLA Ops:
  2.1 11.6 %collective-permute-start = (bf16[6,1,128,256]{3,2,1,0:T(8,128)(2,1)S(1)}, bf16[6,1,128,256]{3,2,1,0:T(8,128)(2,1)S(1)}, u32[]{:S(2)}, u32[]{:S(2)}) collective-permute-start(bf16[6,1,128,256]{3,2,1,0:T(8,128)(2,1)S(1)} %get-tuple-element.167), channel_id=1, source_target_pairs={{0,1},{1,0},{2,3},{3,2},{4,5},{5,4},{6,7},{7,6},{8,9},{9,8},{10,11... | collective-permute-start | bytes 1179656 | tf_op jit(solution)/shard_map/ppermute | solution.py:803
  2.7 11.1 %collective-permute-start.1 = (bf16[6,1,128,256]{3,2,1,0:T(8,128)(2,1)S(1)}, bf16[6,1,128,256]{3,2,1,0:T(8,128)(2,1)S(1)}, u32[]{:S(2)}, u32[]{:S(2)}) collective-permute-start(bf16[6,1,128,256]{3,2,1,0:T(8,128)(2,1)S(1)} %get-tuple-element.168), channel_id=1, source_target_pairs={{0,8},{1,2},{2,1},{3,11},{4,12},{5,6},{6,5},{7,15},{8,0},{9,10},{1... | collective-permute-start | bytes 1179656 | tf_op jit(solution)/shard_map/ppermute | solution.py:803
  14.9 1.3 %collective-permute-start.2 = (f32[72,128]{1,0:T(8,128)S(1)}, f32[72,128]{1,0:T(8,128)S(1)}, u32[]{:S(2)}, u32[]{:S(2)}) collective-permute-start(f32[72,128]{1,0:T(8,128)S(1)} %get-tuple-element.176), channel_id=1, source_target_pairs={{0,1},{1,0},{2,3},{3,2},{4,5},{5,4},{6,7},{7,6},{8,9},{9,8},{10,11... | collective-permute-start | bytes 110600 | tf_op jit(solution)/shard_map/ppermute | solution.py:808
  16.1 4.0 %collective-permute-start.3 = (f32[72,128]{1,0:T(8,128)S(1)}, f32[72,128]{1,0:T(8,128)S(1)}, u32[]{:S(2)}, u32[]{:S(2)}) collective-permute-start(f32[72,128]{1,0:T(8,128)S(1)} %add.21), channel_id=1, source_target_pairs={{0,4},{1,3},{2,6},{3,1},{4,0},{5,7},{6,2},{7,5},{8,12},{9,11},{10,... | collective-permute-start | bytes 110600 | tf_op jit(solution)/shard_map/ppermute | solution.py:808
  20.1 4.3 %collective-permute-start.4 = (f32[72,128]{1,0:T(8,128)S(1)}, f32[72,128]{1,0:T(8,128)S(1)}, u32[]{:S(2)}, u32[]{:S(2)}) collective-permute-start(f32[72,128]{1,0:T(8,128)S(1)} %add.22), channel_id=1, source_target_pairs={{0,2},{1,5},{2,0},{3,7},{4,6},{5,1},{6,4},{7,3},{8,10},{9,13},{10,... | collective-permute-start | bytes 110600 | tf_op jit(solution)/shard_map/ppermute | solution.py:808
  24.4 4.0 %collective-permute-start.5 = (f32[72,128]{1,0:T(8,128)S(1)}, f32[72,128]{1,0:T(8,128)S(1)}, u32[]{:S(2)}, u32[]{:S(2)}) collective-permute-start(f32[72,128]{1,0:T(8,128)S(1)} %add.23), channel_id=1, source_target_pairs={{0,8},{1,9},{2,10},{3,11},{4,12},{5,13},{6,14},{7,15},{8,0},{9,1},... | collective-permute-start | bytes 110600 | tf_op jit(solution)/shard_map/ppermute | solution.py:808
  28.4 6.2 %copy-start = (f32[2,64,64]{2,1,0:T(8,128)S(1)}, f32[2,64,64]{2,1,0:T(8,128)}, u32[]{:S(2)}) copy-start(f32[2,64,64]{2,1,0:T(8,128)} %colors.1) | copy-start | bytes 98308
  28.4 6.2 %copy-start.1 = (f32[128]{0:T(128)S(1)}, f32[128]{0:T(128)}, u32[]{:S(2)}) copy-start(f32[128]{0:T(128)} %param.8) | copy-start | bytes 1540
  28.4 4.9 %collective-permute-start.6 = (f32[72,128]{1,0:T(8,128)S(1)}, f32[72,128]{1,0:T(8,128)S(1)}, u32[]{:S(2)}, u32[]{:S(2)}) collective-permute-start(f32[72,128]{1,0:T(8,128)S(1)} %add.24), channel_id=1, source_target_pairs={{0,16},{1,17},{2,18},{3,19},{4,20},{5,21},{6,22},{7,23},{8,24},{9,... | collective-permute-start | bytes 110600 | tf_op jit(solution)/shard_map/ppermute | solution.py:808
  33.4 1.2 %collective-permute-start.7 = (f32[72,128]{1,0:T(8,128)S(1)}, f32[72,128]{1,0:T(8,128)S(1)}, u32[]{:S(2)}, u32[]{:S(2)}) collective-permute-start(f32[72,128]{1,0:T(8,128)S(1)} %add.25.own), channel_id=1, source_target_pairs={{0,1},{1,0},{2,3},{3,2},{4,5},{5,4},{6,7},{7,6},{8,9},{9,8},{10,11... | collective-permute-start | bytes 110600 | tf_op jit(solution)/shard_map/ppermute | solution.py:808
  37.8 2.0 %collective-permute-start.8 = (f32[1152,128]{1,0:T(8,128)S(1)}, f32[1152,128]{1,0:T(8,128)S(1)}, u32[]{:S(2)}, u32[]{:S(2)}) collective-permute-start(f32[1152,128]{1,0:T(8,128)S(1)} %get-tuple-element.246), channel_id=1, source_target_pairs={{0,1},{1,0},{2,3},{3,2},{4,5},{5,4},{6,7},{7,6},{8,9},{9,8},{10,11... | collective-permute-start | bytes 1769480 | tf_op jit(solution)/shard_map/ppermute | solution.py:808
  39.9 6.8 %collective-permute-start.9 = (f32[576,128]{1,0:T(8,128)S(1)}, f32[576,128]{1,0:T(8,128)S(1)}, u32[]{:S(2)}, u32[]{:S(2)}) collective-permute-start(f32[576,128]{1,0:T(8,128)S(1)} %get-tuple-element.261), channel_id=1, source_target_pairs={{0,4},{1,3},{2,6},{3,1},{4,0},{5,7},{6,2},{7,5},{8,12},{9,11},{10,... | collective-permute-start | bytes 884744 | tf_op jit(solution)/shard_map/ppermute | solution.py:808
  41.5 10.5 %collective-permute-start.11 = (bf16[6,1,128,128]{3,2,1,0:T(8,128)(2,1)S(1)}, bf16[6,1,128,128]{3,2,1,0:T(8,128)(2,1)S(1)}, u32[]{:S(2)}, u32[]{:S(2)}) collective-permute-start(bf16[6,1,128,128]{3,2,1,0:T(8,128)(2,1)S(1)} %get-tuple-element.283), channel_id=1, source_target_pairs={{0,1},{1,0},{2,3},{3,2},{4,5},{5,4},{6,7},{7,6},{8,9},{9,8},{10,11... | collective-permute-start | bytes 589832 | tf_op jit(solution)/shard_map/ppermute | solution.py:803
  41.5 10.5 %collective-permute-start.12 = (bf16[6,1,128,128]{3,2,1,0:T(8,128)(2,1)S(1)}, bf16[6,1,128,128]{3,2,1,0:T(8,128)(2,1)S(1)}, u32[]{:S(2)}, u32[]{:S(2)}) collective-permute-start(bf16[6,1,128,128]{3,2,1,0:T(8,128)(2,1)S(1)} %get-tuple-element.284), channel_id=1, source_target_pairs={{0,8},{1,2},{2,1},{3,11},{4,12},{5,6},{6,5},{7,15},{8,0},{9,10},{1... | collective-permute-start | bytes 589832 | tf_op jit(solution)/shard_map/ppermute | solution.py:803
  46.7 5.2 %collective-permute-start.10 = (f32[288,128]{1,0:T(8,128)S(1)}, f32[288,128]{1,0:T(8,128)S(1)}, u32[]{:S(2)}, u32[]{:S(2)}) collective-permute-start(f32[288,128]{1,0:T(8,128)S(1)} %get-tuple-element.271), channel_id=1, source_target_pairs={{0,2},{1,5},{2,0},{3,7},{4,6},{5,1},{6,4},{7,3},{8,10},{9,13},{10,... | collective-permute-start | bytes 442376 | tf_op jit(solution)/shard_map/ppermute | solution.py:808
  52.0 4.4 %collective-permute-start.13 = (f32[144,128]{1,0:T(8,128)S(1)}, f32[144,128]{1,0:T(8,128)S(1)}, u32[]{:S(2)}, u32[]{:S(2)}) collective-permute-start(f32[144,128]{1,0:T(8,128)S(1)} %get-tuple-element.286), channel_id=1, source_target_pairs={{0,8},{1,9},{2,10},{3,11},{4,12},{5,13},{6,14},{7,15},{8,0},{9,1},... | collective-permute-start | bytes 221192 | tf_op jit(solution)/shard_map/ppermute | solution.py:808
  56.4 6.3 %collective-permute-start.14 = (f32[144,128]{1,0:T(8,128)S(1)}, f32[144,128]{1,0:T(8,128)S(1)}, u32[]{:S(2)}, u32[]{:S(2)}) collective-permute-start(f32[144,128]{1,0:T(8,128)S(1)} %add.26), channel_id=1, source_target_pairs={{0,16},{1,17},{2,18},{3,19},{4,20},{5,21},{6,22},{7,23},{8,24},{9,... | collective-permute-start | bytes 221192 | tf_op jit(solution)/shard_map/ppermute | solution.py:808
  62.8 4.0 %collective-permute-start.15 = (bf16[144,128]{1,0:T(8,128)(2,1)S(1)}, bf16[144,128]{1,0:T(8,128)(2,1)S(1)}, u32[]{:S(2)}, u32[]{:S(2)}) collective-permute-start(bf16[144,128]{1,0:T(8,128)(2,1)S(1)} %add_convert_fusion.value), channel_id=1, source_target_pairs={{0,8},{1,9},{2,10},{3,11},{4,12},{5,13},{6,14},{7,15},{8,0},{9,1},... | collective-permute-start | bytes 110600 | tf_op jit(solution)/shard_map/ppermute | solution.py:808
  66.8 5.2 %collective-permute-start.16 = (bf16[288,128]{1,0:T(8,128)(2,1)S(1)}, bf16[288,128]{1,0:T(8,128)(2,1)S(1)}, u32[]{:S(2)}, u32[]{:S(2)}) collective-permute-start(bf16[288,128]{1,0:T(8,128)(2,1)S(1)} %join.3.value), channel_id=1, source_target_pairs={{0,2},{1,5},{2,0},{3,7},{4,6},{5,1},{6,4},{7,3},{8,10},{9,13},{10,... | collective-permute-start | bytes 221192 | tf_op jit(solution)/shard_map/ppermute | solution.py:808
  72.0 5.2 %collective-permute-start.17 = (bf16[576,128]{1,0:T(8,128)(2,1)S(1)}, bf16[576,128]{1,0:T(8,128)(2,1)S(1)}, u32[]{:S(2)}, u32[]{:S(2)}) collective-permute-start(bf16[576,128]{1,0:T(8,128)(2,1)S(1)} %join.4.value), channel_id=1, source_target_pairs={{0,4},{1,3},{2,6},{3,1},{4,0},{5,7},{6,2},{7,5},{8,12},{9,11},{10,... | collective-permute-start | bytes 442376 | tf_op jit(solution)/shard_map/ppermute | solution.py:808
  77.3 1.6 %collective-permute-start.18 = (bf16[1152,128]{1,0:T(8,128)(2,1)S(1)}, bf16[1152,128]{1,0:T(8,128)(2,1)S(1)}, u32[]{:S(2)}, u32[]{:S(2)}) collective-permute-start(bf16[1152,128]{1,0:T(8,128)(2,1)S(1)} %join.5.value), channel_id=1, source_target_pairs={{0,1},{1,0},{2,3},{3,2},{4,5},{5,4},{6,7},{7,6},{8,9},{9,8},{10,11... | collective-permute-start | bytes 884744 | tf_op jit(solution)/shard_map/ppermute | solution.py:808

commit v5 on v4

--- a/solution.py
+++ b/solution.py
@@ -112,13 +112,14 @@
     )
 
 
-def statistics(held):
-    third = held.shape[1] // 3
-    return dot(held[:, third:], held[:, : 2 * third], ((0,), (0,)))
+def statistics(low, high, up):
+    return dot(
+        jnp.concatenate([high, up], axis=1), jnp.concatenate([low, high], axis=1), ((0,), (0,))
+    )
 
 
 def forward_kernel(
-    first, img, kern, upstream, pre_out, acc, sums, maps, ups, wts, held, map_sems, up_sems
+    many, first, img, kern, upstream, pre_out, acc, sums, maps, ups, wts, held, map_sems, up_sems
 ):
     step = pl.program_id(0)
     last = pl.num_programs(0) - 1
@@ -132,11 +133,41 @@
     def up_copy(image):
         return pltpu.make_async_copy(upstream.at[image], ups.at[image], up_sems.at[image])
 
+    def gather(group):
+        grams, totals = [], []
+        for index in range(many):
+            up = ups[group * many + index, 1 : rows - 1].reshape(inner, cout)
+            grams.append(statistics(held[index, 0], held[index, 1], up))
+            totals.append(jnp.sum(up.astype(F32), axis=0, keepdims=True))
+        acc[...] += functools.reduce(jnp.add, grams)
+        sums[1:2] += functools.reduce(jnp.add, totals)
+
+    def convolve():
+        blank = jnp.zeros((1, width, cin), BF16)
+        shift = sums[2:3]
+        moved = []
+        for index in range(many):
+            image = step * many + index
+            padded = jnp.concatenate([blank, maps[image], blank], axis=0)
+            pre = paired_rows(padded, wts, cout)
+            pre_out[image] = pre
+            mid = pre[1 : rows - 1].reshape(inner, cout)
+            if index == 0:
+                mean = jnp.sum(mid, axis=0, keepdims=True) / inner
+                shift = jnp.where(step == 0, mean, shift)
+                sums[2:3] = shift
+            delta = mid - shift
+            high, low = split(delta)
+            held[index, 0] = low
+            held[index, 1] = high
+            moved.append(jnp.sum(delta, axis=0, keepdims=True))
+        sums[0:1] += functools.reduce(jnp.add, moved)
+
     @pl.when(step == 0)
     def _():
-        up_copy(0).start()
-        for image in range(1, count):
-            map_copy(image).start()
+        for image in range(count):
+            if image >= many:
+                map_copy(image).start()
             up_copy(image).start()
         blank = jnp.zeros((cin, cout), BF16)
         blocks = [(kern[a, 0], kern[a, 1]) for a in range(3)]
@@ -149,34 +180,21 @@
             wts[index * cin : (index + 1) * cin, cout:] = two
         acc[...] = jnp.zeros_like(acc)
         sums[...] = jnp.zeros_like(sums)
-        held[...] = jnp.zeros_like(held)
-        sample = paired_rows(maps[0, 0:4], wts, cout).reshape(2 * width, cout)
-        sums[2:3] = jnp.sum(sample, axis=0, keepdims=True) / (2 * width)
+        convolve()
 
     @pl.when(step > 0)
     def _():
-        map_copy(step).wait()
-
-    up_copy(step).wait()
-    shift = sums[2:3]
-    acc[...] += statistics(held[...])
-    blank = jnp.zeros((1, width, cin), BF16)
-    padded = jnp.concatenate([blank, maps[step], blank], axis=0)
-    pre = paired_rows(padded, wts, cout)
-    pre_out[step] = pre
-    mid = pre[1 : rows - 1].reshape(inner, cout)
-    delta = mid - shift
-    up = ups[step, 1 : rows - 1].reshape(inner, cout)
-    high, low = split(delta)
-    held[:, :cout] = low
-    held[:, cout : 2 * cout] = high
-    held[:, 2 * cout :] = up
-    sums[0:1] += jnp.sum(delta, axis=0, keepdims=True)
-    sums[1:2] += jnp.sum(up.astype(F32), axis=0, keepdims=True)
+        for index in range(many):
+            map_copy(step * many + index).wait()
+            up_copy((step - 1) * many + index).wait()
+        gather(step - 1)
+        convolve()
 
     @pl.when(step == last)
     def _():
-        acc[...] += statistics(held[...])
+        for index in range(many):
+            up_copy(step * many + index).wait()
+        gather(step)
 
 
 def sides(ahead, across):
@@ -192,14 +210,14 @@
     return jnp.where(even, final, first), jnp.where(even, first, final)
 
 
-def fetch_kernel(images, kern, ahead, across, taps, maps, sems):
+def fetch_kernel(many, images, kern, ahead, across, taps, maps, sems):
     last = images.shape[1] - 1
     even = is_even()
     pairs = (
         (images.at[:, pl.ds(jnp.where(even, last, 0), 1)], ahead),
         (images.at[:, pl.ds(jnp.where(even, 0, last), 1)], across),
         (kern, taps),
-        (images.at[0], maps.at[0]),
+        (images.at[:many], maps.at[:many]),
     )
     copies = [
         pltpu.make_async_copy(source, target, sems.at[index])
@@ -230,7 +248,7 @@
         [ups[:, 0].reshape(pixels, cout), ups[:, last].reshape(pixels, cout)], axis=0
     )
     big, small = split(delta)
-    gram = acc[...] + statistics(jnp.concatenate([small, big, up], axis=1))
+    gram = acc[...] + statistics(small, big, up)
     moved = sums[0:1] + jnp.sum(delta, axis=0, keepdims=True)
     up_sum = sums[1:2] + jnp.sum(up.astype(F32), axis=0, keepdims=True)
     mixed = gram[:cout, :cout]
@@ -537,6 +555,7 @@
 def forward(first, images, taps, upstream):
     count, rows, width, cin = images.shape
     cout = taps.shape[3]
+    many = images_per_step(count)
     shapes = [
         ((count, rows, width, cout), F32),
         ((2 * cout, 2 * cout), F32),
@@ -546,19 +565,19 @@
     ]
     space = pl.BlockSpec(memory_space=pltpu.HBM)
     return pl.pallas_call(
-        forward_kernel,
-        grid=(count,),
+        functools.partial(forward_kernel, many),
+        grid=(count // many,),
         in_specs=[resident(), space, resident(), space],
         out_specs=[resident()] * len(shapes),
         out_shape=[jax.ShapeDtypeStruct(shape, dtype) for shape, dtype in shapes],
         scratch_shapes=[
             pltpu.VMEM((10 * cin, 2 * cout), BF16),
-            pltpu.VMEM(((rows - 2) * width, 3 * cout), BF16),
+            pltpu.VMEM((many, 2, (rows - 2) * width, cout), BF16),
             pltpu.SemaphoreType.DMA((count,)),
             pltpu.SemaphoreType.DMA((count,)),
         ],
         input_output_aliases={0: 3},
-        compiler_params=pltpu.CompilerParams(vmem_limit_bytes=20 * MIB),
+        compiler_params=pltpu.CompilerParams(vmem_limit_bytes=28 * MIB),
         cost_estimate=pl.CostEstimate(
             flops=2 * count * rows * width * 9 * cin * cout,
             bytes_accessed=2 * images.size + 2 * upstream.size + 4 * upstream.size,
@@ -726,12 +745,16 @@
     )(*operands)
 
 
+def images_per_step(count):
+    return 2 if count % 2 == 0 else 1
+
+
 def fetched(images, kernel):
     count, rows, width, cin = images.shape
     edge = (count, 1, width, cin)
     space = pl.BlockSpec(memory_space=pltpu.HBM)
     return pl.pallas_call(
-        fetch_kernel,
+        functools.partial(fetch_kernel, images_per_step(count)),
         in_specs=[space, space],
         out_specs=[resident()] * 4,
         out_shape=[

time: 80.1 us -> 78.1 us (0.975)
  Pallas kernels: 41.3 us -> 39.2 us
    pallas_call x2, Pallas kernels: 9.93 us -> 7.91 us  [the longest x1 6.22 us: forward(): pl.pallas_call(functools.partial(forward_kernel, many), grid=(count // ma...]
  transfers between devices with their start and end apart: 19 -> 19, of which waited for: 14 -> 13; matrix products, arithmetic and copies ran while one was open for 0% -> 0% of each run, Pallas kernels for 43% -> 41%
where the time goes in v5:
time: 78.1 us; the launch traced here: 78 us
  Pallas kernels  39.2 us (50%)
  starting transfers between devices  20.9 us (27%)
  waiting for transfers between devices  16.7 us (21%)
  between operations  1.04 us (1%)
    ppermute x15, waiting for transfers between devices, exchange(): return lax.ppermute(value, AXES, pairs)  16.7 us
    ppermute x15, starting transfers between devices, exchange(): return lax.ppermute(value, AXES, pairs)  16.7 us
    pallas_call x4, Pallas kernels, moments(): pl.pallas_call(functools.partial(moment_kernel, first, count), in_specs=[...  9.19 us
    pallas_call x5, Pallas kernels, image_gradient(): pl.pallas_call(functools.partial(image_kernel, first), grid=(count,), in_...  9.09 us
    pallas_call x1, Pallas kernels, forward(): pl.pallas_call(functools.partial(forward_kernel, many), grid=(count // ma...  6.22 us
    ppermute x2, starting transfers between devices, halos(): lax.ppermute(across, AXES, pairs[1])  3.64 us
    pallas_call x1, Pallas kernels, painted(): pl.pallas_call(paint_kernel, grid=(count,), in_specs=[resident()] * 5, ou...  3.4 us
    pallas_call x1, Pallas kernels, whitened(): pl.pallas_call(functools.partial(whitening_kernel, total_pix, stage), in_...  3.23 us
  transfers between devices with their start and end apart: 19, of which 13 were waited for; matrix products, arithmetic and copies ran while one was open for 0% of the time, Pallas kernels for 41%

profile of v5, /device:TPU:0, one launch (start us, length us, event | category | flops | bytes accessed | tf_op | source)
XLA Modules:
  0.0 78.0 jit_solution(16321007790323360032)
XLA Ops:
  0.6 1.7 %edge_rows.1 = (bf16[6,1,128,256]{3,2,1,0:T(8,128)(2,1)S(1)}, bf16[6,1,128,256]{3,2,1,0:T(8,128)(2,1)S(1)}, bf16[3,3,256,128]{3,2,1,0:T(8,128)(2,1)S(1)}, bf16[6,8,128,256]{3,2,1,0:T(8,128)(2,1)S(1)}) custom-call(bf16[6,8,128,256]{3,2,1,0:T(8,128)(2,1)} %img.1, bf16[3,3,256,128]{3,2,1,0:T(8,128)(2,1)} %kern.1), custom_call_target="tpu_custom_call" | custom-call | tf_op jit(solution)/shard_map/edge_rows/pallas_call | solution.py:756
  2.9 2.6 %collective-permute-start.1 = (bf16[6,1,128,256]{3,2,1,0:T(8,128)(2,1)S(1)}, bf16[6,1,128,256]{3,2,1,0:T(8,128)(2,1)S(1)}, u32[]{:S(2)}, u32[]{:S(2)}) collective-permute-start(bf16[6,1,128,256]{3,2,1,0:T(8,128)(2,1)S(1)} %get-tuple-element.168), channel_id=1, source_target_pairs={{0,8},{1,2},{2,1},{3,11},{4,12},{5,6},{6,5},{7,15},{8,0},{9,10},{1... | collective-permute-start | bytes 1179656 | tf_op jit(solution)/shard_map/ppermute | solution.py:826
  5.5 6.2 %forward_inner.1 = (f32[6,8,128,128]{3,2,1,0:T(8,128)S(1)}, f32[256,256]{1,0:T(8,128)S(1)}, f32[8,128]{1,0:T(8,128)S(1)}, bf16[6,8,128,256]{3,2,1,0:T(8,128)(2,1)S(1)}, bf16[6,8,128,128]{3,2,1,0:T(8,128)(2,1)S(1)}) custom-call(bf16[6,8,128,256]{3,2,1,0:T(8,128)(2,1)S(1)} %get-tuple-element.169.first, ...), custom_call_target="tpu_custom_call", output_to_operand_aliasing={{3}: (0, {})} | custom-call | flops 3623878656 | bytes 7864320 | tf_op jit(solution)/shard_map/forward_inner/pallas_call | solution.py:567
  14.1 1.5 %collective-permute-start.3 = (f32[72,128]{1,0:T(8,128)S(1)}, f32[72,128]{1,0:T(8,128)S(1)}, u32[]{:S(2)}, u32[]{:S(2)}) collective-permute-start(f32[72,128]{1,0:T(8,128)S(1)} %add.21), channel_id=1, source_target_pairs={{0,4},{1,3},{2,6},{3,1},{4,0},{5,7},{6,2},{7,5},{8,12},{9,11},{10,... | collective-permute-start | bytes 110600 | tf_op jit(solution)/shard_map/ppermute | solution.py:831
  19.4 2.9 %moments.5 = (f32[768,768]{1,0:T(8,128)S(1)}, f32[768,128]{1,0:T(8,128)S(1)}) custom-call(f32[6,8,128,128]{3,2,1,0:T(8,128)S(1)} %get-tuple-element.272.pre.refs_0_, f32[6,1,128,128]{3,2,1,0:T(8,128)S(1)} %get-tuple-element.273.refs_1_.low, f32[6,1,128,128]{3,2,1,0:T(8,128)S(1)} %get-tuple-element.274.refs_2_.high, ...), custom_call_target="tpu_custom_call", output_to_operand_aliasing={{0}: (8, {}), {1}: (9, {})} | custom-call | flops 2415919104 | bytes 8388608 | tf_op jit(solution)/shard_map/moments/pallas_call | solution.py:616
  23.6 2.9 %moments.6 = (f32[768,768]{1,0:T(8,128)S(1)}, f32[768,128]{1,0:T(8,128)S(1)}) custom-call(f32[6,8,128,128]{3,2,1,0:T(8,128)S(1)} %get-tuple-element.272.pre.refs_0_, f32[6,1,128,128]{3,2,1,0:T(8,128)S(1)} %get-tuple-element.273.refs_1_.low, f32[6,1,128,128]{3,2,1,0:T(8,128)S(1)} %get-tuple-element.274.refs_2_.high, ...), custom_call_target="tpu_custom_call", output_to_operand_aliasing={{0}: (8, {}), {1}: (9, {})} | custom-call | flops 2415919104 | bytes 8388608 | tf_op jit(solution)/shard_map/moments/pallas_call | solution.py:616
  26.6 2.7 %collective-permute-start.6 = (f32[72,128]{1,0:T(8,128)S(1)}, f32[72,128]{1,0:T(8,128)S(1)}, u32[]{:S(2)}, u32[]{:S(2)}) collective-permute-start(f32[72,128]{1,0:T(8,128)S(1)} %add.24), channel_id=1, source_target_pairs={{0,16},{1,17},{2,18},{3,19},{4,20},{5,21},{6,22},{7,23},{8,24},{9,... | collective-permute-start | bytes 110600 | tf_op jit(solution)/shard_map/ppermute | solution.py:831
  29.3 1.9 %moments.7 = (f32[768,768]{1,0:T(8,128)S(1)}, f32[768,128]{1,0:T(8,128)S(1)}) custom-call(f32[6,8,128,128]{3,2,1,0:T(8,128)S(1)} %get-tuple-element.272.pre.refs_0_, f32[6,1,128,128]{3,2,1,0:T(8,128)S(1)} %get-tuple-element.273.refs_1_.low, f32[6,1,128,128]{3,2,1,0:T(8,128)S(1)} %get-tuple-element.274.refs_2_.high, ...), custom_call_target="tpu_custom_call", output_to_operand_aliasing={{0}: (8, {}), {1}: (9, {})} | custom-call | flops 1207959552 | bytes 8388608 | tf_op jit(solution)/shard_map/moments/pallas_call | solution.py:616
  32.8 3.2 %whitening.1 = (f32[1152,128]{1,0:T(8,128)S(1)}, f32[1152,128]{1,0:T(8,128)S(1)}, f32[2,64,64]{2,1,0:T(8,128)}, bf16[384,256]{1,0:T(8,128)(2,1)S(1)}, bf16[256,2...) custom-call(f32[72,128]{1,0:T(8,128)S(1)} %add.25.own, f32[72,128]{1,0:T(8,128)S(1)} %collective-permute-done.7.other, ...), custom_call_target="tpu_custom_call" | custom-call | flops 603979776 | bytes 8388608 | tf_op jit(solution)/shard_map/whitening/pallas_call | solution.py:645
  38.1 1.6 %collective-permute-start.9 = (f32[576,128]{1,0:T(8,128)S(1)}, f32[576,128]{1,0:T(8,128)S(1)}, u32[]{:S(2)}, u32[]{:S(2)}) collective-permute-start(f32[576,128]{1,0:T(8,128)S(1)} %get-tuple-element.261), channel_id=1, source_target_pairs={{0,4},{1,3},{2,6},{3,1},{4,0},{5,7},{6,2},{7,5},{8,12},{9,11},{10,... | collective-permute-start | bytes 884744 | tf_op jit(solution)/shard_map/ppermute | solution.py:831
  40.6 2.6 %pre_gradient.1.pre_grad = bf16[6,8,128,128]{3,2,1,0:T(8,128)(2,1)S(1)} custom-call(f32[6,8,128,128]{3,2,1,0:T(8,128)S(1)} %get-tuple-element.272.pre.refs_0_, f32[6,1,128,128]{3,2,1,0:T(8,128)S(1)} %get-tuple-element.273.refs_1_.low, f32[6,1,128,128]{3,2,1,0:T(8,128)S(1)} %get-tuple-element.274.refs_2_.high, ...), custom_call_target="tpu_custom_call" | custom-call | flops 1207959552 | bytes 6291456 | tf_op jit(solution)/shard_map/pre_gradient/pallas_call | solution.py:672
  43.2 1.6 %collective-permute-done.9.received = f32[576,128]{1,0:T(8,128)S(1)} collective-permute-done((f32[576,128]{1,0:T(8,128)S(1)}, f32[576,128]{1,0:T(8,128)S(1)}, u32[]{:S(2)}, u32[]{:S(2)}) %collective-permute-start.9) | collective-permute-done | bytes 294944 | tf_op jit(solution)/shard_map/ppermute | solution.py:831
  46.0 3.4 %colored.1 = bf16[6,8,128,128]{3,2,1,0:T(8,128)(2,1)} custom-call(f32[6,8,128,128]{3,2,1,0:T(8,128)S(1)} %get-tuple-element.272.pre.refs_0_, f32[6,1,128,128]{3,2,1,0:T(8,128)S(1)} %get-tuple-element.273.refs_1_.low, f32[6,1,128,128]{3,2,1,0:T(8,128)S(1)} %get-tuple-element.274.refs_2_.high, bf16[256,256]{1,0:T(8,128)(2,1)S(1)} %get-tuple-element.275.paint, ...), custom_call_target="tpu_custom_call" | custom-call | flops 805306368 | bytes 4718592 | tf_op jit(solution)/shard_map/colored/pallas_call | solution.py:690
  51.2 1.6 %image_gradient.5.rest_0_ = bf16[6,8,128,256]{3,2,1,0:T(8,128)(2,1)} custom-call(bf16[6,8,128,128]{3,2,1,0:T(8,128)(2,1)S(1)} %pre_gradient.1.pre_grad, bf16[6,1,128,128]{3,2,1,0:T(8,128)(2,1)S(1)} %collective-permute-done.11.ahead, bf16[6,1,128,128]{3,2,1,0:T(8,128)(2,1)S(1)} %collective-permute-done.12.across, bf16[1152,256]{1,0:T(8,128)(2,1)S(1)} %turned_weights.1.wts), custom_call_target="tpu_custom_call" | custom-call | flops 603979776 | bytes 786432 | tf_op jit(solution)/shard_map/image_gradient/pallas_call | solution.py:731
  52.9 1.7 %collective-permute-done.13 = f32[144,128]{1,0:T(8,128)S(1)} collective-permute-done((f32[144,128]{1,0:T(8,128)S(1)}, f32[144,128]{1,0:T(8,128)S(1)}, u32[]{:S(2)}, u32[]{:S(2)}) %collective-permute-start.13) | collective-permute-done | bytes 73760 | tf_op jit(solution)/shard_map/ppermute | solution.py:831
  54.6 2.8 %collective-permute-start.14 = (f32[144,128]{1,0:T(8,128)S(1)}, f32[144,128]{1,0:T(8,128)S(1)}, u32[]{:S(2)}, u32[]{:S(2)}) collective-permute-start(f32[144,128]{1,0:T(8,128)S(1)} %add.26), channel_id=1, source_target_pairs={{0,16},{1,17},{2,18},{3,19},{4,20},{5,21},{6,22},{7,23},{8,24},{9,... | collective-permute-start | bytes 221192 | tf_op jit(solution)/shard_map/ppermute | solution.py:831
  57.4 1.6 %image_gradient.6.rest_0_ = bf16[6,8,128,256]{3,2,1,0:T(8,128)(2,1)} custom-call(bf16[6,8,128,128]{3,2,1,0:T(8,128)(2,1)S(1)} %pre_gradient.1.pre_grad, bf16[6,1,128,128]{3,2,1,0:T(8,128)(2,1)S(1)} %collective-permute-done.11.ahead, bf16[6,1,128,128]{3,2,1,0:T(8,128)(2,1)S(1)} %collective-permute-done.12.across, ...), custom_call_target="tpu_custom_call", output_to_operand_aliasing={{}: (4, {})} | custom-call | flops 603979776 | bytes 786432 | tf_op jit(solution)/shard_map/image_gradient/pallas_call | solution.py:731
  59.0 1.7 %collective-permute-done.14 = f32[144,128]{1,0:T(8,128)S(1)} collective-permute-done((f32[144,128]{1,0:T(8,128)S(1)}, f32[144,128]{1,0:T(8,128)S(1)}, u32[]{:S(2)}, u32[]{:S(2)}) %collective-permute-start.14) | collective-permute-done | bytes 73760 | tf_op jit(solution)/shard_map/ppermute | solution.py:831
  61.1 1.6 %image_gradient.7.rest_0_ = bf16[6,8,128,256]{3,2,1,0:T(8,128)(2,1)} custom-call(bf16[6,8,128,128]{3,2,1,0:T(8,128)(2,1)S(1)} %pre_gradient.1.pre_grad, bf16[6,1,128,128]{3,2,1,0:T(8,128)(2,1)S(1)} %collective-permute-done.11.ahead, bf16[6,1,128,128]{3,2,1,0:T(8,128)(2,1)S(1)} %collective-permute-done.12.across, ...), custom_call_target="tpu_custom_call", output_to_operand_aliasing={{}: (4, {})} | custom-call | flops 603979776 | bytes 786432 | tf_op jit(solution)/shard_map/image_gradient/pallas_call | solution.py:731
  62.7 2.0 %collective-permute-done.15.received = bf16[144,128]{1,0:T(8,128)(2,1)S(1)} collective-permute-done((bf16[144,128]{1,0:T(8,128)(2,1)S(1)}, bf16[144,128]{1,0:T(8,128)(2,1)S(1)}, u32[]{:S(2)}, u32[]{:S(2)}) %collective-permute-start.15) | collective-permute-done | bytes 36896 | tf_op jit(solution)/shard_map/ppermute | solution.py:831
  66.0 1.6 %image_gradient.8.rest_0_ = bf16[6,8,128,256]{3,2,1,0:T(8,128)(2,1)} custom-call(bf16[6,8,128,128]{3,2,1,0:T(8,128)(2,1)S(1)} %pre_gradient.1.pre_grad, bf16[6,1,128,128]{3,2,1,0:T(8,128)(2,1)S(1)} %collective-permute-done.11.ahead, bf16[6,1,128,128]{3,2,1,0:T(8,128)(2,1)S(1)} %collective-permute-done.12.across, ...), custom_call_target="tpu_custom_call", output_to_operand_aliasing={{}: (4, {})} | custom-call | flops 603979776 | bytes 786432 | tf_op jit(solution)/shard_map/image_gradient/pallas_call | solution.py:731
  67.7 2.3 %collective-permute-done.16.received = bf16[288,128]{1,0:T(8,128)(2,1)S(1)} collective-permute-done((bf16[288,128]{1,0:T(8,128)(2,1)S(1)}, bf16[288,128]{1,0:T(8,128)(2,1)S(1)}, u32[]{:S(2)}, u32[]{:S(2)}) %collective-permute-start.16) | collective-permute-done | bytes 73760 | tf_op jit(solution)/shard_map/ppermute | solution.py:831
  70.0 1.5 %collective-permute-start.17 = (bf16[576,128]{1,0:T(8,128)(2,1)S(1)}, bf16[576,128]{1,0:T(8,128)(2,1)S(1)}, u32[]{:S(2)}, u32[]{:S(2)}) collective-permute-start(bf16[576,128]{1,0:T(8,128)(2,1)S(1)} %join.4.value), channel_id=1, source_target_pairs={{0,4},{1,3},{2,6},{3,1},{4,0},{5,7},{6,2},{7,5},{8,12},{9,11},{10,... | collective-permute-start | bytes 442376 | tf_op jit(solution)/shard_map/ppermute | solution.py:831
  71.5 2.5 %image_gradient.9 = bf16[6,8,128,256]{3,2,1,0:T(8,128)(2,1)} custom-call(bf16[6,8,128,128]{3,2,1,0:T(8,128)(2,1)S(1)} %pre_gradient.1.pre_grad, bf16[6,1,128,128]{3,2,1,0:T(8,128)(2,1)S(1)} %collective-permute-done.11.ahead, bf16[6,1,128,128]{3,2,1,0:T(8,128)(2,1)S(1)} %collective-permute-done.12.across, ...), custom_call_target="tpu_custom_call", output_to_operand_aliasing={{}: (4, {})} | custom-call | flops 1207959552 | bytes 1572864 | tf_op jit(solution)/shard_map/image_gradient/pallas_call | solution.py:731
  (50 shorter events, 21.0 us)
Async XLA Ops:
  2.3 9.4 %collective-permute-start = (bf16[6,1,128,256]{3,2,1,0:T(8,128)(2,1)S(1)}, bf16[6,1,128,256]{3,2,1,0:T(8,128)(2,1)S(1)}, u32[]{:S(2)}, u32[]{:S(2)}) collective-permute-start(bf16[6,1,128,256]{3,2,1,0:T(8,128)(2,1)S(1)} %get-tuple-element.167), channel_id=1, source_target_pairs={{0,1},{1,0},{2,3},{3,2},{4,5},{5,4},{6,7},{7,6},{8,9},{9,8},{10,11... | collective-permute-start | bytes 1179656 | tf_op jit(solution)/shard_map/ppermute | solution.py:826
  2.9 8.9 %collective-permute-start.1 = (bf16[6,1,128,256]{3,2,1,0:T(8,128)(2,1)S(1)}, bf16[6,1,128,256]{3,2,1,0:T(8,128)(2,1)S(1)}, u32[]{:S(2)}, u32[]{:S(2)}) collective-permute-start(bf16[6,1,128,256]{3,2,1,0:T(8,128)(2,1)S(1)} %get-tuple-element.168), channel_id=1, source_target_pairs={{0,8},{1,2},{2,1},{3,11},{4,12},{5,6},{6,5},{7,15},{8,0},{9,10},{1... | collective-permute-start | bytes 1179656 | tf_op jit(solution)/shard_map/ppermute | solution.py:826
  12.8 1.3 %collective-permute-start.2 = (f32[72,128]{1,0:T(8,128)S(1)}, f32[72,128]{1,0:T(8,128)S(1)}, u32[]{:S(2)}, u32[]{:S(2)}) collective-permute-start(f32[72,128]{1,0:T(8,128)S(1)} %get-tuple-element.176), channel_id=1, source_target_pairs={{0,1},{1,0},{2,3},{3,2},{4,5},{5,4},{6,7},{7,6},{8,9},{9,8},{10,11... | collective-permute-start | bytes 110600 | tf_op jit(solution)/shard_map/ppermute | solution.py:831
  14.1 4.0 %collective-permute-start.3 = (f32[72,128]{1,0:T(8,128)S(1)}, f32[72,128]{1,0:T(8,128)S(1)}, u32[]{:S(2)}, u32[]{:S(2)}) collective-permute-start(f32[72,128]{1,0:T(8,128)S(1)} %add.21), channel_id=1, source_target_pairs={{0,4},{1,3},{2,6},{3,1},{4,0},{5,7},{6,2},{7,5},{8,12},{9,11},{10,... | collective-permute-start | bytes 110600 | tf_op jit(solution)/shard_map/ppermute | solution.py:831
  18.1 4.3 %collective-permute-start.4 = (f32[72,128]{1,0:T(8,128)S(1)}, f32[72,128]{1,0:T(8,128)S(1)}, u32[]{:S(2)}, u32[]{:S(2)}) collective-permute-start(f32[72,128]{1,0:T(8,128)S(1)} %add.22), channel_id=1, source_target_pairs={{0,2},{1,5},{2,0},{3,7},{4,6},{5,1},{6,4},{7,3},{8,10},{9,13},{10,... | collective-permute-start | bytes 110600 | tf_op jit(solution)/shard_map/ppermute | solution.py:831
  22.4 4.2 %collective-permute-start.5 = (f32[72,128]{1,0:T(8,128)S(1)}, f32[72,128]{1,0:T(8,128)S(1)}, u32[]{:S(2)}, u32[]{:S(2)}) collective-permute-start(f32[72,128]{1,0:T(8,128)S(1)} %add.23), channel_id=1, source_target_pairs={{0,8},{1,9},{2,10},{3,11},{4,12},{5,13},{6,14},{7,15},{8,0},{9,1},... | collective-permute-start | bytes 110600 | tf_op jit(solution)/shard_map/ppermute | solution.py:831
  26.6 6.2 %copy-start = (f32[2,64,64]{2,1,0:T(8,128)S(1)}, f32[2,64,64]{2,1,0:T(8,128)}, u32[]{:S(2)}) copy-start(f32[2,64,64]{2,1,0:T(8,128)} %colors.1) | copy-start | bytes 98308
  26.6 6.2 %copy-start.1 = (f32[128]{0:T(128)S(1)}, f32[128]{0:T(128)}, u32[]{:S(2)}) copy-start(f32[128]{0:T(128)} %param.8) | copy-start | bytes 1540
  26.6 4.9 %collective-permute-start.6 = (f32[72,128]{1,0:T(8,128)S(1)}, f32[72,128]{1,0:T(8,128)S(1)}, u32[]{:S(2)}, u32[]{:S(2)}) collective-permute-start(f32[72,128]{1,0:T(8,128)S(1)} %add.24), channel_id=1, source_target_pairs={{0,16},{1,17},{2,18},{3,19},{4,20},{5,21},{6,22},{7,23},{8,24},{9,... | collective-permute-start | bytes 110600 | tf_op jit(solution)/shard_map/ppermute | solution.py:831
  31.5 1.2 %collective-permute-start.7 = (f32[72,128]{1,0:T(8,128)S(1)}, f32[72,128]{1,0:T(8,128)S(1)}, u32[]{:S(2)}, u32[]{:S(2)}) collective-permute-start(f32[72,128]{1,0:T(8,128)S(1)} %add.25.own), channel_id=1, source_target_pairs={{0,1},{1,0},{2,3},{3,2},{4,5},{5,4},{6,7},{7,6},{8,9},{9,8},{10,11... | collective-permute-start | bytes 110600 | tf_op jit(solution)/shard_map/ppermute | solution.py:831
  36.0 2.0 %collective-permute-start.8 = (f32[1152,128]{1,0:T(8,128)S(1)}, f32[1152,128]{1,0:T(8,128)S(1)}, u32[]{:S(2)}, u32[]{:S(2)}) collective-permute-start(f32[1152,128]{1,0:T(8,128)S(1)} %get-tuple-element.246), channel_id=1, source_target_pairs={{0,1},{1,0},{2,3},{3,2},{4,5},{5,4},{6,7},{7,6},{8,9},{9,8},{10,11... | collective-permute-start | bytes 1769480 | tf_op jit(solution)/shard_map/ppermute | solution.py:831
  38.1 6.8 %collective-permute-start.9 = (f32[576,128]{1,0:T(8,128)S(1)}, f32[576,128]{1,0:T(8,128)S(1)}, u32[]{:S(2)}, u32[]{:S(2)}) collective-permute-start(f32[576,128]{1,0:T(8,128)S(1)} %get-tuple-element.261), channel_id=1, source_target_pairs={{0,4},{1,3},{2,6},{3,1},{4,0},{5,7},{6,2},{7,5},{8,12},{9,11},{10,... | collective-permute-start | bytes 884744 | tf_op jit(solution)/shard_map/ppermute | solution.py:831
  39.6 10.5 %collective-permute-start.11 = (bf16[6,1,128,128]{3,2,1,0:T(8,128)(2,1)S(1)}, bf16[6,1,128,128]{3,2,1,0:T(8,128)(2,1)S(1)}, u32[]{:S(2)}, u32[]{:S(2)}) collective-permute-start(bf16[6,1,128,128]{3,2,1,0:T(8,128)(2,1)S(1)} %get-tuple-element.283), channel_id=1, source_target_pairs={{0,1},{1,0},{2,3},{3,2},{4,5},{5,4},{6,7},{7,6},{8,9},{9,8},{10,11... | collective-permute-start | bytes 589832 | tf_op jit(solution)/shard_map/ppermute | solution.py:826
  39.6 10.5 %collective-permute-start.12 = (bf16[6,1,128,128]{3,2,1,0:T(8,128)(2,1)S(1)}, bf16[6,1,128,128]{3,2,1,0:T(8,128)(2,1)S(1)}, u32[]{:S(2)}, u32[]{:S(2)}) collective-permute-start(bf16[6,1,128,128]{3,2,1,0:T(8,128)(2,1)S(1)} %get-tuple-element.284), channel_id=1, source_target_pairs={{0,8},{1,2},{2,1},{3,11},{4,12},{5,6},{6,5},{7,15},{8,0},{9,10},{1... | collective-permute-start | bytes 589832 | tf_op jit(solution)/shard_map/ppermute | solution.py:826
  44.9 5.2 %collective-permute-start.10 = (f32[288,128]{1,0:T(8,128)S(1)}, f32[288,128]{1,0:T(8,128)S(1)}, u32[]{:S(2)}, u32[]{:S(2)}) collective-permute-start(f32[288,128]{1,0:T(8,128)S(1)} %get-tuple-element.271), channel_id=1, source_target_pairs={{0,2},{1,5},{2,0},{3,7},{4,6},{5,1},{6,4},{7,3},{8,10},{9,13},{10,... | collective-permute-start | bytes 442376 | tf_op jit(solution)/shard_map/ppermute | solution.py:831
  50.2 4.4 %collective-permute-start.13 = (f32[144,128]{1,0:T(8,128)S(1)}, f32[144,128]{1,0:T(8,128)S(1)}, u32[]{:S(2)}, u32[]{:S(2)}) collective-permute-start(f32[144,128]{1,0:T(8,128)S(1)} %get-tuple-element.286), channel_id=1, source_target_pairs={{0,8},{1,9},{2,10},{3,11},{4,12},{5,13},{6,14},{7,15},{8,0},{9,1},... | collective-permute-start | bytes 221192 | tf_op jit(solution)/shard_map/ppermute | solution.py:831
  54.6 6.1 %collective-permute-start.14 = (f32[144,128]{1,0:T(8,128)S(1)}, f32[144,128]{1,0:T(8,128)S(1)}, u32[]{:S(2)}, u32[]{:S(2)}) collective-permute-start(f32[144,128]{1,0:T(8,128)S(1)} %add.26), channel_id=1, source_target_pairs={{0,16},{1,17},{2,18},{3,19},{4,20},{5,21},{6,22},{7,23},{8,24},{9,... | collective-permute-start | bytes 221192 | tf_op jit(solution)/shard_map/ppermute | solution.py:831
  60.7 4.0 %collective-permute-start.15 = (bf16[144,128]{1,0:T(8,128)(2,1)S(1)}, bf16[144,128]{1,0:T(8,128)(2,1)S(1)}, u32[]{:S(2)}, u32[]{:S(2)}) collective-permute-start(bf16[144,128]{1,0:T(8,128)(2,1)S(1)} %add_convert_fusion.value), channel_id=1, source_target_pairs={{0,8},{1,9},{2,10},{3,11},{4,12},{5,13},{6,14},{7,15},{8,0},{9,1},... | collective-permute-start | bytes 110600 | tf_op jit(solution)/shard_map/ppermute | solution.py:831
  64.8 5.2 %collective-permute-start.16 = (bf16[288,128]{1,0:T(8,128)(2,1)S(1)}, bf16[288,128]{1,0:T(8,128)(2,1)S(1)}, u32[]{:S(2)}, u32[]{:S(2)}) collective-permute-start(bf16[288,128]{1,0:T(8,128)(2,1)S(1)} %join.3.value), channel_id=1, source_target_pairs={{0,2},{1,5},{2,0},{3,7},{4,6},{5,1},{6,4},{7,3},{8,10},{9,13},{10,... | collective-permute-start | bytes 221192 | tf_op jit(solution)/shard_map/ppermute | solution.py:831
  70.0 5.2 %collective-permute-start.17 = (bf16[576,128]{1,0:T(8,128)(2,1)S(1)}, bf16[576,128]{1,0:T(8,128)(2,1)S(1)}, u32[]{:S(2)}, u32[]{:S(2)}) collective-permute-start(bf16[576,128]{1,0:T(8,128)(2,1)S(1)} %join.4.value), channel_id=1, source_target_pairs={{0,4},{1,3},{2,6},{3,1},{4,0},{5,7},{6,2},{7,5},{8,12},{9,11},{10,... | collective-permute-start | bytes 442376 | tf_op jit(solution)/shard_map/ppermute | solution.py:831
  75.3 1.6 %collective-permute-start.18 = (bf16[1152,128]{1,0:T(8,128)(2,1)S(1)}, bf16[1152,128]{1,0:T(8,128)(2,1)S(1)}, u32[]{:S(2)}, u32[]{:S(2)}) collective-permute-start(bf16[1152,128]{1,0:T(8,128)(2,1)S(1)} %join.5.value), channel_id=1, source_target_pairs={{0,1},{1,0},{2,3},{3,2},{4,5},{5,4},{6,7},{7,6},{8,9},{9,8},{10,11... | collective-permute-start | bytes 884744 | tf_op jit(solution)/shard_map/ppermute | solution.py:831

commit v6 on v5

--- a/solution.py
+++ b/solution.py
@@ -577,7 +577,7 @@
             pltpu.SemaphoreType.DMA((count,)),
         ],
         input_output_aliases={0: 3},
-        compiler_params=pltpu.CompilerParams(vmem_limit_bytes=28 * MIB),
+        compiler_params=pltpu.CompilerParams(vmem_limit_bytes=36 * MIB),
         cost_estimate=pl.CostEstimate(
             flops=2 * count * rows * width * 9 * cin * cout,
             bytes_accessed=2 * images.size + 2 * upstream.size + 4 * upstream.size,
@@ -746,7 +746,7 @@
 
 
 def images_per_step(count):
-    return 2 if count % 2 == 0 else 1
+    return next(many for many in (3, 2, 1) if count % many == 0)
 
 
 def fetched(images, kernel):
@@ -864,7 +864,7 @@
 
     value = value + exchange(send, devices, plan[0])
     for stage in plan[1:]:
-        value = value + summed(value, stage, 2 if stage in plan[2:4] else 1)
+        value = value + summed(value, stage, 2 if stage in plan[1:3] else 1)
     received = exchange(value, devices, plan[0])
     first = state["next"]
     if first < count:

time: 78.1 us -> 78.6 us (level)
  starting transfers between devices: 20.9 us -> 19.7 us
  waiting for transfers between devices: 16.7 us -> 17.6 us
  Pallas kernels: 39.2 us -> 40 us
    ppermute x15, starting transfers between devices: 16.7 us -> 15.6 us  [exchange(): return lax.ppermute(value, AXES, pairs)]
    ppermute x15, waiting for transfers between devices: 16.7 us -> 17.6 us  [exchange(): return lax.ppermute(value, AXES, pairs)]
  transfers between devices with their start and end apart: 19 -> 19, of which waited for: 13 -> 13; matrix products, arithmetic and copies ran while one was open for 0% -> 0% of each run, Pallas kernels for 41% -> 42%
where the time goes in v6:
time: 78.6 us; the launch traced here: 78.4 us
  Pallas kernels  40 us (51%)
  starting transfers between devices  19.7 us (25%)
  waiting for transfers between devices  17.6 us (22%)
  between operations  1.03 us (1%)
    ppermute x15, waiting for transfers between devices, exchange(): return lax.ppermute(value, AXES, pairs)  17.6 us
    ppermute x15, starting transfers between devices, exchange(): return lax.ppermute(value, AXES, pairs)  15.6 us
    pallas_call x4, Pallas kernels, moments(): pl.pallas_call(functools.partial(moment_kernel, first, count), in_specs=[...  9.34 us
    pallas_call x5, Pallas kernels, image_gradient(): pl.pallas_call(functools.partial(image_kernel, first), grid=(count,), in_...  9.09 us
    pallas_call x1, Pallas kernels, forward(): pl.pallas_call(functools.partial(forward_kernel, many), grid=(count // ma...  6.61 us
    ppermute x2, starting transfers between devices, halos(): lax.ppermute(across, AXES, pairs[1])  3.6 us
    pallas_call x1, Pallas kernels, painted(): pl.pallas_call(paint_kernel, grid=(count,), in_specs=[resident()] * 5, ou...  3.4 us
    pallas_call x1, Pallas kernels, whitened(): pl.pallas_call(functools.partial(whitening_kernel, total_pix, stage), in_...  3.24 us
  transfers between devices with their start and end apart: 19, of which 13 were waited for; matrix products, arithmetic and copies ran while one was open for 0% of the time, Pallas kernels for 42%

profile of v6, /device:TPU:0, one launch (start us, length us, event | category | flops | bytes accessed | tf_op | source)
XLA Modules:
  0.0 78.4 jit_solution(5578982446588155746)
XLA Ops:
  0.6 1.9 %edge_rows.1 = (bf16[6,1,128,256]{3,2,1,0:T(8,128)(2,1)S(1)}, bf16[6,1,128,256]{3,2,1,0:T(8,128)(2,1)S(1)}, bf16[3,3,256,128]{3,2,1,0:T(8,128)(2,1)S(1)}, bf16[6,8,128,256]{3,2,1,0:T(8,128)(2,1)S(1)}) custom-call(bf16[6,8,128,256]{3,2,1,0:T(8,128)(2,1)} %img.1, bf16[3,3,256,128]{3,2,1,0:T(8,128)(2,1)} %kern.1), custom_call_target="tpu_custom_call" | custom-call | tf_op jit(solution)/shard_map/edge_rows/pallas_call | solution.py:756
  3.0 2.6 %collective-permute-start.1 = (bf16[6,1,128,256]{3,2,1,0:T(8,128)(2,1)S(1)}, bf16[6,1,128,256]{3,2,1,0:T(8,128)(2,1)S(1)}, u32[]{:S(2)}, u32[]{:S(2)}) collective-permute-start(bf16[6,1,128,256]{3,2,1,0:T(8,128)(2,1)S(1)} %get-tuple-element.168), channel_id=1, source_target_pairs={{0,8},{1,2},{2,1},{3,11},{4,12},{5,6},{6,5},{7,15},{8,0},{9,10},{1... | collective-permute-start | bytes 1179656 | tf_op jit(solution)/shard_map/ppermute | solution.py:826
  5.7 6.6 %forward_inner.1 = (f32[6,8,128,128]{3,2,1,0:T(8,128)S(1)}, f32[256,256]{1,0:T(8,128)S(1)}, f32[8,128]{1,0:T(8,128)S(1)}, bf16[6,8,128,256]{3,2,1,0:T(8,128)(2,1)S(1)}, bf16[6,8,128,128]{3,2,1,0:T(8,128)(2,1)S(1)}) custom-call(bf16[6,8,128,256]{3,2,1,0:T(8,128)(2,1)S(1)} %get-tuple-element.169.first, ...), custom_call_target="tpu_custom_call", output_to_operand_aliasing={{3}: (0, {})} | custom-call | flops 3623878656 | bytes 7864320 | tf_op jit(solution)/shard_map/forward_inner/pallas_call | solution.py:567
  14.7 1.5 %collective-permute-start.3 = (f32[72,128]{1,0:T(8,128)S(1)}, f32[72,128]{1,0:T(8,128)S(1)}, u32[]{:S(2)}, u32[]{:S(2)}) collective-permute-start(f32[72,128]{1,0:T(8,128)S(1)} %add.21), channel_id=1, source_target_pairs={{0,4},{1,3},{2,6},{3,1},{4,0},{5,7},{6,2},{7,5},{8,12},{9,11},{10,... | collective-permute-start | bytes 110600 | tf_op jit(solution)/shard_map/ppermute | solution.py:831
  16.2 2.7 %moments.4 = (f32[768,768]{1,0:T(8,128)S(1)}, f32[768,128]{1,0:T(8,128)S(1)}) custom-call(f32[6,8,128,128]{3,2,1,0:T(8,128)S(1)} %get-tuple-element.272.pre.refs_0_, f32[6,1,128,128]{3,2,1,0:T(8,128)S(1)} %get-tuple-element.273.refs_1_.low, f32[6,1,128,128]{3,2,1,0:T(8,128)S(1)} %get-tuple-element.274.refs_2_.high, ...), custom_call_target="tpu_custom_call" | custom-call | flops 2415919104 | bytes 8388608 | tf_op jit(solution)/shard_map/moments/pallas_call | solution.py:616
  20.3 2.9 %moments.5 = (f32[768,768]{1,0:T(8,128)S(1)}, f32[768,128]{1,0:T(8,128)S(1)}) custom-call(f32[6,8,128,128]{3,2,1,0:T(8,128)S(1)} %get-tuple-element.272.pre.refs_0_, f32[6,1,128,128]{3,2,1,0:T(8,128)S(1)} %get-tuple-element.273.refs_1_.low, f32[6,1,128,128]{3,2,1,0:T(8,128)S(1)} %get-tuple-element.274.refs_2_.high, ...), custom_call_target="tpu_custom_call", output_to_operand_aliasing={{0}: (8, {}), {1}: (9, {})} | custom-call | flops 2415919104 | bytes 8388608 | tf_op jit(solution)/shard_map/moments/pallas_call | solution.py:616
  24.3 1.8 %moments.6 = (f32[768,768]{1,0:T(8,128)S(1)}, f32[768,128]{1,0:T(8,128)S(1)}) custom-call(f32[6,8,128,128]{3,2,1,0:T(8,128)S(1)} %get-tuple-element.272.pre.refs_0_, f32[6,1,128,128]{3,2,1,0:T(8,128)S(1)} %get-tuple-element.273.refs_1_.low, f32[6,1,128,128]{3,2,1,0:T(8,128)S(1)} %get-tuple-element.274.refs_2_.high, ...), custom_call_target="tpu_custom_call", output_to_operand_aliasing={{0}: (8, {}), {1}: (9, {})} | custom-call | flops 1207959552 | bytes 8388608 | tf_op jit(solution)/shard_map/moments/pallas_call | solution.py:616
  27.3 2.7 %collective-permute-start.6 = (f32[72,128]{1,0:T(8,128)S(1)}, f32[72,128]{1,0:T(8,128)S(1)}, u32[]{:S(2)}, u32[]{:S(2)}) collective-permute-start(f32[72,128]{1,0:T(8,128)S(1)} %add.24), channel_id=1, source_target_pairs={{0,16},{1,17},{2,18},{3,19},{4,20},{5,21},{6,22},{7,23},{8,24},{9,... | collective-permute-start | bytes 110600 | tf_op jit(solution)/shard_map/ppermute | solution.py:831
  30.0 1.8 %moments.7 = (f32[768,768]{1,0:T(8,128)S(1)}, f32[768,128]{1,0:T(8,128)S(1)}) custom-call(f32[6,8,128,128]{3,2,1,0:T(8,128)S(1)} %get-tuple-element.272.pre.refs_0_, f32[6,1,128,128]{3,2,1,0:T(8,128)S(1)} %get-tuple-element.273.refs_1_.low, f32[6,1,128,128]{3,2,1,0:T(8,128)S(1)} %get-tuple-element.274.refs_2_.high, ...), custom_call_target="tpu_custom_call", output_to_operand_aliasing={{0}: (8, {}), {1}: (9, {})} | custom-call | flops 1207959552 | bytes 8388608 | tf_op jit(solution)/shard_map/moments/pallas_call | solution.py:616
  33.5 3.2 %whitening.1 = (f32[1152,128]{1,0:T(8,128)S(1)}, f32[1152,128]{1,0:T(8,128)S(1)}, f32[2,64,64]{2,1,0:T(8,128)}, bf16[384,256]{1,0:T(8,128)(2,1)S(1)}, bf16[256,2...) custom-call(f32[72,128]{1,0:T(8,128)S(1)} %add.25.own, f32[72,128]{1,0:T(8,128)S(1)} %collective-permute-done.7.other, ...), custom_call_target="tpu_custom_call" | custom-call | flops 603979776 | bytes 8388608 | tf_op jit(solution)/shard_map/whitening/pallas_call | solution.py:645
  41.0 2.6 %pre_gradient.1.pre_grad = bf16[6,8,128,128]{3,2,1,0:T(8,128)(2,1)S(1)} custom-call(f32[6,8,128,128]{3,2,1,0:T(8,128)S(1)} %get-tuple-element.272.pre.refs_0_, f32[6,1,128,128]{3,2,1,0:T(8,128)S(1)} %get-tuple-element.273.refs_1_.low, f32[6,1,128,128]{3,2,1,0:T(8,128)S(1)} %get-tuple-element.274.refs_2_.high, ...), custom_call_target="tpu_custom_call" | custom-call | flops 1207959552 | bytes 6291456 | tf_op jit(solution)/shard_map/pre_gradient/pallas_call | solution.py:672
  43.6 2.0 %collective-permute-done.9.received = f32[576,128]{1,0:T(8,128)S(1)} collective-permute-done((f32[576,128]{1,0:T(8,128)S(1)}, f32[576,128]{1,0:T(8,128)S(1)}, u32[]{:S(2)}, u32[]{:S(2)}) %collective-permute-start.9) | collective-permute-done | bytes 294944 | tf_op jit(solution)/shard_map/ppermute | solution.py:831
  46.6 3.4 %colored.1 = bf16[6,8,128,128]{3,2,1,0:T(8,128)(2,1)} custom-call(f32[6,8,128,128]{3,2,1,0:T(8,128)S(1)} %get-tuple-element.272.pre.refs_0_, f32[6,1,128,128]{3,2,1,0:T(8,128)S(1)} %get-tuple-element.273.refs_1_.low, f32[6,1,128,128]{3,2,1,0:T(8,128)S(1)} %get-tuple-element.274.refs_2_.high, bf16[256,256]{1,0:T(8,128)(2,1)S(1)} %get-tuple-element.275.paint, ...), custom_call_target="tpu_custom_call" | custom-call | flops 805306368 | bytes 4718592 | tf_op jit(solution)/shard_map/colored/pallas_call | solution.py:690
  51.9 1.6 %image_gradient.5.rest_0_ = bf16[6,8,128,256]{3,2,1,0:T(8,128)(2,1)} custom-call(bf16[6,8,128,128]{3,2,1,0:T(8,128)(2,1)S(1)} %pre_gradient.1.pre_grad, bf16[6,1,128,128]{3,2,1,0:T(8,128)(2,1)S(1)} %collective-permute-done.11.ahead, bf16[6,1,128,128]{3,2,1,0:T(8,128)(2,1)S(1)} %collective-permute-done.12.across, bf16[1152,256]{1,0:T(8,128)(2,1)S(1)} %turned_weights.1.wts), custom_call_target="tpu_custom_call" | custom-call | flops 603979776 | bytes 786432 | tf_op jit(solution)/shard_map/image_gradient/pallas_call | solution.py:731
  53.6 1.8 %collective-permute-done.13 = f32[144,128]{1,0:T(8,128)S(1)} collective-permute-done((f32[144,128]{1,0:T(8,128)S(1)}, f32[144,128]{1,0:T(8,128)S(1)}, u32[]{:S(2)}, u32[]{:S(2)}) %collective-permute-start.13) | collective-permute-done | bytes 73760 | tf_op jit(solution)/shard_map/ppermute | solution.py:831
  55.4 2.6 %collective-permute-start.14 = (f32[144,128]{1,0:T(8,128)S(1)}, f32[144,128]{1,0:T(8,128)S(1)}, u32[]{:S(2)}, u32[]{:S(2)}) collective-permute-start(f32[144,128]{1,0:T(8,128)S(1)} %add.26), channel_id=1, source_target_pairs={{0,16},{1,17},{2,18},{3,19},{4,20},{5,21},{6,22},{7,23},{8,24},{9,... | collective-permute-start | bytes 221192 | tf_op jit(solution)/shard_map/ppermute | solution.py:831
  58.0 1.6 %image_gradient.6.rest_0_ = bf16[6,8,128,256]{3,2,1,0:T(8,128)(2,1)} custom-call(bf16[6,8,128,128]{3,2,1,0:T(8,128)(2,1)S(1)} %pre_gradient.1.pre_grad, bf16[6,1,128,128]{3,2,1,0:T(8,128)(2,1)S(1)} %collective-permute-done.11.ahead, bf16[6,1,128,128]{3,2,1,0:T(8,128)(2,1)S(1)} %collective-permute-done.12.across, ...), custom_call_target="tpu_custom_call", output_to_operand_aliasing={{}: (4, {})} | custom-call | flops 603979776 | bytes 786432 | tf_op jit(solution)/shard_map/image_gradient/pallas_call | solution.py:731
  59.6 1.8 %collective-permute-done.14 = f32[144,128]{1,0:T(8,128)S(1)} collective-permute-done((f32[144,128]{1,0:T(8,128)S(1)}, f32[144,128]{1,0:T(8,128)S(1)}, u32[]{:S(2)}, u32[]{:S(2)}) %collective-permute-start.14) | collective-permute-done | bytes 73760 | tf_op jit(solution)/shard_map/ppermute | solution.py:831
  61.8 1.6 %image_gradient.7.rest_0_ = bf16[6,8,128,256]{3,2,1,0:T(8,128)(2,1)} custom-call(bf16[6,8,128,128]{3,2,1,0:T(8,128)(2,1)S(1)} %pre_gradient.1.pre_grad, bf16[6,1,128,128]{3,2,1,0:T(8,128)(2,1)S(1)} %collective-permute-done.11.ahead, bf16[6,1,128,128]{3,2,1,0:T(8,128)(2,1)S(1)} %collective-permute-done.12.across, ...), custom_call_target="tpu_custom_call", output_to_operand_aliasing={{}: (4, {})} | custom-call | flops 603979776 | bytes 786432 | tf_op jit(solution)/shard_map/image_gradient/pallas_call | solution.py:731
  63.5 2.0 %collective-permute-done.15.received = bf16[144,128]{1,0:T(8,128)(2,1)S(1)} collective-permute-done((bf16[144,128]{1,0:T(8,128)(2,1)S(1)}, bf16[144,128]{1,0:T(8,128)(2,1)S(1)}, u32[]{:S(2)}, u32[]{:S(2)}) %collective-permute-start.15) | collective-permute-done | bytes 36896 | tf_op jit(solution)/shard_map/ppermute | solution.py:831
  66.8 1.6 %image_gradient.8.rest_0_ = bf16[6,8,128,256]{3,2,1,0:T(8,128)(2,1)} custom-call(bf16[6,8,128,128]{3,2,1,0:T(8,128)(2,1)S(1)} %pre_gradient.1.pre_grad, bf16[6,1,128,128]{3,2,1,0:T(8,128)(2,1)S(1)} %collective-permute-done.11.ahead, bf16[6,1,128,128]{3,2,1,0:T(8,128)(2,1)S(1)} %collective-permute-done.12.across, ...), custom_call_target="tpu_custom_call", output_to_operand_aliasing={{}: (4, {})} | custom-call | flops 603979776 | bytes 786432 | tf_op jit(solution)/shard_map/image_gradient/pallas_call | solution.py:731
  68.5 1.9 %collective-permute-done.16.received = bf16[288,128]{1,0:T(8,128)(2,1)S(1)} collective-permute-done((bf16[288,128]{1,0:T(8,128)(2,1)S(1)}, bf16[288,128]{1,0:T(8,128)(2,1)S(1)}, u32[]{:S(2)}, u32[]{:S(2)}) %collective-permute-start.16) | collective-permute-done | bytes 73760 | tf_op jit(solution)/shard_map/ppermute | solution.py:831
  71.7 2.5 %image_gradient.9 = bf16[6,8,128,256]{3,2,1,0:T(8,128)(2,1)} custom-call(bf16[6,8,128,128]{3,2,1,0:T(8,128)(2,1)S(1)} %pre_gradient.1.pre_grad, bf16[6,1,128,128]{3,2,1,0:T(8,128)(2,1)S(1)} %collective-permute-done.11.ahead, bf16[6,1,128,128]{3,2,1,0:T(8,128)(2,1)S(1)} %collective-permute-done.12.across, ...), custom_call_target="tpu_custom_call", output_to_operand_aliasing={{}: (4, {})} | custom-call | flops 1207959552 | bytes 1572864 | tf_op jit(solution)/shard_map/image_gradient/pallas_call | solution.py:731
  74.2 1.5 %collective-permute-done.17.received = bf16[576,128]{1,0:T(8,128)(2,1)S(1)} collective-permute-done((bf16[576,128]{1,0:T(8,128)(2,1)S(1)}, bf16[576,128]{1,0:T(8,128)(2,1)S(1)}, u32[]{:S(2)}, u32[]{:S(2)}) %collective-permute-start.17) | collective-permute-done | bytes 147488 | tf_op jit(solution)/shard_map/ppermute | solution.py:831
  (50 shorter events, 20.7 us)
Async XLA Ops:
  2.5 9.8 %collective-permute-start = (bf16[6,1,128,256]{3,2,1,0:T(8,128)(2,1)S(1)}, bf16[6,1,128,256]{3,2,1,0:T(8,128)(2,1)S(1)}, u32[]{:S(2)}, u32[]{:S(2)}) collective-permute-start(bf16[6,1,128,256]{3,2,1,0:T(8,128)(2,1)S(1)} %get-tuple-element.167), channel_id=1, source_target_pairs={{0,1},{1,0},{2,3},{3,2},{4,5},{5,4},{6,7},{7,6},{8,9},{9,8},{10,11... | collective-permute-start | bytes 1179656 | tf_op jit(solution)/shard_map/ppermute | solution.py:826
  3.0 9.3 %collective-permute-start.1 = (bf16[6,1,128,256]{3,2,1,0:T(8,128)(2,1)S(1)}, bf16[6,1,128,256]{3,2,1,0:T(8,128)(2,1)S(1)}, u32[]{:S(2)}, u32[]{:S(2)}) collective-permute-start(bf16[6,1,128,256]{3,2,1,0:T(8,128)(2,1)S(1)} %get-tuple-element.168), channel_id=1, source_target_pairs={{0,8},{1,2},{2,1},{3,11},{4,12},{5,6},{6,5},{7,15},{8,0},{9,10},{1... | collective-permute-start | bytes 1179656 | tf_op jit(solution)/shard_map/ppermute | solution.py:826
  13.4 1.3 %collective-permute-start.2 = (f32[72,128]{1,0:T(8,128)S(1)}, f32[72,128]{1,0:T(8,128)S(1)}, u32[]{:S(2)}, u32[]{:S(2)}) collective-permute-start(f32[72,128]{1,0:T(8,128)S(1)} %get-tuple-element.176), channel_id=1, source_target_pairs={{0,1},{1,0},{2,3},{3,2},{4,5},{5,4},{6,7},{7,6},{8,9},{9,8},{10,11... | collective-permute-start | bytes 110600 | tf_op jit(solution)/shard_map/ppermute | solution.py:831
  14.7 4.2 %collective-permute-start.3 = (f32[72,128]{1,0:T(8,128)S(1)}, f32[72,128]{1,0:T(8,128)S(1)}, u32[]{:S(2)}, u32[]{:S(2)}) collective-permute-start(f32[72,128]{1,0:T(8,128)S(1)} %add.21), channel_id=1, source_target_pairs={{0,4},{1,3},{2,6},{3,1},{4,0},{5,7},{6,2},{7,5},{8,12},{9,11},{10,... | collective-permute-start | bytes 110600 | tf_op jit(solution)/shard_map/ppermute | solution.py:831
  18.9 4.3 %collective-permute-start.4 = (f32[72,128]{1,0:T(8,128)S(1)}, f32[72,128]{1,0:T(8,128)S(1)}, u32[]{:S(2)}, u32[]{:S(2)}) collective-permute-start(f32[72,128]{1,0:T(8,128)S(1)} %add.22), channel_id=1, source_target_pairs={{0,2},{1,5},{2,0},{3,7},{4,6},{5,1},{6,4},{7,3},{8,10},{9,13},{10,... | collective-permute-start | bytes 110600 | tf_op jit(solution)/shard_map/ppermute | solution.py:831
  23.3 4.0 %collective-permute-start.5 = (f32[72,128]{1,0:T(8,128)S(1)}, f32[72,128]{1,0:T(8,128)S(1)}, u32[]{:S(2)}, u32[]{:S(2)}) collective-permute-start(f32[72,128]{1,0:T(8,128)S(1)} %add.23), channel_id=1, source_target_pairs={{0,8},{1,9},{2,10},{3,11},{4,12},{5,13},{6,14},{7,15},{8,0},{9,1},... | collective-permute-start | bytes 110600 | tf_op jit(solution)/shard_map/ppermute | solution.py:831
  27.3 6.2 %copy-start = (f32[2,64,64]{2,1,0:T(8,128)S(1)}, f32[2,64,64]{2,1,0:T(8,128)}, u32[]{:S(2)}) copy-start(f32[2,64,64]{2,1,0:T(8,128)} %colors.1) | copy-start | bytes 98308
  27.3 6.2 %copy-start.1 = (f32[128]{0:T(128)S(1)}, f32[128]{0:T(128)}, u32[]{:S(2)}) copy-start(f32[128]{0:T(128)} %param.8) | copy-start | bytes 1540
  27.3 4.9 %collective-permute-start.6 = (f32[72,128]{1,0:T(8,128)S(1)}, f32[72,128]{1,0:T(8,128)S(1)}, u32[]{:S(2)}, u32[]{:S(2)}) collective-permute-start(f32[72,128]{1,0:T(8,128)S(1)} %add.24), channel_id=1, source_target_pairs={{0,16},{1,17},{2,18},{3,19},{4,20},{5,21},{6,22},{7,23},{8,24},{9,... | collective-permute-start | bytes 110600 | tf_op jit(solution)/shard_map/ppermute | solution.py:831
  32.3 1.2 %collective-permute-start.7 = (f32[72,128]{1,0:T(8,128)S(1)}, f32[72,128]{1,0:T(8,128)S(1)}, u32[]{:S(2)}, u32[]{:S(2)}) collective-permute-start(f32[72,128]{1,0:T(8,128)S(1)} %add.25.own), channel_id=1, source_target_pairs={{0,1},{1,0},{2,3},{3,2},{4,5},{5,4},{6,7},{7,6},{8,9},{9,8},{10,11... | collective-permute-start | bytes 110600 | tf_op jit(solution)/shard_map/ppermute | solution.py:831
  36.7 2.0 %collective-permute-start.8 = (f32[1152,128]{1,0:T(8,128)S(1)}, f32[1152,128]{1,0:T(8,128)S(1)}, u32[]{:S(2)}, u32[]{:S(2)}) collective-permute-start(f32[1152,128]{1,0:T(8,128)S(1)} %get-tuple-element.246), channel_id=1, source_target_pairs={{0,1},{1,0},{2,3},{3,2},{4,5},{5,4},{6,7},{7,6},{8,9},{9,8},{10,11... | collective-permute-start | bytes 1769480 | tf_op jit(solution)/shard_map/ppermute | solution.py:831
  38.8 6.8 %collective-permute-start.9 = (f32[576,128]{1,0:T(8,128)S(1)}, f32[576,128]{1,0:T(8,128)S(1)}, u32[]{:S(2)}, u32[]{:S(2)}) collective-permute-start(f32[576,128]{1,0:T(8,128)S(1)} %get-tuple-element.261), channel_id=1, source_target_pairs={{0,4},{1,3},{2,6},{3,1},{4,0},{5,7},{6,2},{7,5},{8,12},{9,11},{10,... | collective-permute-start | bytes 884744 | tf_op jit(solution)/shard_map/ppermute | solution.py:831
  40.1 10.9 %collective-permute-start.11 = (bf16[6,1,128,128]{3,2,1,0:T(8,128)(2,1)S(1)}, bf16[6,1,128,128]{3,2,1,0:T(8,128)(2,1)S(1)}, u32[]{:S(2)}, u32[]{:S(2)}) collective-permute-start(bf16[6,1,128,128]{3,2,1,0:T(8,128)(2,1)S(1)} %get-tuple-element.283), channel_id=1, source_target_pairs={{0,1},{1,0},{2,3},{3,2},{4,5},{5,4},{6,7},{7,6},{8,9},{9,8},{10,11... | collective-permute-start | bytes 589832 | tf_op jit(solution)/shard_map/ppermute | solution.py:826
  40.1 10.9 %collective-permute-start.12 = (bf16[6,1,128,128]{3,2,1,0:T(8,128)(2,1)S(1)}, bf16[6,1,128,128]{3,2,1,0:T(8,128)(2,1)S(1)}, u32[]{:S(2)}, u32[]{:S(2)}) collective-permute-start(bf16[6,1,128,128]{3,2,1,0:T(8,128)(2,1)S(1)} %get-tuple-element.284), channel_id=1, source_target_pairs={{0,8},{1,2},{2,1},{3,11},{4,12},{5,6},{6,5},{7,15},{8,0},{9,10},{1... | collective-permute-start | bytes 589832 | tf_op jit(solution)/shard_map/ppermute | solution.py:826
  45.7 5.2 %collective-permute-start.10 = (f32[288,128]{1,0:T(8,128)S(1)}, f32[288,128]{1,0:T(8,128)S(1)}, u32[]{:S(2)}, u32[]{:S(2)}) collective-permute-start(f32[288,128]{1,0:T(8,128)S(1)} %get-tuple-element.271), channel_id=1, source_target_pairs={{0,2},{1,5},{2,0},{3,7},{4,6},{5,1},{6,4},{7,3},{8,10},{9,13},{10,... | collective-permute-start | bytes 442376 | tf_op jit(solution)/shard_map/ppermute | solution.py:831
  50.9 4.4 %collective-permute-start.13 = (f32[144,128]{1,0:T(8,128)S(1)}, f32[144,128]{1,0:T(8,128)S(1)}, u32[]{:S(2)}, u32[]{:S(2)}) collective-permute-start(f32[144,128]{1,0:T(8,128)S(1)} %get-tuple-element.286), channel_id=1, source_target_pairs={{0,8},{1,9},{2,10},{3,11},{4,12},{5,13},{6,14},{7,15},{8,0},{9,1},... | collective-permute-start | bytes 221192 | tf_op jit(solution)/shard_map/ppermute | solution.py:831
  55.4 6.1 %collective-permute-start.14 = (f32[144,128]{1,0:T(8,128)S(1)}, f32[144,128]{1,0:T(8,128)S(1)}, u32[]{:S(2)}, u32[]{:S(2)}) collective-permute-start(f32[144,128]{1,0:T(8,128)S(1)} %add.26), channel_id=1, source_target_pairs={{0,16},{1,17},{2,18},{3,19},{4,20},{5,21},{6,22},{7,23},{8,24},{9,... | collective-permute-start | bytes 221192 | tf_op jit(solution)/shard_map/ppermute | solution.py:831
  61.5 4.0 %collective-permute-start.15 = (bf16[144,128]{1,0:T(8,128)(2,1)S(1)}, bf16[144,128]{1,0:T(8,128)(2,1)S(1)}, u32[]{:S(2)}, u32[]{:S(2)}) collective-permute-start(bf16[144,128]{1,0:T(8,128)(2,1)S(1)} %add_convert_fusion.value), channel_id=1, source_target_pairs={{0,8},{1,9},{2,10},{3,11},{4,12},{5,13},{6,14},{7,15},{8,0},{9,1},... | collective-permute-start | bytes 110600 | tf_op jit(solution)/shard_map/ppermute | solution.py:831
  65.5 4.9 %collective-permute-start.16 = (bf16[288,128]{1,0:T(8,128)(2,1)S(1)}, bf16[288,128]{1,0:T(8,128)(2,1)S(1)}, u32[]{:S(2)}, u32[]{:S(2)}) collective-permute-start(bf16[288,128]{1,0:T(8,128)(2,1)S(1)} %join.3.value), channel_id=1, source_target_pairs={{0,2},{1,5},{2,0},{3,7},{4,6},{5,1},{6,4},{7,3},{8,10},{9,13},{10,... | collective-permute-start | bytes 221192 | tf_op jit(solution)/shard_map/ppermute | solution.py:831
  70.5 5.2 %collective-permute-start.17 = (bf16[576,128]{1,0:T(8,128)(2,1)S(1)}, bf16[576,128]{1,0:T(8,128)(2,1)S(1)}, u32[]{:S(2)}, u32[]{:S(2)}) collective-permute-start(bf16[576,128]{1,0:T(8,128)(2,1)S(1)} %join.4.value), channel_id=1, source_target_pairs={{0,4},{1,3},{2,6},{3,1},{4,0},{5,7},{6,2},{7,5},{8,12},{9,11},{10,... | collective-permute-start | bytes 442376 | tf_op jit(solution)/shard_map/ppermute | solution.py:831
  75.8 1.6 %collective-permute-start.18 = (bf16[1152,128]{1,0:T(8,128)(2,1)S(1)}, bf16[1152,128]{1,0:T(8,128)(2,1)S(1)}, u32[]{:S(2)}, u32[]{:S(2)}) collective-permute-start(bf16[1152,128]{1,0:T(8,128)(2,1)S(1)} %join.5.value), channel_id=1, source_target_pairs={{0,1},{1,0},{2,3},{3,2},{4,5},{5,4},{6,7},{7,6},{8,9},{9,8},{10,11... | collective-permute-start | bytes 884744 | tf_op jit(solution)/shard_map/ppermute | solution.py:831

commit v7 on v5

--- a/solution.py
+++ b/solution.py
@@ -142,7 +142,7 @@
         acc[...] += functools.reduce(jnp.add, grams)
         sums[1:2] += functools.reduce(jnp.add, totals)
 
-    def convolve():
+    def convolve(initial):
         blank = jnp.zeros((1, width, cin), BF16)
         shift = sums[2:3]
         moved = []
@@ -152,9 +152,8 @@
             pre = paired_rows(padded, wts, cout)
             pre_out[image] = pre
             mid = pre[1 : rows - 1].reshape(inner, cout)
-            if index == 0:
-                mean = jnp.sum(mid, axis=0, keepdims=True) / inner
-                shift = jnp.where(step == 0, mean, shift)
+            if initial and index == 0:
+                shift = jnp.sum(mid, axis=0, keepdims=True) / inner
                 sums[2:3] = shift
             delta = mid - shift
             high, low = split(delta)
@@ -180,7 +179,7 @@
             wts[index * cin : (index + 1) * cin, cout:] = two
         acc[...] = jnp.zeros_like(acc)
         sums[...] = jnp.zeros_like(sums)
-        convolve()
+        convolve(True)
 
     @pl.when(step > 0)
     def _():
@@ -188,7 +187,7 @@
             map_copy(step * many + index).wait()
             up_copy((step - 1) * many + index).wait()
         gather(step - 1)
-        convolve()
+        convolve(False)
 
     @pl.when(step == last)
     def _():
@@ -355,16 +354,22 @@
     middle = functools.reduce(jnp.add, tiles[2:rows])
     outer = ((0, 1), (1, rows), (rows, rows + 1))
     totals = jnp.concatenate([middle + tiles[one] + tiles[two] for one, two in outer], axis=0)
-    return dot(left, right), totals
+    return left, right, totals
 
 
 def moment_kernel(first, count, *refs):
     acc, maps = refs[-2:]
     found = [image_moments(first + index, *refs[:8]) for index in range(count)]
+    product = dot(
+        jnp.concatenate([left for left, _, _ in found], axis=1),
+        jnp.concatenate([right for _, right, _ in found], axis=0),
+    )
+    totals = functools.reduce(jnp.add, [part for _, _, part in found])
     if len(refs) == 12:
-        found.append((refs[8][...], refs[9][...]))
-    acc[...] = functools.reduce(jnp.add, [product for product, _ in found])
-    maps[...] = functools.reduce(jnp.add, [totals for _, totals in found])
+        product = refs[8][...] + product
+        totals = refs[9][...] + totals
+    acc[...] = product
+    maps[...] = totals
 
 
 def whitening_kernel(

time: 78.1 us -> 78.1 us (level)
  no operation moved by 1% of the time
where the time goes in v7:
time: 78.1 us; the launch traced here: 77.9 us
  Pallas kernels  38.9 us (50%)
  starting transfers between devices  20.7 us (27%)
  waiting for transfers between devices  17.2 us (22%)
  between operations  1.04 us (1%)
    ppermute x15, waiting for transfers between devices, exchange(): return lax.ppermute(value, AXES, pairs)  17.1 us
    ppermute x15, starting transfers between devices, exchange(): return lax.ppermute(value, AXES, pairs)  16.6 us
    pallas_call x5, Pallas kernels, image_gradient(): pl.pallas_call(functools.partial(image_kernel, first), grid=(count,), in_...  9.09 us
    pallas_call x4, Pallas kernels, moments(): pl.pallas_call(functools.partial(moment_kernel, first, count), in_specs=[...  8.97 us
    pallas_call x1, Pallas kernels, forward(): pl.pallas_call(functools.partial(forward_kernel, many), grid=(count // ma...  6.12 us
    ppermute x2, starting transfers between devices, halos(): lax.ppermute(across, AXES, pairs[1])  3.64 us
    pallas_call x1, Pallas kernels, painted(): pl.pallas_call(paint_kernel, grid=(count,), in_specs=[resident()] * 5, ou...  3.41 us
    pallas_call x1, Pallas kernels, whitened(): pl.pallas_call(functools.partial(whitening_kernel, total_pix, stage), in_...  3.22 us
  transfers between devices with their start and end apart: 19, of which 13 were waited for; matrix products, arithmetic and copies ran while one was open for 0% of the time, Pallas kernels for 41%

profile of v7, /device:TPU:0, one launch (start us, length us, event | category | flops | bytes accessed | tf_op | source)
XLA Modules:
  0.0 77.9 jit_solution(5920228601966298175)
XLA Ops:
  0.6 1.7 %edge_rows.1 = (bf16[6,1,128,256]{3,2,1,0:T(8,128)(2,1)S(1)}, bf16[6,1,128,256]{3,2,1,0:T(8,128)(2,1)S(1)}, bf16[3,3,256,128]{3,2,1,0:T(8,128)(2,1)S(1)}, bf16[6,8,128,256]{3,2,1,0:T(8,128)(2,1)S(1)}) custom-call(bf16[6,8,128,256]{3,2,1,0:T(8,128)(2,1)} %img.1, bf16[3,3,256,128]{3,2,1,0:T(8,128)(2,1)} %kern.1), custom_call_target="tpu_custom_call" | custom-call | tf_op jit(solution)/shard_map/edge_rows/pallas_call | solution.py:761
  2.9 2.6 %collective-permute-start.1 = (bf16[6,1,128,256]{3,2,1,0:T(8,128)(2,1)S(1)}, bf16[6,1,128,256]{3,2,1,0:T(8,128)(2,1)S(1)}, u32[]{:S(2)}, u32[]{:S(2)}) collective-permute-start(bf16[6,1,128,256]{3,2,1,0:T(8,128)(2,1)S(1)} %get-tuple-element.168), channel_id=1, source_target_pairs={{0,8},{1,2},{2,1},{3,11},{4,12},{5,6},{6,5},{7,15},{8,0},{9,10},{1... | collective-permute-start | bytes 1179656 | tf_op jit(solution)/shard_map/ppermute | solution.py:831
  5.5 6.1 %forward_inner.1 = (f32[6,8,128,128]{3,2,1,0:T(8,128)S(1)}, f32[256,256]{1,0:T(8,128)S(1)}, f32[8,128]{1,0:T(8,128)S(1)}, bf16[6,8,128,256]{3,2,1,0:T(8,128)(2,1)S(1)}, bf16[6,8,128,128]{3,2,1,0:T(8,128)(2,1)S(1)}) custom-call(bf16[6,8,128,256]{3,2,1,0:T(8,128)(2,1)S(1)} %get-tuple-element.169.first, ...), custom_call_target="tpu_custom_call", output_to_operand_aliasing={{3}: (0, {})} | custom-call | flops 3623878656 | bytes 7864320 | tf_op jit(solution)/shard_map/forward_inner/pallas_call | solution.py:572
  14.0 1.5 %collective-permute-start.3 = (f32[72,128]{1,0:T(8,128)S(1)}, f32[72,128]{1,0:T(8,128)S(1)}, u32[]{:S(2)}, u32[]{:S(2)}) collective-permute-start(f32[72,128]{1,0:T(8,128)S(1)} %add.21), channel_id=1, source_target_pairs={{0,4},{1,3},{2,6},{3,1},{4,0},{5,7},{6,2},{7,5},{8,12},{9,11},{10,... | collective-permute-start | bytes 110600 | tf_op jit(solution)/shard_map/ppermute | solution.py:836
  15.6 1.5 %moments.4 = (f32[768,768]{1,0:T(8,128)S(1)}, f32[768,128]{1,0:T(8,128)S(1)}) custom-call(f32[6,8,128,128]{3,2,1,0:T(8,128)S(1)} %get-tuple-element.272.pre.refs_0_, f32[6,1,128,128]{3,2,1,0:T(8,128)S(1)} %get-tuple-element.273.refs_1_.low, f32[6,1,128,128]{3,2,1,0:T(8,128)S(1)} %get-tuple-element.274.refs_2_.high, ...), custom_call_target="tpu_custom_call" | custom-call | flops 1207959552 | bytes 8388608 | tf_op jit(solution)/shard_map/moments/pallas_call | solution.py:621
  19.3 2.9 %moments.5 = (f32[768,768]{1,0:T(8,128)S(1)}, f32[768,128]{1,0:T(8,128)S(1)}) custom-call(f32[6,8,128,128]{3,2,1,0:T(8,128)S(1)} %get-tuple-element.272.pre.refs_0_, f32[6,1,128,128]{3,2,1,0:T(8,128)S(1)} %get-tuple-element.273.refs_1_.low, f32[6,1,128,128]{3,2,1,0:T(8,128)S(1)} %get-tuple-element.274.refs_2_.high, ...), custom_call_target="tpu_custom_call", output_to_operand_aliasing={{0}: (8, {}), {1}: (9, {})} | custom-call | flops 2415919104 | bytes 8388608 | tf_op jit(solution)/shard_map/moments/pallas_call | solution.py:621
  23.6 2.9 %moments.6 = (f32[768,768]{1,0:T(8,128)S(1)}, f32[768,128]{1,0:T(8,128)S(1)}) custom-call(f32[6,8,128,128]{3,2,1,0:T(8,128)S(1)} %get-tuple-element.272.pre.refs_0_, f32[6,1,128,128]{3,2,1,0:T(8,128)S(1)} %get-tuple-element.273.refs_1_.low, f32[6,1,128,128]{3,2,1,0:T(8,128)S(1)} %get-tuple-element.274.refs_2_.high, ...), custom_call_target="tpu_custom_call", output_to_operand_aliasing={{0}: (8, {}), {1}: (9, {})} | custom-call | flops 2415919104 | bytes 8388608 | tf_op jit(solution)/shard_map/moments/pallas_call | solution.py:621
  26.6 2.7 %collective-permute-start.6 = (f32[72,128]{1,0:T(8,128)S(1)}, f32[72,128]{1,0:T(8,128)S(1)}, u32[]{:S(2)}, u32[]{:S(2)}) collective-permute-start(f32[72,128]{1,0:T(8,128)S(1)} %add.24), channel_id=1, source_target_pairs={{0,16},{1,17},{2,18},{3,19},{4,20},{5,21},{6,22},{7,23},{8,24},{9,... | collective-permute-start | bytes 110600 | tf_op jit(solution)/shard_map/ppermute | solution.py:836
  29.3 1.6 %moments.7 = (f32[768,768]{1,0:T(8,128)S(1)}, f32[768,128]{1,0:T(8,128)S(1)}) custom-call(f32[6,8,128,128]{3,2,1,0:T(8,128)S(1)} %get-tuple-element.272.pre.refs_0_, f32[6,1,128,128]{3,2,1,0:T(8,128)S(1)} %get-tuple-element.273.refs_1_.low, f32[6,1,128,128]{3,2,1,0:T(8,128)S(1)} %get-tuple-element.274.refs_2_.high, ...), custom_call_target="tpu_custom_call", output_to_operand_aliasing={{0}: (8, {}), {1}: (9, {})} | custom-call | flops 1207959552 | bytes 8388608 | tf_op jit(solution)/shard_map/moments/pallas_call | solution.py:621
  32.8 3.2 %whitening.1 = (f32[1152,128]{1,0:T(8,128)S(1)}, f32[1152,128]{1,0:T(8,128)S(1)}, f32[2,64,64]{2,1,0:T(8,128)}, bf16[384,256]{1,0:T(8,128)(2,1)S(1)}, bf16[256,2...) custom-call(f32[72,128]{1,0:T(8,128)S(1)} %add.25.own, f32[72,128]{1,0:T(8,128)S(1)} %collective-permute-done.7.other, ...), custom_call_target="tpu_custom_call" | custom-call | flops 603979776 | bytes 8388608 | tf_op jit(solution)/shard_map/whitening/pallas_call | solution.py:650
  38.1 1.6 %collective-permute-start.9 = (f32[576,128]{1,0:T(8,128)S(1)}, f32[576,128]{1,0:T(8,128)S(1)}, u32[]{:S(2)}, u32[]{:S(2)}) collective-permute-start(f32[576,128]{1,0:T(8,128)S(1)} %get-tuple-element.261), channel_id=1, source_target_pairs={{0,4},{1,3},{2,6},{3,1},{4,0},{5,7},{6,2},{7,5},{8,12},{9,11},{10,... | collective-permute-start | bytes 884744 | tf_op jit(solution)/shard_map/ppermute | solution.py:836
  40.6 2.6 %pre_gradient.1.pre_grad = bf16[6,8,128,128]{3,2,1,0:T(8,128)(2,1)S(1)} custom-call(f32[6,8,128,128]{3,2,1,0:T(8,128)S(1)} %get-tuple-element.272.pre.refs_0_, f32[6,1,128,128]{3,2,1,0:T(8,128)S(1)} %get-tuple-element.273.refs_1_.low, f32[6,1,128,128]{3,2,1,0:T(8,128)S(1)} %get-tuple-element.274.refs_2_.high, ...), custom_call_target="tpu_custom_call" | custom-call | flops 1207959552 | bytes 6291456 | tf_op jit(solution)/shard_map/pre_gradient/pallas_call | solution.py:677
  43.2 1.6 %collective-permute-done.9.received = f32[576,128]{1,0:T(8,128)S(1)} collective-permute-done((f32[576,128]{1,0:T(8,128)S(1)}, f32[576,128]{1,0:T(8,128)S(1)}, u32[]{:S(2)}, u32[]{:S(2)}) %collective-permute-start.9) | collective-permute-done | bytes 294944 | tf_op jit(solution)/shard_map/ppermute | solution.py:836
  46.0 3.4 %colored.1 = bf16[6,8,128,128]{3,2,1,0:T(8,128)(2,1)} custom-call(f32[6,8,128,128]{3,2,1,0:T(8,128)S(1)} %get-tuple-element.272.pre.refs_0_, f32[6,1,128,128]{3,2,1,0:T(8,128)S(1)} %get-tuple-element.273.refs_1_.low, f32[6,1,128,128]{3,2,1,0:T(8,128)S(1)} %get-tuple-element.274.refs_2_.high, bf16[256,256]{1,0:T(8,128)(2,1)S(1)} %get-tuple-element.275.paint, ...), custom_call_target="tpu_custom_call" | custom-call | flops 805306368 | bytes 4718592 | tf_op jit(solution)/shard_map/colored/pallas_call | solution.py:695
  51.2 1.6 %image_gradient.5.rest_0_ = bf16[6,8,128,256]{3,2,1,0:T(8,128)(2,1)} custom-call(bf16[6,8,128,128]{3,2,1,0:T(8,128)(2,1)S(1)} %pre_gradient.1.pre_grad, bf16[6,1,128,128]{3,2,1,0:T(8,128)(2,1)S(1)} %collective-permute-done.11.ahead, bf16[6,1,128,128]{3,2,1,0:T(8,128)(2,1)S(1)} %collective-permute-done.12.across, bf16[1152,256]{1,0:T(8,128)(2,1)S(1)} %turned_weights.1.wts), custom_call_target="tpu_custom_call" | custom-call | flops 603979776 | bytes 786432 | tf_op jit(solution)/shard_map/image_gradient/pallas_call | solution.py:736
  52.9 1.7 %collective-permute-done.13 = f32[144,128]{1,0:T(8,128)S(1)} collective-permute-done((f32[144,128]{1,0:T(8,128)S(1)}, f32[144,128]{1,0:T(8,128)S(1)}, u32[]{:S(2)}, u32[]{:S(2)}) %collective-permute-start.13) | collective-permute-done | bytes 73760 | tf_op jit(solution)/shard_map/ppermute | solution.py:836
  54.6 2.7 %collective-permute-start.14 = (f32[144,128]{1,0:T(8,128)S(1)}, f32[144,128]{1,0:T(8,128)S(1)}, u32[]{:S(2)}, u32[]{:S(2)}) collective-permute-start(f32[144,128]{1,0:T(8,128)S(1)} %add.26), channel_id=1, source_target_pairs={{0,16},{1,17},{2,18},{3,19},{4,20},{5,21},{6,22},{7,23},{8,24},{9,... | collective-permute-start | bytes 221192 | tf_op jit(solution)/shard_map/ppermute | solution.py:836
  57.2 1.6 %image_gradient.6.rest_0_ = bf16[6,8,128,256]{3,2,1,0:T(8,128)(2,1)} custom-call(bf16[6,8,128,128]{3,2,1,0:T(8,128)(2,1)S(1)} %pre_gradient.1.pre_grad, bf16[6,1,128,128]{3,2,1,0:T(8,128)(2,1)S(1)} %collective-permute-done.11.ahead, bf16[6,1,128,128]{3,2,1,0:T(8,128)(2,1)S(1)} %collective-permute-done.12.across, ...), custom_call_target="tpu_custom_call", output_to_operand_aliasing={{}: (4, {})} | custom-call | flops 603979776 | bytes 786432 | tf_op jit(solution)/shard_map/image_gradient/pallas_call | solution.py:736
  58.9 1.8 %collective-permute-done.14 = f32[144,128]{1,0:T(8,128)S(1)} collective-permute-done((f32[144,128]{1,0:T(8,128)S(1)}, f32[144,128]{1,0:T(8,128)S(1)}, u32[]{:S(2)}, u32[]{:S(2)}) %collective-permute-start.14) | collective-permute-done | bytes 73760 | tf_op jit(solution)/shard_map/ppermute | solution.py:836
  61.1 1.6 %image_gradient.7.rest_0_ = bf16[6,8,128,256]{3,2,1,0:T(8,128)(2,1)} custom-call(bf16[6,8,128,128]{3,2,1,0:T(8,128)(2,1)S(1)} %pre_gradient.1.pre_grad, bf16[6,1,128,128]{3,2,1,0:T(8,128)(2,1)S(1)} %collective-permute-done.11.ahead, bf16[6,1,128,128]{3,2,1,0:T(8,128)(2,1)S(1)} %collective-permute-done.12.across, ...), custom_call_target="tpu_custom_call", output_to_operand_aliasing={{}: (4, {})} | custom-call | flops 603979776 | bytes 786432 | tf_op jit(solution)/shard_map/image_gradient/pallas_call | solution.py:736
  62.7 2.0 %collective-permute-done.15.received = bf16[144,128]{1,0:T(8,128)(2,1)S(1)} collective-permute-done((bf16[144,128]{1,0:T(8,128)(2,1)S(1)}, bf16[144,128]{1,0:T(8,128)(2,1)S(1)}, u32[]{:S(2)}, u32[]{:S(2)}) %collective-permute-start.15) | collective-permute-done | bytes 36896 | tf_op jit(solution)/shard_map/ppermute | solution.py:836
  65.9 1.6 %image_gradient.8.rest_0_ = bf16[6,8,128,256]{3,2,1,0:T(8,128)(2,1)} custom-call(bf16[6,8,128,128]{3,2,1,0:T(8,128)(2,1)S(1)} %pre_gradient.1.pre_grad, bf16[6,1,128,128]{3,2,1,0:T(8,128)(2,1)S(1)} %collective-permute-done.11.ahead, bf16[6,1,128,128]{3,2,1,0:T(8,128)(2,1)S(1)} %collective-permute-done.12.across, ...), custom_call_target="tpu_custom_call", output_to_operand_aliasing={{}: (4, {})} | custom-call | flops 603979776 | bytes 786432 | tf_op jit(solution)/shard_map/image_gradient/pallas_call | solution.py:736
  67.6 2.3 %collective-permute-done.16.received = bf16[288,128]{1,0:T(8,128)(2,1)S(1)} collective-permute-done((bf16[288,128]{1,0:T(8,128)(2,1)S(1)}, bf16[288,128]{1,0:T(8,128)(2,1)S(1)}, u32[]{:S(2)}, u32[]{:S(2)}) %collective-permute-start.16) | collective-permute-done | bytes 73760 | tf_op jit(solution)/shard_map/ppermute | solution.py:836
  71.3 2.5 %image_gradient.9 = bf16[6,8,128,256]{3,2,1,0:T(8,128)(2,1)} custom-call(bf16[6,8,128,128]{3,2,1,0:T(8,128)(2,1)S(1)} %pre_gradient.1.pre_grad, bf16[6,1,128,128]{3,2,1,0:T(8,128)(2,1)S(1)} %collective-permute-done.11.ahead, bf16[6,1,128,128]{3,2,1,0:T(8,128)(2,1)S(1)} %collective-permute-done.12.across, ...), custom_call_target="tpu_custom_call", output_to_operand_aliasing={{}: (4, {})} | custom-call | flops 1207959552 | bytes 1572864 | tf_op jit(solution)/shard_map/image_gradient/pallas_call | solution.py:736
  (50 shorter events, 21.2 us)
Async XLA Ops:
  2.3 9.3 %collective-permute-start = (bf16[6,1,128,256]{3,2,1,0:T(8,128)(2,1)S(1)}, bf16[6,1,128,256]{3,2,1,0:T(8,128)(2,1)S(1)}, u32[]{:S(2)}, u32[]{:S(2)}) collective-permute-start(bf16[6,1,128,256]{3,2,1,0:T(8,128)(2,1)S(1)} %get-tuple-element.167), channel_id=1, source_target_pairs={{0,1},{1,0},{2,3},{3,2},{4,5},{5,4},{6,7},{7,6},{8,9},{9,8},{10,11... | collective-permute-start | bytes 1179656 | tf_op jit(solution)/shard_map/ppermute | solution.py:831
  2.9 8.8 %collective-permute-start.1 = (bf16[6,1,128,256]{3,2,1,0:T(8,128)(2,1)S(1)}, bf16[6,1,128,256]{3,2,1,0:T(8,128)(2,1)S(1)}, u32[]{:S(2)}, u32[]{:S(2)}) collective-permute-start(bf16[6,1,128,256]{3,2,1,0:T(8,128)(2,1)S(1)} %get-tuple-element.168), channel_id=1, source_target_pairs={{0,8},{1,2},{2,1},{3,11},{4,12},{5,6},{6,5},{7,15},{8,0},{9,10},{1... | collective-permute-start | bytes 1179656 | tf_op jit(solution)/shard_map/ppermute | solution.py:831
  12.7 1.3 %collective-permute-start.2 = (f32[72,128]{1,0:T(8,128)S(1)}, f32[72,128]{1,0:T(8,128)S(1)}, u32[]{:S(2)}, u32[]{:S(2)}) collective-permute-start(f32[72,128]{1,0:T(8,128)S(1)} %get-tuple-element.176), channel_id=1, source_target_pairs={{0,1},{1,0},{2,3},{3,2},{4,5},{5,4},{6,7},{7,6},{8,9},{9,8},{10,11... | collective-permute-start | bytes 110600 | tf_op jit(solution)/shard_map/ppermute | solution.py:836
  14.0 4.0 %collective-permute-start.3 = (f32[72,128]{1,0:T(8,128)S(1)}, f32[72,128]{1,0:T(8,128)S(1)}, u32[]{:S(2)}, u32[]{:S(2)}) collective-permute-start(f32[72,128]{1,0:T(8,128)S(1)} %add.21), channel_id=1, source_target_pairs={{0,4},{1,3},{2,6},{3,1},{4,0},{5,7},{6,2},{7,5},{8,12},{9,11},{10,... | collective-permute-start | bytes 110600 | tf_op jit(solution)/shard_map/ppermute | solution.py:836
  18.0 4.3 %collective-permute-start.4 = (f32[72,128]{1,0:T(8,128)S(1)}, f32[72,128]{1,0:T(8,128)S(1)}, u32[]{:S(2)}, u32[]{:S(2)}) collective-permute-start(f32[72,128]{1,0:T(8,128)S(1)} %add.22), channel_id=1, source_target_pairs={{0,2},{1,5},{2,0},{3,7},{4,6},{5,1},{6,4},{7,3},{8,10},{9,13},{10,... | collective-permute-start | bytes 110600 | tf_op jit(solution)/shard_map/ppermute | solution.py:836
  22.3 4.3 %collective-permute-start.5 = (f32[72,128]{1,0:T(8,128)S(1)}, f32[72,128]{1,0:T(8,128)S(1)}, u32[]{:S(2)}, u32[]{:S(2)}) collective-permute-start(f32[72,128]{1,0:T(8,128)S(1)} %add.23), channel_id=1, source_target_pairs={{0,8},{1,9},{2,10},{3,11},{4,12},{5,13},{6,14},{7,15},{8,0},{9,1},... | collective-permute-start | bytes 110600 | tf_op jit(solution)/shard_map/ppermute | solution.py:836
  26.6 6.2 %copy-start = (f32[2,64,64]{2,1,0:T(8,128)S(1)}, f32[2,64,64]{2,1,0:T(8,128)}, u32[]{:S(2)}) copy-start(f32[2,64,64]{2,1,0:T(8,128)} %colors.1) | copy-start | bytes 98308
  26.6 6.2 %copy-start.1 = (f32[128]{0:T(128)S(1)}, f32[128]{0:T(128)}, u32[]{:S(2)}) copy-start(f32[128]{0:T(128)} %param.8) | copy-start | bytes 1540
  26.6 4.9 %collective-permute-start.6 = (f32[72,128]{1,0:T(8,128)S(1)}, f32[72,128]{1,0:T(8,128)S(1)}, u32[]{:S(2)}, u32[]{:S(2)}) collective-permute-start(f32[72,128]{1,0:T(8,128)S(1)} %add.24), channel_id=1, source_target_pairs={{0,16},{1,17},{2,18},{3,19},{4,20},{5,21},{6,22},{7,23},{8,24},{9,... | collective-permute-start | bytes 110600 | tf_op jit(solution)/shard_map/ppermute | solution.py:836
  31.5 1.2 %collective-permute-start.7 = (f32[72,128]{1,0:T(8,128)S(1)}, f32[72,128]{1,0:T(8,128)S(1)}, u32[]{:S(2)}, u32[]{:S(2)}) collective-permute-start(f32[72,128]{1,0:T(8,128)S(1)} %add.25.own), channel_id=1, source_target_pairs={{0,1},{1,0},{2,3},{3,2},{4,5},{5,4},{6,7},{7,6},{8,9},{9,8},{10,11... | collective-permute-start | bytes 110600 | tf_op jit(solution)/shard_map/ppermute | solution.py:836
  36.0 2.0 %collective-permute-start.8 = (f32[1152,128]{1,0:T(8,128)S(1)}, f32[1152,128]{1,0:T(8,128)S(1)}, u32[]{:S(2)}, u32[]{:S(2)}) collective-permute-start(f32[1152,128]{1,0:T(8,128)S(1)} %get-tuple-element.246), channel_id=1, source_target_pairs={{0,1},{1,0},{2,3},{3,2},{4,5},{5,4},{6,7},{7,6},{8,9},{9,8},{10,11... | collective-permute-start | bytes 1769480 | tf_op jit(solution)/shard_map/ppermute | solution.py:836
  38.1 6.8 %collective-permute-start.9 = (f32[576,128]{1,0:T(8,128)S(1)}, f32[576,128]{1,0:T(8,128)S(1)}, u32[]{:S(2)}, u32[]{:S(2)}) collective-permute-start(f32[576,128]{1,0:T(8,128)S(1)} %get-tuple-element.261), channel_id=1, source_target_pairs={{0,4},{1,3},{2,6},{3,1},{4,0},{5,7},{6,2},{7,5},{8,12},{9,11},{10,... | collective-permute-start | bytes 884744 | tf_op jit(solution)/shard_map/ppermute | solution.py:836
  39.6 10.5 %collective-permute-start.11 = (bf16[6,1,128,128]{3,2,1,0:T(8,128)(2,1)S(1)}, bf16[6,1,128,128]{3,2,1,0:T(8,128)(2,1)S(1)}, u32[]{:S(2)}, u32[]{:S(2)}) collective-permute-start(bf16[6,1,128,128]{3,2,1,0:T(8,128)(2,1)S(1)} %get-tuple-element.283), channel_id=1, source_target_pairs={{0,1},{1,0},{2,3},{3,2},{4,5},{5,4},{6,7},{7,6},{8,9},{9,8},{10,11... | collective-permute-start | bytes 589832 | tf_op jit(solution)/shard_map/ppermute | solution.py:831
  39.6 10.5 %collective-permute-start.12 = (bf16[6,1,128,128]{3,2,1,0:T(8,128)(2,1)S(1)}, bf16[6,1,128,128]{3,2,1,0:T(8,128)(2,1)S(1)}, u32[]{:S(2)}, u32[]{:S(2)}) collective-permute-start(bf16[6,1,128,128]{3,2,1,0:T(8,128)(2,1)S(1)} %get-tuple-element.284), channel_id=1, source_target_pairs={{0,8},{1,2},{2,1},{3,11},{4,12},{5,6},{6,5},{7,15},{8,0},{9,10},{1... | collective-permute-start | bytes 589832 | tf_op jit(solution)/shard_map/ppermute | solution.py:831
  44.9 5.2 %collective-permute-start.10 = (f32[288,128]{1,0:T(8,128)S(1)}, f32[288,128]{1,0:T(8,128)S(1)}, u32[]{:S(2)}, u32[]{:S(2)}) collective-permute-start(f32[288,128]{1,0:T(8,128)S(1)} %get-tuple-element.271), channel_id=1, source_target_pairs={{0,2},{1,5},{2,0},{3,7},{4,6},{5,1},{6,4},{7,3},{8,10},{9,13},{10,... | collective-permute-start | bytes 442376 | tf_op jit(solution)/shard_map/ppermute | solution.py:836
  50.2 4.4 %collective-permute-start.13 = (f32[144,128]{1,0:T(8,128)S(1)}, f32[144,128]{1,0:T(8,128)S(1)}, u32[]{:S(2)}, u32[]{:S(2)}) collective-permute-start(f32[144,128]{1,0:T(8,128)S(1)} %get-tuple-element.286), channel_id=1, source_target_pairs={{0,8},{1,9},{2,10},{3,11},{4,12},{5,13},{6,14},{7,15},{8,0},{9,1},... | collective-permute-start | bytes 221192 | tf_op jit(solution)/shard_map/ppermute | solution.py:836
  54.6 6.1 %collective-permute-start.14 = (f32[144,128]{1,0:T(8,128)S(1)}, f32[144,128]{1,0:T(8,128)S(1)}, u32[]{:S(2)}, u32[]{:S(2)}) collective-permute-start(f32[144,128]{1,0:T(8,128)S(1)} %add.26), channel_id=1, source_target_pairs={{0,16},{1,17},{2,18},{3,19},{4,20},{5,21},{6,22},{7,23},{8,24},{9,... | collective-permute-start | bytes 221192 | tf_op jit(solution)/shard_map/ppermute | solution.py:836
  60.7 4.0 %collective-permute-start.15 = (bf16[144,128]{1,0:T(8,128)(2,1)S(1)}, bf16[144,128]{1,0:T(8,128)(2,1)S(1)}, u32[]{:S(2)}, u32[]{:S(2)}) collective-permute-start(bf16[144,128]{1,0:T(8,128)(2,1)S(1)} %add_convert_fusion.value), channel_id=1, source_target_pairs={{0,8},{1,9},{2,10},{3,11},{4,12},{5,13},{6,14},{7,15},{8,0},{9,1},... | collective-permute-start | bytes 110600 | tf_op jit(solution)/shard_map/ppermute | solution.py:836
  64.8 5.2 %collective-permute-start.16 = (bf16[288,128]{1,0:T(8,128)(2,1)S(1)}, bf16[288,128]{1,0:T(8,128)(2,1)S(1)}, u32[]{:S(2)}, u32[]{:S(2)}) collective-permute-start(bf16[288,128]{1,0:T(8,128)(2,1)S(1)} %join.3.value), channel_id=1, source_target_pairs={{0,2},{1,5},{2,0},{3,7},{4,6},{5,1},{6,4},{7,3},{8,10},{9,13},{10,... | collective-permute-start | bytes 221192 | tf_op jit(solution)/shard_map/ppermute | solution.py:836
  70.0 5.2 %collective-permute-start.17 = (bf16[576,128]{1,0:T(8,128)(2,1)S(1)}, bf16[576,128]{1,0:T(8,128)(2,1)S(1)}, u32[]{:S(2)}, u32[]{:S(2)}) collective-permute-start(bf16[576,128]{1,0:T(8,128)(2,1)S(1)} %join.4.value), channel_id=1, source_target_pairs={{0,4},{1,3},{2,6},{3,1},{4,0},{5,7},{6,2},{7,5},{8,12},{9,11},{10,... | collective-permute-start | bytes 442376 | tf_op jit(solution)/shard_map/ppermute | solution.py:836
  75.2 1.6 %collective-permute-start.18 = (bf16[1152,128]{1,0:T(8,128)(2,1)S(1)}, bf16[1152,128]{1,0:T(8,128)(2,1)S(1)}, u32[]{:S(2)}, u32[]{:S(2)}) collective-permute-start(bf16[1152,128]{1,0:T(8,128)(2,1)S(1)} %join.5.value), channel_id=1, source_target_pairs={{0,1},{1,0},{2,3},{3,2},{4,5},{5,4},{6,7},{7,6},{8,9},{9,8},{10,11... | collective-permute-start | bytes 884744 | tf_op jit(solution)/shard_map/ppermute | solution.py:836

commit v8 on v7

--- a/solution.py
+++ b/solution.py
@@ -235,21 +235,18 @@
     top, bot = sides(ahead[...], across[...])
     pixels = count * width
     shape = (count, width, cout)
-    edges = []
+    shift = sums[2:3]
+    gram, moved, up_sum = acc[...], sums[0:1], sums[1:2]
     for a, source, row, out in ((0, top, 0, low), (2, bot, last, high)):
         taps = jnp.concatenate([kern[a, c] for c in range(3)], axis=1)
         value = merged(dot(source.reshape(pixels, cin), taps), shape) + pre[:, row]
         out[:, 0] = value
-        edges.append(value.reshape(pixels, cout))
-    shift = sums[2:3]
-    delta = jnp.concatenate(edges, axis=0) - shift
-    up = jnp.concatenate(
-        [ups[:, 0].reshape(pixels, cout), ups[:, last].reshape(pixels, cout)], axis=0
-    )
-    big, small = split(delta)
-    gram = acc[...] + statistics(small, big, up)
-    moved = sums[0:1] + jnp.sum(delta, axis=0, keepdims=True)
-    up_sum = sums[1:2] + jnp.sum(up.astype(F32), axis=0, keepdims=True)
+        delta = value.reshape(pixels, cout) - shift
+        up = ups[:, row].reshape(pixels, cout)
+        big, small = split(delta)
+        gram = gram + statistics(small, big, up)
+        moved = moved + jnp.sum(delta, axis=0, keepdims=True)
+        up_sum = up_sum + jnp.sum(up.astype(F32), axis=0, keepdims=True)
     mixed = gram[:cout, :cout]
     square = gram[:cout, cout:] + mixed + mixed.T
     cross = gram[cout:, :cout] + gram[cout:, cout:]

time: 78.1 us -> 78.3 us (level)
  no operation moved by 1% of the time
where the time goes in v8:
time: 78.3 us; the launch traced here: 78.2 us
  Pallas kernels  39.2 us (50%)
  starting transfers between devices  20.6 us (26%)
  waiting for transfers between devices  17.3 us (22%)
  between operations  1.04 us (1%)
    ppermute x15, waiting for transfers between devices, exchange(): return lax.ppermute(value, AXES, pairs)  17.2 us
    ppermute x15, starting transfers between devices, exchange(): return lax.ppermute(value, AXES, pairs)  16.5 us
    pallas_call x5, Pallas kernels, image_gradient(): pl.pallas_call(functools.partial(image_kernel, first), grid=(count,), in_...  9.09 us
    pallas_call x4, Pallas kernels, moments(): pl.pallas_call(functools.partial(moment_kernel, first, count), in_specs=[...  8.98 us
    pallas_call x1, Pallas kernels, forward(): pl.pallas_call(functools.partial(forward_kernel, many), grid=(count // ma...  6.12 us
    ppermute x2, starting transfers between devices, halos(): lax.ppermute(across, AXES, pairs[1])  3.64 us
    pallas_call x1, Pallas kernels, painted(): pl.pallas_call(paint_kernel, grid=(count,), in_specs=[resident()] * 5, ou...  3.41 us
    pallas_call x1, Pallas kernels, whitened(): pl.pallas_call(functools.partial(whitening_kernel, total_pix, stage), in_...  3.23 us
  transfers between devices with their start and end apart: 19, of which 13 were waited for; matrix products, arithmetic and copies ran while one was open for 0% of the time, Pallas kernels for 41%

profile of v8, /device:TPU:0, one launch (start us, length us, event | category | flops | bytes accessed | tf_op | source)
XLA Modules:
  0.0 78.2 jit_solution(4221509957932258135)
XLA Ops:
  0.6 1.7 %edge_rows.1 = (bf16[6,1,128,256]{3,2,1,0:T(8,128)(2,1)S(1)}, bf16[6,1,128,256]{3,2,1,0:T(8,128)(2,1)S(1)}, bf16[3,3,256,128]{3,2,1,0:T(8,128)(2,1)S(1)}, bf16[6,8,128,256]{3,2,1,0:T(8,128)(2,1)S(1)}) custom-call(bf16[6,8,128,256]{3,2,1,0:T(8,128)(2,1)} %img.1, bf16[3,3,256,128]{3,2,1,0:T(8,128)(2,1)} %kern.1), custom_call_target="tpu_custom_call" | custom-call | tf_op jit(solution)/shard_map/edge_rows/pallas_call | solution.py:758
  2.9 2.6 %collective-permute-start.1 = (bf16[6,1,128,256]{3,2,1,0:T(8,128)(2,1)S(1)}, bf16[6,1,128,256]{3,2,1,0:T(8,128)(2,1)S(1)}, u32[]{:S(2)}, u32[]{:S(2)}) collective-permute-start(bf16[6,1,128,256]{3,2,1,0:T(8,128)(2,1)S(1)} %get-tuple-element.168), channel_id=1, source_target_pairs={{0,8},{1,2},{2,1},{3,11},{4,12},{5,6},{6,5},{7,15},{8,0},{9,10},{1... | collective-permute-start | bytes 1179656 | tf_op jit(solution)/shard_map/ppermute | solution.py:828
  5.5 6.1 %forward_inner.1 = (f32[6,8,128,128]{3,2,1,0:T(8,128)S(1)}, f32[256,256]{1,0:T(8,128)S(1)}, f32[8,128]{1,0:T(8,128)S(1)}, bf16[6,8,128,256]{3,2,1,0:T(8,128)(2,1)S(1)}, bf16[6,8,128,128]{3,2,1,0:T(8,128)(2,1)S(1)}) custom-call(bf16[6,8,128,256]{3,2,1,0:T(8,128)(2,1)S(1)} %get-tuple-element.169.first, ...), custom_call_target="tpu_custom_call", output_to_operand_aliasing={{3}: (0, {})} | custom-call | flops 3623878656 | bytes 7864320 | tf_op jit(solution)/shard_map/forward_inner/pallas_call | solution.py:569
  14.3 1.5 %collective-permute-start.3 = (f32[72,128]{1,0:T(8,128)S(1)}, f32[72,128]{1,0:T(8,128)S(1)}, u32[]{:S(2)}, u32[]{:S(2)}) collective-permute-start(f32[72,128]{1,0:T(8,128)S(1)} %add.21), channel_id=1, source_target_pairs={{0,4},{1,3},{2,6},{3,1},{4,0},{5,7},{6,2},{7,5},{8,12},{9,11},{10,... | collective-permute-start | bytes 110600 | tf_op jit(solution)/shard_map/ppermute | solution.py:833
  15.8 1.5 %moments.4 = (f32[768,768]{1,0:T(8,128)S(1)}, f32[768,128]{1,0:T(8,128)S(1)}) custom-call(f32[6,8,128,128]{3,2,1,0:T(8,128)S(1)} %get-tuple-element.272.pre.refs_0_, f32[6,1,128,128]{3,2,1,0:T(8,128)S(1)} %get-tuple-element.273.refs_1_.low, f32[6,1,128,128]{3,2,1,0:T(8,128)S(1)} %get-tuple-element.274.refs_2_.high, ...), custom_call_target="tpu_custom_call" | custom-call | flops 1207959552 | bytes 8388608 | tf_op jit(solution)/shard_map/moments/pallas_call | solution.py:618
  19.5 2.9 %moments.5 = (f32[768,768]{1,0:T(8,128)S(1)}, f32[768,128]{1,0:T(8,128)S(1)}) custom-call(f32[6,8,128,128]{3,2,1,0:T(8,128)S(1)} %get-tuple-element.272.pre.refs_0_, f32[6,1,128,128]{3,2,1,0:T(8,128)S(1)} %get-tuple-element.273.refs_1_.low, f32[6,1,128,128]{3,2,1,0:T(8,128)S(1)} %get-tuple-element.274.refs_2_.high, ...), custom_call_target="tpu_custom_call", output_to_operand_aliasing={{0}: (8, {}), {1}: (9, {})} | custom-call | flops 2415919104 | bytes 8388608 | tf_op jit(solution)/shard_map/moments/pallas_call | solution.py:618
  23.9 2.9 %moments.6 = (f32[768,768]{1,0:T(8,128)S(1)}, f32[768,128]{1,0:T(8,128)S(1)}) custom-call(f32[6,8,128,128]{3,2,1,0:T(8,128)S(1)} %get-tuple-element.272.pre.refs_0_, f32[6,1,128,128]{3,2,1,0:T(8,128)S(1)} %get-tuple-element.273.refs_1_.low, f32[6,1,128,128]{3,2,1,0:T(8,128)S(1)} %get-tuple-element.274.refs_2_.high, ...), custom_call_target="tpu_custom_call", output_to_operand_aliasing={{0}: (8, {}), {1}: (9, {})} | custom-call | flops 2415919104 | bytes 8388608 | tf_op jit(solution)/shard_map/moments/pallas_call | solution.py:618
  26.8 2.7 %collective-permute-start.6 = (f32[72,128]{1,0:T(8,128)S(1)}, f32[72,128]{1,0:T(8,128)S(1)}, u32[]{:S(2)}, u32[]{:S(2)}) collective-permute-start(f32[72,128]{1,0:T(8,128)S(1)} %add.24), channel_id=1, source_target_pairs={{0,16},{1,17},{2,18},{3,19},{4,20},{5,21},{6,22},{7,23},{8,24},{9,... | collective-permute-start | bytes 110600 | tf_op jit(solution)/shard_map/ppermute | solution.py:833
  29.5 1.6 %moments.7 = (f32[768,768]{1,0:T(8,128)S(1)}, f32[768,128]{1,0:T(8,128)S(1)}) custom-call(f32[6,8,128,128]{3,2,1,0:T(8,128)S(1)} %get-tuple-element.272.pre.refs_0_, f32[6,1,128,128]{3,2,1,0:T(8,128)S(1)} %get-tuple-element.273.refs_1_.low, f32[6,1,128,128]{3,2,1,0:T(8,128)S(1)} %get-tuple-element.274.refs_2_.high, ...), custom_call_target="tpu_custom_call", output_to_operand_aliasing={{0}: (8, {}), {1}: (9, {})} | custom-call | flops 1207959552 | bytes 8388608 | tf_op jit(solution)/shard_map/moments/pallas_call | solution.py:618
  33.0 3.2 %whitening.1 = (f32[1152,128]{1,0:T(8,128)S(1)}, f32[1152,128]{1,0:T(8,128)S(1)}, f32[2,64,64]{2,1,0:T(8,128)}, bf16[384,256]{1,0:T(8,128)(2,1)S(1)}, bf16[256,2...) custom-call(f32[72,128]{1,0:T(8,128)S(1)} %add.25.own, f32[72,128]{1,0:T(8,128)S(1)} %collective-permute-done.7.other, ...), custom_call_target="tpu_custom_call" | custom-call | flops 603979776 | bytes 8388608 | tf_op jit(solution)/shard_map/whitening/pallas_call | solution.py:647
  38.3 1.6 %collective-permute-start.9 = (f32[576,128]{1,0:T(8,128)S(1)}, f32[576,128]{1,0:T(8,128)S(1)}, u32[]{:S(2)}, u32[]{:S(2)}) collective-permute-start(f32[576,128]{1,0:T(8,128)S(1)} %get-tuple-element.261), channel_id=1, source_target_pairs={{0,4},{1,3},{2,6},{3,1},{4,0},{5,7},{6,2},{7,5},{8,12},{9,11},{10,... | collective-permute-start | bytes 884744 | tf_op jit(solution)/shard_map/ppermute | solution.py:833
  40.8 2.6 %pre_gradient.1.pre_grad = bf16[6,8,128,128]{3,2,1,0:T(8,128)(2,1)S(1)} custom-call(f32[6,8,128,128]{3,2,1,0:T(8,128)S(1)} %get-tuple-element.272.pre.refs_0_, f32[6,1,128,128]{3,2,1,0:T(8,128)S(1)} %get-tuple-element.273.refs_1_.low, f32[6,1,128,128]{3,2,1,0:T(8,128)S(1)} %get-tuple-element.274.refs_2_.high, ...), custom_call_target="tpu_custom_call" | custom-call | flops 1207959552 | bytes 6291456 | tf_op jit(solution)/shard_map/pre_gradient/pallas_call | solution.py:674
  43.5 1.6 %collective-permute-done.9.received = f32[576,128]{1,0:T(8,128)S(1)} collective-permute-done((f32[576,128]{1,0:T(8,128)S(1)}, f32[576,128]{1,0:T(8,128)S(1)}, u32[]{:S(2)}, u32[]{:S(2)}) %collective-permute-start.9) | collective-permute-done | bytes 294944 | tf_op jit(solution)/shard_map/ppermute | solution.py:833
  46.3 3.4 %colored.1 = bf16[6,8,128,128]{3,2,1,0:T(8,128)(2,1)} custom-call(f32[6,8,128,128]{3,2,1,0:T(8,128)S(1)} %get-tuple-element.272.pre.refs_0_, f32[6,1,128,128]{3,2,1,0:T(8,128)S(1)} %get-tuple-element.273.refs_1_.low, f32[6,1,128,128]{3,2,1,0:T(8,128)S(1)} %get-tuple-element.274.refs_2_.high, bf16[256,256]{1,0:T(8,128)(2,1)S(1)} %get-tuple-element.275.paint, ...), custom_call_target="tpu_custom_call" | custom-call | flops 805306368 | bytes 4718592 | tf_op jit(solution)/shard_map/colored/pallas_call | solution.py:692
  51.4 1.6 %image_gradient.5.rest_0_ = bf16[6,8,128,256]{3,2,1,0:T(8,128)(2,1)} custom-call(bf16[6,8,128,128]{3,2,1,0:T(8,128)(2,1)S(1)} %pre_gradient.1.pre_grad, bf16[6,1,128,128]{3,2,1,0:T(8,128)(2,1)S(1)} %collective-permute-done.11.ahead, bf16[6,1,128,128]{3,2,1,0:T(8,128)(2,1)S(1)} %collective-permute-done.12.across, bf16[1152,256]{1,0:T(8,128)(2,1)S(1)} %turned_weights.1.wts), custom_call_target="tpu_custom_call" | custom-call | flops 603979776 | bytes 786432 | tf_op jit(solution)/shard_map/image_gradient/pallas_call | solution.py:733
  53.1 1.7 %collective-permute-done.13 = f32[144,128]{1,0:T(8,128)S(1)} collective-permute-done((f32[144,128]{1,0:T(8,128)S(1)}, f32[144,128]{1,0:T(8,128)S(1)}, u32[]{:S(2)}, u32[]{:S(2)}) %collective-permute-start.13) | collective-permute-done | bytes 73760 | tf_op jit(solution)/shard_map/ppermute | solution.py:833
  54.8 2.7 %collective-permute-start.14 = (f32[144,128]{1,0:T(8,128)S(1)}, f32[144,128]{1,0:T(8,128)S(1)}, u32[]{:S(2)}, u32[]{:S(2)}) collective-permute-start(f32[144,128]{1,0:T(8,128)S(1)} %add.26), channel_id=1, source_target_pairs={{0,16},{1,17},{2,18},{3,19},{4,20},{5,21},{6,22},{7,23},{8,24},{9,... | collective-permute-start | bytes 221192 | tf_op jit(solution)/shard_map/ppermute | solution.py:833
  57.5 1.6 %image_gradient.6.rest_0_ = bf16[6,8,128,256]{3,2,1,0:T(8,128)(2,1)} custom-call(bf16[6,8,128,128]{3,2,1,0:T(8,128)(2,1)S(1)} %pre_gradient.1.pre_grad, bf16[6,1,128,128]{3,2,1,0:T(8,128)(2,1)S(1)} %collective-permute-done.11.ahead, bf16[6,1,128,128]{3,2,1,0:T(8,128)(2,1)S(1)} %collective-permute-done.12.across, ...), custom_call_target="tpu_custom_call", output_to_operand_aliasing={{}: (4, {})} | custom-call | flops 603979776 | bytes 786432 | tf_op jit(solution)/shard_map/image_gradient/pallas_call | solution.py:733
  59.1 1.8 %collective-permute-done.14 = f32[144,128]{1,0:T(8,128)S(1)} collective-permute-done((f32[144,128]{1,0:T(8,128)S(1)}, f32[144,128]{1,0:T(8,128)S(1)}, u32[]{:S(2)}, u32[]{:S(2)}) %collective-permute-start.14) | collective-permute-done | bytes 73760 | tf_op jit(solution)/shard_map/ppermute | solution.py:833
  61.3 1.6 %image_gradient.7.rest_0_ = bf16[6,8,128,256]{3,2,1,0:T(8,128)(2,1)} custom-call(bf16[6,8,128,128]{3,2,1,0:T(8,128)(2,1)S(1)} %pre_gradient.1.pre_grad, bf16[6,1,128,128]{3,2,1,0:T(8,128)(2,1)S(1)} %collective-permute-done.11.ahead, bf16[6,1,128,128]{3,2,1,0:T(8,128)(2,1)S(1)} %collective-permute-done.12.across, ...), custom_call_target="tpu_custom_call", output_to_operand_aliasing={{}: (4, {})} | custom-call | flops 603979776 | bytes 786432 | tf_op jit(solution)/shard_map/image_gradient/pallas_call | solution.py:733
  63.0 2.0 %collective-permute-done.15.received = bf16[144,128]{1,0:T(8,128)(2,1)S(1)} collective-permute-done((bf16[144,128]{1,0:T(8,128)(2,1)S(1)}, bf16[144,128]{1,0:T(8,128)(2,1)S(1)}, u32[]{:S(2)}, u32[]{:S(2)}) %collective-permute-start.15) | collective-permute-done | bytes 36896 | tf_op jit(solution)/shard_map/ppermute | solution.py:833
  66.1 1.6 %image_gradient.8.rest_0_ = bf16[6,8,128,256]{3,2,1,0:T(8,128)(2,1)} custom-call(bf16[6,8,128,128]{3,2,1,0:T(8,128)(2,1)S(1)} %pre_gradient.1.pre_grad, bf16[6,1,128,128]{3,2,1,0:T(8,128)(2,1)S(1)} %collective-permute-done.11.ahead, bf16[6,1,128,128]{3,2,1,0:T(8,128)(2,1)S(1)} %collective-permute-done.12.across, ...), custom_call_target="tpu_custom_call", output_to_operand_aliasing={{}: (4, {})} | custom-call | flops 603979776 | bytes 786432 | tf_op jit(solution)/shard_map/image_gradient/pallas_call | solution.py:733
  67.8 2.4 %collective-permute-done.16.received = bf16[288,128]{1,0:T(8,128)(2,1)S(1)} collective-permute-done((bf16[288,128]{1,0:T(8,128)(2,1)S(1)}, bf16[288,128]{1,0:T(8,128)(2,1)S(1)}, u32[]{:S(2)}, u32[]{:S(2)}) %collective-permute-start.16) | collective-permute-done | bytes 73760 | tf_op jit(solution)/shard_map/ppermute | solution.py:833
  71.5 2.5 %image_gradient.9 = bf16[6,8,128,256]{3,2,1,0:T(8,128)(2,1)} custom-call(bf16[6,8,128,128]{3,2,1,0:T(8,128)(2,1)S(1)} %pre_gradient.1.pre_grad, bf16[6,1,128,128]{3,2,1,0:T(8,128)(2,1)S(1)} %collective-permute-done.11.ahead, bf16[6,1,128,128]{3,2,1,0:T(8,128)(2,1)S(1)} %collective-permute-done.12.across, ...), custom_call_target="tpu_custom_call", output_to_operand_aliasing={{}: (4, {})} | custom-call | flops 1207959552 | bytes 1572864 | tf_op jit(solution)/shard_map/image_gradient/pallas_call | solution.py:733
  (50 shorter events, 21.4 us)
Async XLA Ops:
  2.3 9.3 %collective-permute-start = (bf16[6,1,128,256]{3,2,1,0:T(8,128)(2,1)S(1)}, bf16[6,1,128,256]{3,2,1,0:T(8,128)(2,1)S(1)}, u32[]{:S(2)}, u32[]{:S(2)}) collective-permute-start(bf16[6,1,128,256]{3,2,1,0:T(8,128)(2,1)S(1)} %get-tuple-element.167), channel_id=1, source_target_pairs={{0,1},{1,0},{2,3},{3,2},{4,5},{5,4},{6,7},{7,6},{8,9},{9,8},{10,11... | collective-permute-start | bytes 1179656 | tf_op jit(solution)/shard_map/ppermute | solution.py:828
  2.9 8.8 %collective-permute-start.1 = (bf16[6,1,128,256]{3,2,1,0:T(8,128)(2,1)S(1)}, bf16[6,1,128,256]{3,2,1,0:T(8,128)(2,1)S(1)}, u32[]{:S(2)}, u32[]{:S(2)}) collective-permute-start(bf16[6,1,128,256]{3,2,1,0:T(8,128)(2,1)S(1)} %get-tuple-element.168), channel_id=1, source_target_pairs={{0,8},{1,2},{2,1},{3,11},{4,12},{5,6},{6,5},{7,15},{8,0},{9,10},{1... | collective-permute-start | bytes 1179656 | tf_op jit(solution)/shard_map/ppermute | solution.py:828
  13.0 1.3 %collective-permute-start.2 = (f32[72,128]{1,0:T(8,128)S(1)}, f32[72,128]{1,0:T(8,128)S(1)}, u32[]{:S(2)}, u32[]{:S(2)}) collective-permute-start(f32[72,128]{1,0:T(8,128)S(1)} %get-tuple-element.176), channel_id=1, source_target_pairs={{0,1},{1,0},{2,3},{3,2},{4,5},{5,4},{6,7},{7,6},{8,9},{9,8},{10,11... | collective-permute-start | bytes 110600 | tf_op jit(solution)/shard_map/ppermute | solution.py:833
  14.3 4.0 %collective-permute-start.3 = (f32[72,128]{1,0:T(8,128)S(1)}, f32[72,128]{1,0:T(8,128)S(1)}, u32[]{:S(2)}, u32[]{:S(2)}) collective-permute-start(f32[72,128]{1,0:T(8,128)S(1)} %add.21), channel_id=1, source_target_pairs={{0,4},{1,3},{2,6},{3,1},{4,0},{5,7},{6,2},{7,5},{8,12},{9,11},{10,... | collective-permute-start | bytes 110600 | tf_op jit(solution)/shard_map/ppermute | solution.py:833
  18.2 4.3 %collective-permute-start.4 = (f32[72,128]{1,0:T(8,128)S(1)}, f32[72,128]{1,0:T(8,128)S(1)}, u32[]{:S(2)}, u32[]{:S(2)}) collective-permute-start(f32[72,128]{1,0:T(8,128)S(1)} %add.22), channel_id=1, source_target_pairs={{0,2},{1,5},{2,0},{3,7},{4,6},{5,1},{6,4},{7,3},{8,10},{9,13},{10,... | collective-permute-start | bytes 110600 | tf_op jit(solution)/shard_map/ppermute | solution.py:833
  22.5 4.3 %collective-permute-start.5 = (f32[72,128]{1,0:T(8,128)S(1)}, f32[72,128]{1,0:T(8,128)S(1)}, u32[]{:S(2)}, u32[]{:S(2)}) collective-permute-start(f32[72,128]{1,0:T(8,128)S(1)} %add.23), channel_id=1, source_target_pairs={{0,8},{1,9},{2,10},{3,11},{4,12},{5,13},{6,14},{7,15},{8,0},{9,1},... | collective-permute-start | bytes 110600 | tf_op jit(solution)/shard_map/ppermute | solution.py:833
  26.8 6.2 %copy-start = (f32[2,64,64]{2,1,0:T(8,128)S(1)}, f32[2,64,64]{2,1,0:T(8,128)}, u32[]{:S(2)}) copy-start(f32[2,64,64]{2,1,0:T(8,128)} %colors.1) | copy-start | bytes 98308
  26.8 6.2 %copy-start.1 = (f32[128]{0:T(128)S(1)}, f32[128]{0:T(128)}, u32[]{:S(2)}) copy-start(f32[128]{0:T(128)} %param.8) | copy-start | bytes 1540
  26.8 4.9 %collective-permute-start.6 = (f32[72,128]{1,0:T(8,128)S(1)}, f32[72,128]{1,0:T(8,128)S(1)}, u32[]{:S(2)}, u32[]{:S(2)}) collective-permute-start(f32[72,128]{1,0:T(8,128)S(1)} %add.24), channel_id=1, source_target_pairs={{0,16},{1,17},{2,18},{3,19},{4,20},{5,21},{6,22},{7,23},{8,24},{9,... | collective-permute-start | bytes 110600 | tf_op jit(solution)/shard_map/ppermute | solution.py:833
  31.8 1.2 %collective-permute-start.7 = (f32[72,128]{1,0:T(8,128)S(1)}, f32[72,128]{1,0:T(8,128)S(1)}, u32[]{:S(2)}, u32[]{:S(2)}) collective-permute-start(f32[72,128]{1,0:T(8,128)S(1)} %add.25.own), channel_id=1, source_target_pairs={{0,1},{1,0},{2,3},{3,2},{4,5},{5,4},{6,7},{7,6},{8,9},{9,8},{10,11... | collective-permute-start | bytes 110600 | tf_op jit(solution)/shard_map/ppermute | solution.py:833
  36.2 2.0 %collective-permute-start.8 = (f32[1152,128]{1,0:T(8,128)S(1)}, f32[1152,128]{1,0:T(8,128)S(1)}, u32[]{:S(2)}, u32[]{:S(2)}) collective-permute-start(f32[1152,128]{1,0:T(8,128)S(1)} %get-tuple-element.246), channel_id=1, source_target_pairs={{0,1},{1,0},{2,3},{3,2},{4,5},{5,4},{6,7},{7,6},{8,9},{9,8},{10,11... | collective-permute-start | bytes 1769480 | tf_op jit(solution)/shard_map/ppermute | solution.py:833
  38.3 6.8 %collective-permute-start.9 = (f32[576,128]{1,0:T(8,128)S(1)}, f32[576,128]{1,0:T(8,128)S(1)}, u32[]{:S(2)}, u32[]{:S(2)}) collective-permute-start(f32[576,128]{1,0:T(8,128)S(1)} %get-tuple-element.261), channel_id=1, source_target_pairs={{0,4},{1,3},{2,6},{3,1},{4,0},{5,7},{6,2},{7,5},{8,12},{9,11},{10,... | collective-permute-start | bytes 884744 | tf_op jit(solution)/shard_map/ppermute | solution.py:833
  39.9 10.5 %collective-permute-start.11 = (bf16[6,1,128,128]{3,2,1,0:T(8,128)(2,1)S(1)}, bf16[6,1,128,128]{3,2,1,0:T(8,128)(2,1)S(1)}, u32[]{:S(2)}, u32[]{:S(2)}) collective-permute-start(bf16[6,1,128,128]{3,2,1,0:T(8,128)(2,1)S(1)} %get-tuple-element.283), channel_id=1, source_target_pairs={{0,1},{1,0},{2,3},{3,2},{4,5},{5,4},{6,7},{7,6},{8,9},{9,8},{10,11... | collective-permute-start | bytes 589832 | tf_op jit(solution)/shard_map/ppermute | solution.py:828
  39.9 10.5 %collective-permute-start.12 = (bf16[6,1,128,128]{3,2,1,0:T(8,128)(2,1)S(1)}, bf16[6,1,128,128]{3,2,1,0:T(8,128)(2,1)S(1)}, u32[]{:S(2)}, u32[]{:S(2)}) collective-permute-start(bf16[6,1,128,128]{3,2,1,0:T(8,128)(2,1)S(1)} %get-tuple-element.284), channel_id=1, source_target_pairs={{0,8},{1,2},{2,1},{3,11},{4,12},{5,6},{6,5},{7,15},{8,0},{9,10},{1... | collective-permute-start | bytes 589832 | tf_op jit(solution)/shard_map/ppermute | solution.py:828
  45.1 5.2 %collective-permute-start.10 = (f32[288,128]{1,0:T(8,128)S(1)}, f32[288,128]{1,0:T(8,128)S(1)}, u32[]{:S(2)}, u32[]{:S(2)}) collective-permute-start(f32[288,128]{1,0:T(8,128)S(1)} %get-tuple-element.271), channel_id=1, source_target_pairs={{0,2},{1,5},{2,0},{3,7},{4,6},{5,1},{6,4},{7,3},{8,10},{9,13},{10,... | collective-permute-start | bytes 442376 | tf_op jit(solution)/shard_map/ppermute | solution.py:833
  50.4 4.4 %collective-permute-start.13 = (f32[144,128]{1,0:T(8,128)S(1)}, f32[144,128]{1,0:T(8,128)S(1)}, u32[]{:S(2)}, u32[]{:S(2)}) collective-permute-start(f32[144,128]{1,0:T(8,128)S(1)} %get-tuple-element.286), channel_id=1, source_target_pairs={{0,8},{1,9},{2,10},{3,11},{4,12},{5,13},{6,14},{7,15},{8,0},{9,1},... | collective-permute-start | bytes 221192 | tf_op jit(solution)/shard_map/ppermute | solution.py:833
  54.8 6.1 %collective-permute-start.14 = (f32[144,128]{1,0:T(8,128)S(1)}, f32[144,128]{1,0:T(8,128)S(1)}, u32[]{:S(2)}, u32[]{:S(2)}) collective-permute-start(f32[144,128]{1,0:T(8,128)S(1)} %add.26), channel_id=1, source_target_pairs={{0,16},{1,17},{2,18},{3,19},{4,20},{5,21},{6,22},{7,23},{8,24},{9,... | collective-permute-start | bytes 221192 | tf_op jit(solution)/shard_map/ppermute | solution.py:833
  60.9 4.0 %collective-permute-start.15 = (bf16[144,128]{1,0:T(8,128)(2,1)S(1)}, bf16[144,128]{1,0:T(8,128)(2,1)S(1)}, u32[]{:S(2)}, u32[]{:S(2)}) collective-permute-start(bf16[144,128]{1,0:T(8,128)(2,1)S(1)} %add_convert_fusion.value), channel_id=1, source_target_pairs={{0,8},{1,9},{2,10},{3,11},{4,12},{5,13},{6,14},{7,15},{8,0},{9,1},... | collective-permute-start | bytes 110600 | tf_op jit(solution)/shard_map/ppermute | solution.py:833
  65.0 5.2 %collective-permute-start.16 = (bf16[288,128]{1,0:T(8,128)(2,1)S(1)}, bf16[288,128]{1,0:T(8,128)(2,1)S(1)}, u32[]{:S(2)}, u32[]{:S(2)}) collective-permute-start(bf16[288,128]{1,0:T(8,128)(2,1)S(1)} %join.3.value), channel_id=1, source_target_pairs={{0,2},{1,5},{2,0},{3,7},{4,6},{5,1},{6,4},{7,3},{8,10},{9,13},{10,... | collective-permute-start | bytes 221192 | tf_op jit(solution)/shard_map/ppermute | solution.py:833
  70.2 5.2 %collective-permute-start.17 = (bf16[576,128]{1,0:T(8,128)(2,1)S(1)}, bf16[576,128]{1,0:T(8,128)(2,1)S(1)}, u32[]{:S(2)}, u32[]{:S(2)}) collective-permute-start(bf16[576,128]{1,0:T(8,128)(2,1)S(1)} %join.4.value), channel_id=1, source_target_pairs={{0,4},{1,3},{2,6},{3,1},{4,0},{5,7},{6,2},{7,5},{8,12},{9,11},{10,... | collective-permute-start | bytes 442376 | tf_op jit(solution)/shard_map/ppermute | solution.py:833
  75.5 1.6 %collective-permute-start.18 = (bf16[1152,128]{1,0:T(8,128)(2,1)S(1)}, bf16[1152,128]{1,0:T(8,128)(2,1)S(1)}, u32[]{:S(2)}, u32[]{:S(2)}) collective-permute-start(bf16[1152,128]{1,0:T(8,128)(2,1)S(1)} %join.5.value), channel_id=1, source_target_pairs={{0,1},{1,0},{2,3},{3,2},{4,5},{5,4},{6,7},{7,6},{8,9},{9,8},{10,11... | collective-permute-start | bytes 884744 | tf_op jit(solution)/shard_map/ppermute | solution.py:833
